TPU v7x, 32 devices: a whole 2x2x4 slice. The times are simulated.
32 devices in a mesh: mem: 2 (over y), gx: 16 (over z, x, core).
Axes of the slice: x: 2, y: 2, z: 4, core: 2. Of those that a mesh axis runs over, the one named last changes fastest.
Arguments:
- density: float32 [32, 128, 256], P('mem', 'gx'), may hold values from 0.5 to 2
- momenta: float32 [32, 2, 128, 256], P('mem', None, 'gx'), may hold values from -1 to 1
- desired: float32 [2, 128, 256], P(None, 'gx'), may hold values from -1.5 to 1.5
- factor_x: float32 [128, 128], P('gx'), may hold values from -1 to 1, as said below
- factor_y: float32 [256, 128], replicated, may hold values from -1 to 1, as said below
- factor_m: float32 [32, 32], P('mem'), may hold values from -1 to 1, as said below
Outputs:
- core: float32 [32, 3, 128, 128], P('mem', None, 'gx')
Inputs may be any that keep to these rules, and one draw needn't show every extreme that they name: `factor_x`: columns are orthonormal. `factor_y`: columns are orthonormal. `factor_m`: columns are orthonormal.
All inputs are finite; a program needn't handle non-finite values.
Results may differ from a plain program's by a relative error of at most 0.00013.
Values sent between devices are 32-bit elements; how exact they have to be, the bound alone decides.
No kernel may reach another device: no remote copies, remote signals or barrier semaphores. Data moves between devices by JAX's collectives and lax.ppermute only.
A program may use at most 64 MiB of HBM per device.

v0:
```python
import jax
import jax.numpy as jnp
from jax import lax
from jax.sharding import PartitionSpec as P

STEPS = 2


STIFF = 1.0
RELAX = 1.0
DTIME = 0.2


def with_halo(cells, sides, width):
    for axis, dim in sides:
        count = lax.axis_size(axis)
        head = lax.slice_in_dim(cells, 0, width, axis=dim)
        tail = lax.slice_in_dim(cells, cells.shape[dim] - width, cells.shape[dim], axis=dim)
        cells = jnp.concatenate(
            [
                lax.ppermute(tail, axis, [(i, (i + 1) % count) for i in range(count)]),
                cells,
                lax.ppermute(head, axis, [((i + 1) % count, i) for i in range(count)]),
            ],
            axis=dim,
        )
    return cells


def tendency(fields, desired):
    density = fields[:, 0]
    moment_x = fields[:, 1]
    moment_y = fields[:, 2]
    speed_x = moment_x / density
    speed_y = moment_y / density
    sound = jnp.sqrt(STIFF * density)
    pressure = 0.5 * STIFF * density * density
    conserved = (density, moment_x, moment_y)
    fluxes_x = (moment_x, moment_x * speed_x + pressure, moment_y * speed_x)
    fluxes_y = (moment_y, moment_x * speed_y, moment_y * speed_y + pressure)
    reach_x = jnp.abs(speed_x) + sound
    bound_x = jnp.maximum(reach_x[:, :-1], reach_x[:, 1:])
    reach_y = (jnp.abs(speed_y) + sound)[:, 1:-1]
    bound_y = jnp.maximum(reach_y, jnp.roll(reach_y, -1, axis=-1))
    changes = []
    for quantity, normal_flux, cross_flux in zip(conserved, fluxes_x, fluxes_y):
        face_x = 0.5 * (normal_flux[:, :-1] + normal_flux[:, 1:]) - 0.5 * bound_x * (
            quantity[:, 1:] - quantity[:, :-1]
        )
        middle = quantity[:, 1:-1]
        cross_mid = cross_flux[:, 1:-1]
        face_y = 0.5 * (cross_mid + jnp.roll(cross_mid, -1, axis=-1)) - 0.5 * bound_y * (
            jnp.roll(middle, -1, axis=-1) - middle
        )
        changes.append(-(face_x[:, 1:] - face_x[:, :-1]) - (face_y - jnp.roll(face_y, 1, axis=-1)))
    centre = density[:, 1:-1]
    changes[1] = changes[1] + (centre * desired[0] - moment_x[:, 1:-1]) / RELAX
    changes[2] = changes[2] + (centre * desired[1] - moment_y[:, 1:-1]) / RELAX
    return jnp.stack(changes, axis=1)


def single_rims(fields):
    return with_halo(fields, (("gx", 2),), 1)


def on_device(density, momenta, desired, factor_x, factor_y, factor_m):
    highest = lax.Precision.HIGHEST
    fields = jnp.concatenate([density[:, None], momenta], axis=1)
    for repeat in range(STEPS):
        sectioned = fields + DTIME * tendency(single_rims(fields), desired)
        second = sectioned + DTIME * tendency(single_rims(sectioned), desired)
        fields = 0.5 * fields + 0.5 * second
    along_y = jnp.einsum("mcxy,yb->mcxb", fields, factor_y, precision=highest)
    spread = lax.all_to_all(along_y, "gx", split_axis=3, concat_axis=2, tiled=True)
    projected = jnp.einsum(
        "mcxb,xa->mcab",
        spread,
        lax.all_gather(factor_x, "gx", axis=0, tiled=True),
        precision=highest,
    )
    returned = lax.all_to_all(projected, "gx", split_axis=2, concat_axis=3, tiled=True)
    member_terms = jnp.einsum("mcab,mk->kcab", returned, factor_m, precision=highest)
    core = lax.psum_scatter(member_terms, "mem", scatter_dimension=0, tiled=True)
    return core


def solution(mesh):
    return jax.shard_map(
        on_device,
        mesh=mesh,
        in_specs=(
            P("mem", "gx", None),
            P("mem", None, "gx", None),
            P(None, "gx", None),
            P("gx", None),
            P(),
            P("mem", None),
        ),
        out_specs=P("mem", None, "gx", None),
        check_vma=False,
    )
```

profile of v0, /device:TPU:1, one launch (start us, length us, event | category | flops | bytes accessed | tf_op | source)
XLA Modules:
  0.0 115.8 jit_solution(7056669775666274553)
XLA Ops:
  6.5 1.2 %fusion.155 = (f32[16,3,1,256]{3,2,0,1:T(1,128)S(1)}, f32[16,3,1,256]{3,2,0,1:T(1,128)S(1)}) fusion(f32[16,2,8,256]{3,2,1,0:T(8,128)} %param.7, f32[16,1,8,256]{3,2,1,0:T(8,128)} %bitcast.254), kind=kLoop, calls=%fused_computation.263 | loop fusion | flops 98304 | bytes 491520 | tf_op jit(solution)/shard_map/slice | solution.py:18
  7.8 2.7 %collective-permute-start = (f32[16,3,1,256]{3,2,0,1:T(1,128)S(1)}, f32[16,3,1,256]{3,2,0,1:T(1,128)S(1)}, u32[]{:S(2)}, u32[]{:S(2)}) collective-permute-start(f32[16,3,1,256]{3,2,0,1:T(1,128)S(1)} %get-tuple-element.63), channel_id=1, source_target_pairs={{0,1},{1,2},{2,3},{3,4},{4,5},{5,6},{6,7},{7,8},{8,9},{9,10},{10,1... | collective-permute-start | bytes 147464 | tf_op jit(solution)/shard_map/ppermute | solution.py:21
  10.4 0.7 slice_bitcast_fusion.13
  11.1 0.5 collective-permute-done
  11.6 2.6 %collective-permute-done.1 = f32[16,3,1,256]{3,2,0,1:T(1,128)S(1)} collective-permute-done((f32[16,3,1,256]{3,2,0,1:T(1,128)S(1)}, f32[16,3,1,256]{3,2,0,1:T(1,128)S(1)}, u32[]{:S(2)}, u32[]{:S(2)}) %collective-permute-start.1) | collective-permute-done | bytes 49184 | tf_op jit(solution)/shard_map/ppermute | solution.py:23
  14.2 1.1 pad_maximum_fusion
  15.6 0.2 fusion.132
  16.6 0.2 fusion.105
  17.0 0.3 fusion.45
  17.6 0.7 copy-done.1
  18.5 1.0 collective-permute-start.3
  19.4 0.7 collective-permute-done.2
  20.1 2.4 %collective-permute-done.3 = f32[16,3,1,256]{3,2,0,1:T(1,128)S(1)} collective-permute-done((f32[16,3,1,256]{3,2,0,1:T(1,128)S(1)}, f32[16,3,1,256]{3,2,0,1:T(1,128)S(1)}, u32[]{:S(2)}, u32[]{:S(2)}) %collective-permute-start.3) | collective-permute-done | bytes 49184 | tf_op jit(solution)/shard_map/ppermute | solution.py:23
  22.6 0.2 fusion.136
  23.9 0.2 fusion.89
  24.2 0.3 fusion.37
  25.1 3.2 %collective-permute-start.5 = (f32[16,3,1,256]{3,2,0,1:T(1,128)S(1)}, f32[16,3,1,256]{3,2,0,1:T(1,128)S(1)}, u32[]{:S(2)}, u32[]{:S(2)}) collective-permute-start(f32[16,3,1,256]{3,2,0,1:T(1,128)S(1)} %get-tuple-element.60), channel_id=1, source_target_pairs={{1,0},{2,1},{3,2},{4,3},{5,4},{6,5},{7,6},{8,7},{9,8},{10,9},{11,1... | collective-permute-start | bytes 147464 | tf_op jit(solution)/shard_map/ppermute | solution.py:23
  28.2 0.7 collective-permute-done.4
  28.9 0.6 collective-permute-done.5
  29.7 0.2 fusion.140
  30.9 0.2 fusion.73
  31.3 0.3 fusion.29
  32.0 5.0 %collective-permute-start.7 = (f32[16,3,1,256]{3,2,0,1:T(1,128)S(1)}, f32[16,3,1,256]{3,2,0,1:T(1,128)S(1)}, u32[]{:S(2)}, u32[]{:S(2)}) collective-permute-start(f32[16,3,1,256]{3,2,0,1:T(1,128)S(1)} %get-tuple-element.58), channel_id=1, source_target_pairs={{1,0},{2,1},{3,2},{4,3},{5,4},{6,5},{7,6},{8,7},{9,8},{10,9},{11,1... | collective-permute-start | bytes 147464 | tf_op jit(solution)/shard_map/ppermute | solution.py:23
  37.0 0.7 collective-permute-done.6
  37.7 0.2 collective-permute-done.7
  37.9 0.2 pad_maximum_fusion.3
  38.0 0.2 fusion.144
  39.3 0.2 fusion.57
  39.6 0.3 fusion.21
  40.3 0.6 fusion.12
  40.9 0.6 copy.90
  41.5 1.2 %reshape.3 = f32[16,1,3072]{2,1,0:T(1,128)} reshape(f32[128,3,8,16]{3,2,1,0:T(8,128)S(1)} %bitcast.249) | data formatting | bytes 393216
  42.7 11.1 %all-to-all-start = ((f32[16,1,3072]{2,1,0:T(1,128)}), f32[16,1,3072]{2,1,0:T(1,128)S(1)}, u32[]{:S(2)}, u32[]{:S(2)}) async-start(f32[16,1,3072]{2,1,0:T(1,128)} %reshape.3), calls=%async_computation | async-start | bytes 393216 | tf_op jit(solution)/shard_map/all_to_all | solution.py:74
  53.8 22.0 %all_gather.3 = f32[128,128]{1,0:T(8,128)S(1)} all-gather(f32[8,128]{1,0:T(8,128)S(1)} %copy-done.4), channel_id=1, replica_groups=mesh['mem'=2,'gx'=16] {'gx'}, dimensions={0}, use_global_device_ids=true | all-gather | bytes 69632 | tf_op jit(solution)/shard_map/all_gather | solution.py:78
  75.9 0.5 broadcast.110
  76.4 1.1 reduce
  77.5 0.5 reshape.4
  78.0 0.3 copy.92
  78.4 0.5 copy.93
  78.8 0.3 convolution_bitcast_fusion
  79.2 0.6 copy.94
  79.7 0.6 reshape.5
  80.3 10.6 %all_to_all.36 = f32[16,1,3072]{2,1,0:T(1,128)S(1)} all-to-all(f32[16,1,3072]{2,1,0:T(1,128)S(1)} %reshape.5), channel_id=1, replica_groups=mesh['mem'=2,'gx'=16] {'gx'}, dimensions={0} | all-to-all | bytes 393216 | tf_op jit(solution)/shard_map/all_to_all | solution.py:81
  90.9 1.1 reduce.1
  92.0 0.5 reshape.6
  92.6 2.5 %fusion.3 = f32[32,3,8,128]{3,0,2,1:T(8,128)} fusion(f32[16,3,8,16,8]{0,4,1,2,3:T(8,128)S(1)} %bitcast.253, f32[16,32]{1,0:T(8,128)S(1)} %copy-done.3), kind=kOutput, calls=%fused_computation.3 | convolution fusion | flops 18874368 | bytes 591872 | tf_op jit(solution)/shard_map/mcab,mk->kcab/dot_general | solution.py:82
  95.1 12.2 %reduce-scatter.2.cloned.1.call-done = f32[16,3,8,128]{3,0,2,1:T(8,128)} async-done(((f32[32,3,8,128]{3,0,2,1:T(8,128)}), f32[16,3,8,128]{3,0,2,1:T(8,128)}) %reduce-scatter.2.cloned.1.call-update) | async-done | bytes 196624 | tf_op jit(solution)/shard_map/reduce_scatter | solution.py:83
  107.3 1.7 %copy.98 = f32[16,3,8,128]{3,2,1,0:T(8,128)} copy(f32[16,3,8,128]{3,0,2,1:T(8,128)} %reduce-scatter.2.cloned.1.call-done) | data formatting | bytes 393216 | tf_op jit(solution)/shard_map/reduce_scatter | solution.py:83
  (100 shorter events, 6.3 us)
Async XLA Ops:
  6.5 33.7 %copy-start = (f32[256,128]{1,0:T(8,128)S(1)}, f32[256,128]{1,0:T(8,128)}, u32[]{:S(2)}) copy-start(f32[256,128]{1,0:T(8,128)} %param.10) | copy-start | bytes 393220
  7.8 3.8 %collective-permute-start = (f32[16,3,1,256]{3,2,0,1:T(1,128)S(1)}, f32[16,3,1,256]{3,2,0,1:T(1,128)S(1)}, u32[]{:S(2)}, u32[]{:S(2)}) collective-permute-start(f32[16,3,1,256]{3,2,0,1:T(1,128)S(1)} %get-tuple-element.63), channel_id=1, source_target_pairs={{0,1},{1,2},{2,3},{3,4},{4,5},{5,6},{6,7},{7,8},{8,9},{9,10},{10,1... | collective-permute-start | bytes 147464 | tf_op jit(solution)/shard_map/ppermute | solution.py:21
  10.4 3.8 %collective-permute-start.1 = (f32[16,3,1,256]{3,2,0,1:T(1,128)S(1)}, f32[16,3,1,256]{3,2,0,1:T(1,128)S(1)}, u32[]{:S(2)}, u32[]{:S(2)}) collective-permute-start(f32[16,3,1,256]{3,2,0,1:T(1,128)S(1)} %get-tuple-element.64), channel_id=1, source_target_pairs={{1,0},{2,1},{3,2},{4,3},{5,4},{6,5},{7,6},{8,7},{9,8},{10,9},{11,1... | collective-permute-start | bytes 147464 | tf_op jit(solution)/shard_map/ppermute | solution.py:23
  17.3 1.0 copy-start.1
  17.3 1.0 copy-start.2
  18.4 1.7 %collective-permute-start.2 = (f32[16,3,1,256]{3,2,0,1:T(1,128)S(1)}, f32[16,3,1,256]{3,2,0,1:T(1,128)S(1)}, u32[]{:S(2)}, u32[]{:S(2)}) collective-permute-start(f32[16,3,1,256]{3,2,0,1:T(1,128)S(1)} %get-tuple-element.61), channel_id=1, source_target_pairs={{0,1},{1,2},{2,3},{3,4},{4,5},{5,6},{6,7},{7,8},{8,9},{9,10},{10,1... | collective-permute-start | bytes 147464 | tf_op jit(solution)/shard_map/ppermute | solution.py:21
  18.5 4.0 %collective-permute-start.3 = (f32[16,3,1,256]{3,2,0,1:T(1,128)S(1)}, f32[16,3,1,256]{3,2,0,1:T(1,128)S(1)}, u32[]{:S(2)}, u32[]{:S(2)}) collective-permute-start(f32[16,3,1,256]{3,2,0,1:T(1,128)S(1)} %get-tuple-element.62), channel_id=1, source_target_pairs={{1,0},{2,1},{3,2},{4,3},{5,4},{6,5},{7,6},{8,7},{9,8},{10,9},{11,1... | collective-permute-start | bytes 147464 | tf_op jit(solution)/shard_map/ppermute | solution.py:23
  25.0 3.9 %collective-permute-start.4 = (f32[16,3,1,256]{3,2,0,1:T(1,128)S(1)}, f32[16,3,1,256]{3,2,0,1:T(1,128)S(1)}, u32[]{:S(2)}, u32[]{:S(2)}) collective-permute-start(f32[16,3,1,256]{3,2,0,1:T(1,128)S(1)} %get-tuple-element.59), channel_id=1, source_target_pairs={{0,1},{1,2},{2,3},{3,4},{4,5},{5,6},{6,7},{7,8},{8,9},{9,10},{10,1... | collective-permute-start | bytes 147464 | tf_op jit(solution)/shard_map/ppermute | solution.py:21
  25.1 4.5 %collective-permute-start.5 = (f32[16,3,1,256]{3,2,0,1:T(1,128)S(1)}, f32[16,3,1,256]{3,2,0,1:T(1,128)S(1)}, u32[]{:S(2)}, u32[]{:S(2)}) collective-permute-start(f32[16,3,1,256]{3,2,0,1:T(1,128)S(1)} %get-tuple-element.60), channel_id=1, source_target_pairs={{1,0},{2,1},{3,2},{4,3},{5,4},{6,5},{7,6},{8,7},{9,8},{10,9},{11,1... | collective-permute-start | bytes 147464 | tf_op jit(solution)/shard_map/ppermute | solution.py:23
  32.0 5.7 %collective-permute-start.6 = (f32[16,3,1,256]{3,2,0,1:T(1,128)S(1)}, f32[16,3,1,256]{3,2,0,1:T(1,128)S(1)}, u32[]{:S(2)}, u32[]{:S(2)}) collective-permute-start(f32[16,3,1,256]{3,2,0,1:T(1,128)S(1)} %get-tuple-element.57), channel_id=1, source_target_pairs={{0,1},{1,2},{2,3},{3,4},{4,5},{5,6},{6,7},{7,8},{8,9},{9,10},{10,1... | collective-permute-start | bytes 147464 | tf_op jit(solution)/shard_map/ppermute | solution.py:21
  32.0 5.9 %collective-permute-start.7 = (f32[16,3,1,256]{3,2,0,1:T(1,128)S(1)}, f32[16,3,1,256]{3,2,0,1:T(1,128)S(1)}, u32[]{:S(2)}, u32[]{:S(2)}) collective-permute-start(f32[16,3,1,256]{3,2,0,1:T(1,128)S(1)} %get-tuple-element.58), channel_id=1, source_target_pairs={{1,0},{2,1},{3,2},{4,3},{5,4},{6,5},{7,6},{8,7},{9,8},{10,9},{11,1... | collective-permute-start | bytes 147464 | tf_op jit(solution)/shard_map/ppermute | solution.py:23
  40.9 13.0 %copy-start.4 = (f32[8,128]{1,0:T(8,128)S(1)}, f32[8,128]{1,0:T(8,128)}, u32[]{:S(2)}) copy-start(f32[8,128]{1,0:T(8,128)} %param.9) | copy-start | bytes 12292
  42.7 33.1 %all-to-all-start = ((f32[16,1,3072]{2,1,0:T(1,128)}), f32[16,1,3072]{2,1,0:T(1,128)S(1)}, u32[]{:S(2)}, u32[]{:S(2)}) async-start(f32[16,1,3072]{2,1,0:T(1,128)} %reshape.3), calls=%async_computation | async-start | bytes 393216 | tf_op jit(solution)/shard_map/all_to_all | solution.py:74
  53.8 53.5 %reduce-scatter.2.cloned.1.call-start = ((), (), s32[]{:S(2)}) async-start(), calls=%async_computation.3 | async-start | bytes 589824 | tf_op jit(solution)/shard_map/reduce_scatter | solution.py:83
  80.3 12.3 %copy-start.3 = (f32[16,32]{1,0:T(8,128)S(1)}, f32[16,32]{1,0:T(8,128)}, u32[]{:S(2)}) copy-start(f32[16,32]{1,0:T(8,128)} %param.11) | copy-start | bytes 6148
Sparse Core Ops, SparseCore 0:
  95.2 11.9 reduce-scatter.1
where the time goes:
time: 117 us; the launch traced here: 116 us
  blocking collectives  32.6 us (28%)
  starting transfers between devices  23.1 us (20%)
  waiting for transfers between devices  20.5 us (18%)
  between operations  14.2 us (12%)
  local copies, waits for them, and re-layouts  12.3 us (11%)
  other arithmetic  9.68 us (8%)
  matrix products  3.46 us (3%)
    all_gather x1, blocking collectives, on_device(): lax.all_gather(factor_x, 'gx', axis=0, tiled=True)  22 us
    reduce_scatter x1, waiting for transfers between devices, on_device(): lax.psum_scatter(member_terms, 'mem', scatter_dimension=0, tiled=True)  12.2 us
    all_to_all x1, starting transfers between devices, on_device(): lax.all_to_all(along_y, 'gx', split_axis=3, concat_axis=2, tiled=True)  11.1 us
    all_to_all x1, blocking collectives, on_device(): lax.all_to_all(projected, 'gx', split_axis=2, concat_axis=3, tiled=True)  10.6 us
    ppermute x4, starting transfers between devices, with_halo(): lax.ppermute(head, axis, [((i + 1) % count, i) for i in range(count)])  9.11 us
    ppermute x4, waiting for transfers between devices, with_halo(): lax.ppermute(head, axis, [((i + 1) % count, i) for i in range(count)])  5.88 us
    unnamed x14, local copies, waits for them, and re-layouts  3.6 us
    ppermute x4, starting transfers between devices, with_halo(): lax.ppermute(tail, axis, [(i, (i + 1) % count) for i in range(count)])  2.83 us
  transfers between devices with their start and end apart: 10, of which 9 were waited for; matrix products, arithmetic and copies ran while one was open for 1% of the time, Pallas kernels for 0%

commit v1 on v0

--- a/solution.py
+++ b/solution.py
@@ -1,6 +1,10 @@
+import functools
+
 import jax
 import jax.numpy as jnp
 from jax import lax
+from jax.experimental import pallas as pl
+from jax.experimental.pallas import tpu as pltpu
 from jax.sharding import PartitionSpec as P
 
 STEPS = 2
@@ -9,6 +13,10 @@
 STIFF = 1.0
 RELAX = 1.0
 DTIME = 0.2
+
+HIGHEST = lax.Precision.HIGHEST
+LANES = 128
+SUBLANES = 8
 
 
 def with_halo(cells, sides, width):
@@ -63,25 +71,332 @@
     return with_halo(fields, (("gx", 2),), 1)
 
 
-def on_device(density, momenta, desired, factor_x, factor_y, factor_m):
-    highest = lax.Precision.HIGHEST
+def plain(density, momenta, desired, factor_x, factor_y, factor_m):
     fields = jnp.concatenate([density[:, None], momenta], axis=1)
     for repeat in range(STEPS):
         sectioned = fields + DTIME * tendency(single_rims(fields), desired)
         second = sectioned + DTIME * tendency(single_rims(sectioned), desired)
         fields = 0.5 * fields + 0.5 * second
-    along_y = jnp.einsum("mcxy,yb->mcxb", fields, factor_y, precision=highest)
+    along_y = jnp.einsum("mcxy,yb->mcxb", fields, factor_y, precision=HIGHEST)
     spread = lax.all_to_all(along_y, "gx", split_axis=3, concat_axis=2, tiled=True)
     projected = jnp.einsum(
         "mcxb,xa->mcab",
         spread,
         lax.all_gather(factor_x, "gx", axis=0, tiled=True),
-        precision=highest,
+        precision=HIGHEST,
     )
     returned = lax.all_to_all(projected, "gx", split_axis=2, concat_axis=3, tiled=True)
-    member_terms = jnp.einsum("mcab,mk->kcab", returned, factor_m, precision=highest)
-    core = lax.psum_scatter(member_terms, "mem", scatter_dimension=0, tiled=True)
-    return core
+    member_terms = jnp.einsum("mcab,mk->kcab", returned, factor_m, precision=HIGHEST)
+    return lax.psum_scatter(member_terms, "mem", scatter_dimension=0, tiled=True)
+
+
+def cell_terms(q):
+    rho, mx, my = q
+    root = lax.rsqrt(rho)
+    inverse = root * root
+    sound = rho * root
+    u = mx * inverse
+    v = my * inverse
+    pressure = (0.5 * STIFF) * (rho * rho)
+    cross = my * u
+    return dict(
+        q=q,
+        f=(mx, mx * u + pressure, cross),
+        g=(my, cross, my * v + pressure),
+        ax=jnp.abs(u) + sound,
+        ay=jnp.abs(v) + sound,
+    )
+
+
+def x_face(low, high):
+    bound = jnp.maximum(low["ax"], high["ax"])
+    return tuple(
+        fa + fb - bound * (b - a)
+        for fa, fb, a, b in zip(low["f"], high["f"], low["q"], high["q"])
+    )
+
+
+def y_difference(row):
+    axis = row["ay"].ndim - 1
+    size = row["ay"].shape[axis]
+    after = lambda a: pltpu.roll(a, size - 1, axis)
+    before = lambda a: pltpu.roll(a, 1, axis)
+    moved_q = tuple(after(a) for a in row["q"])
+    moved_g = (moved_q[2], after(row["g"][1]), after(row["g"][2]))
+    bound = jnp.maximum(row["ay"], after(row["ay"]))
+    face = tuple(
+        ga + gb - bound * (b - a)
+        for ga, gb, a, b in zip(row["g"], moved_g, row["q"], moved_q)
+    )
+    return tuple(a - before(a) for a in face)
+
+
+def section(row, low_face, high_face, wish):
+    cross = y_difference(row)
+    rho, mx, my = row["q"]
+    half = 0.5 * DTIME
+    spread = tuple(h - l + d for h, l, d in zip(high_face, low_face, cross))
+    keep = 1.0 - DTIME / RELAX
+    wished = (DTIME / RELAX) * rho
+    return (
+        rho - half * spread[0],
+        keep * mx + wished * wish[0] - half * spread[1],
+        keep * my + wished * wish[1] - half * spread[2],
+    )
+
+
+def advance_kernel(
+    n_gx, left_d, own_d, left_m, own_m, left_w, own_w, fy, fx, fm, out, state, *tiled
+):
+    rows = own_w.shape[0] // 2
+    members = own_d.shape[0] // rows
+    tiles = own_d.shape[1] // LANES
+    for whole, cut in zip((left_d, own_d, left_m, own_m), tiled):
+        for t in range(tiles):
+            cut[t] = whole[:, t * LANES : (t + 1) * LANES]
+    left_d, own_d, left_m, own_m = tiled
+
+    def every(ref, first, stride):
+        return jnp.concatenate(
+            [ref[t, pl.ds(first, SUBLANES, stride=stride), :] for t in range(tiles)], axis=1
+        )
+
+    count = 2 * rows
+    sections = 2 * STEPS
+    for group in range(members // SUBLANES):
+        def load(x):
+            d, m = (left_d, left_m) if x < rows else (own_d, own_m)
+            at = x % rows
+            first = group * SUBLANES
+            return (
+                every(d, first * rows + at, rows),
+                every(m, first * 2 * rows + at, 2 * rows),
+                every(m, (first * 2 + 1) * rows + at, 2 * rows),
+            )
+
+        def wish(x):
+            w = left_w if x < rows else own_w
+            at = x % rows
+            return tuple(
+                jnp.broadcast_to(w[pl.ds(c * rows + at, 1), :], (SUBLANES, w.shape[1]))
+                for c in range(2)
+            )
+
+        cells = [{} for _ in range(sections + 1)]
+        faces = [{} for _ in range(sections)]
+        for t in range(count):
+            cells[0][t] = cell_terms(load(t))
+            if t:
+                faces[0][t - 1] = x_face(cells[0][t - 1], cells[0][t])
+            for s in range(1, sections + 1):
+                x = t - s
+                if x < s:
+                    break
+                new = section(cells[s - 1][x], faces[s - 1][x - 1], faces[s - 1][x], wish(x))
+                if s % 2 == 0:
+                    old = cells[s - 2][x]["q"]
+                    new = tuple(0.5 * a + 0.5 * b for a, b in zip(old, new))
+                if s < sections:
+                    cells[s][x] = cell_terms(new)
+                    if x > s:
+                        faces[s][x - 1] = x_face(cells[s][x - 1], cells[s][x])
+                else:
+                    at = (x - sections) * members + group * SUBLANES
+                    for c in range(3):
+                        state[pl.ds(c * rows * members + at, SUBLANES), :] = new[c]
+    devices = 2 * n_gx
+    shares = fy.shape[1] // devices
+    height = out.shape[0] // devices
+    for c in range(3):
+        block = state[pl.ds(c * rows * members, rows * members), :]
+        along = jnp.dot(block, fy[...], precision=HIGHEST, preferred_element_type=jnp.float32)
+        turned = along.T
+        for r in range(shares):
+            out[pl.ds(c * shares + r, devices, stride=height), :] = turned[
+                r * devices : (r + 1) * devices
+            ]
+    mem, gx = lax.axis_index("mem"), lax.axis_index("gx")
+    half = rows // 2
+    for r in range(half):
+        line = fx[pl.ds(mem * half + r, 1), :]
+        out[pl.ds(3 * shares + r, devices, stride=height), :] = jnp.broadcast_to(
+            line, (devices, line.shape[1])
+        )
+    line = fm[pl.ds(gx, 1), :]
+    line = jnp.concatenate([line] * (LANES // line.shape[1]), axis=1)
+    out[pl.ds(3 * shares + half, devices, stride=height), :] = jnp.broadcast_to(
+        line, (devices, LANES)
+    )
+
+
+def project_kernel(n_gx, rows, shares, rm, inp, out, blocks, tall):
+    devices = 2 * n_gx
+    members = n_gx
+    height = inp.shape[0] // devices
+    half = rows // 2
+    pieces = 3 * shares
+    columns = [inp[pl.ds(j, devices, stride=height), :] for j in range(pieces)]
+    lhs = jnp.concatenate(
+        [
+            jnp.concatenate([d[:n_gx] for d in columns], axis=0),
+            jnp.concatenate([d[n_gx:] for d in columns], axis=0),
+        ],
+        axis=1,
+    )
+    fm = inp[pl.ds(pieces + half, devices, stride=height), :]
+    group = lax.broadcasted_iota(jnp.int32, (members, LANES), 1) // rm
+    per = LANES // rm
+    zero = jnp.zeros((members, LANES), jnp.float32)
+    lines = []
+    for mem in range(2):
+        part = fm[mem * members : (mem + 1) * members]
+        for x in range(rows):
+            kept = jnp.where(group == x % per, part, 0.0)
+            lines.append(
+                jnp.concatenate(
+                    [kept if x // per == t else zero for t in range(rows // per)], axis=1
+                )
+            )
+    diagonal = jnp.concatenate(lines, axis=0)
+    mixed = jnp.dot(lhs, diagonal, precision=HIGHEST, preferred_element_type=jnp.float32)
+    lows = rm // 2
+    orders = (range(pieces), [j % pieces for j in range(pieces - shares, 2 * pieces - shares)])
+    for x in range(rows):
+        for k in range(2):
+            blocks[pl.ds(x * n_gx, n_gx), pl.ds(k * pieces * lows, pieces * lows)] = jnp.concatenate(
+                [
+                    mixed[j * n_gx : (j + 1) * n_gx, x * rm + k * lows : x * rm + (k + 1) * lows]
+                    for j in orders[k]
+                ],
+                axis=1,
+            )
+    halves = [inp[pl.ds(pieces + r, devices, stride=height), :] for r in range(half)]
+    lines = []
+    for r in range(half):
+        late = halves[r][n_gx:]
+        lines.append(pltpu.roll(late, 1, 0))
+    for r in range(half):
+        lines.append(halves[r][:n_gx])
+    fx = jnp.concatenate(lines, axis=0)
+    core = jnp.dot(fx.T, blocks[...], precision=HIGHEST, preferred_element_type=jnp.float32)
+    high = out.shape[0] // devices
+    for t in range(3):
+        tall[t] = core[:, t * LANES : (t + 1) * LANES]
+    lane = lax.broadcasted_iota(jnp.int32, (n_gx, LANES), 1)
+    for a in range(SUBLANES):
+        for k in range(2):
+            out[pl.ds(k * n_gx * high + a, n_gx, stride=high), :] = tall[
+                2 * k, pl.ds(a, n_gx, stride=SUBLANES), :
+            ]
+    for i in range(SUBLANES // 2):
+        upper = tall[1, pl.ds(i, n_gx, stride=SUBLANES), :]
+        lower = tall[1, pl.ds(i + SUBLANES // 2, n_gx, stride=SUBLANES), :]
+        first = jnp.where(lane < LANES // 2, upper, pltpu.roll(lower, LANES // 2, 1))
+        second = jnp.where(lane < LANES // 2, pltpu.roll(upper, LANES // 2, 1), lower)
+        out[pl.ds(SUBLANES + i, n_gx, stride=high), :] = first
+        out[pl.ds(n_gx * high + SUBLANES + i, n_gx, stride=high), :] = second
+
+
+def gather_kernel(shares, lows, inp, out):
+    devices = LANES // shares
+    high = inp.shape[0] // devices
+    quarter = SUBLANES // 2
+    step = out.shape[0] // lows
+
+    def turn(first):
+        return jnp.concatenate(
+            [inp[pl.ds(first + i, devices, stride=high), :] for i in range(quarter)], axis=0
+        ).T
+
+    def place(turned, base, c, a0):
+        for i in range(quarter):
+            line = jnp.concatenate(
+                [
+                    turned[base + r * lows : base + (r + 1) * lows, i * devices : (i + 1) * devices]
+                    for r in range(shares)
+                ],
+                axis=1,
+            )
+            out[pl.ds(c * SUBLANES + a0 + i, lows, stride=step), :] = line
+
+    for h in range(2):
+        turned = turn(h * quarter)
+        for c in range(2):
+            place(turned, c * shares * lows, c, h * quarter)
+    turned = turn(SUBLANES)
+    for h in range(2):
+        place(turned, h * shares * lows, 2, h * quarter)
+
+
+def exchange(chunks, devices):
+    block = chunks.reshape(devices, chunks.shape[0] // devices, 1, chunks.shape[1])
+    moved = lax.all_to_all(block, ("mem", "gx"), split_axis=0, concat_axis=0, tiled=True)
+    return moved.reshape(chunks.shape)
+
+
+def laid_out(density, factor_x, factor_y, factor_m):
+    members, rows, cells_y = density.shape
+    n_mem, n_gx = lax.axis_size("mem"), lax.axis_size("gx")
+    rx, ry, rm = factor_x.shape[1], factor_y.shape[1], factor_m.shape[1]
+    shares = ry // (n_mem * n_gx)
+    return (
+        n_mem == 2
+        and rows == 4 * STEPS == SUBLANES
+        and members == n_gx
+        and members * rows == LANES
+        and members % SUBLANES == 0
+        and cells_y % LANES == 0
+        and rx == LANES == n_gx * SUBLANES
+        and ry == LANES == shares * n_mem * n_gx
+        and shares * rm == LANES
+        and shares * rm // 2 * 2 == LANES
+        and rows * rm == 2 * LANES
+    )
+
+
+def on_device(density, momenta, desired, factor_x, factor_y, factor_m):
+    if not laid_out(density, factor_x, factor_y, factor_m):
+        return plain(density, momenta, desired, factor_x, factor_y, factor_m)
+    members, rows, cells_y = density.shape
+    n_gx = lax.axis_size("gx")
+    devices = 2 * n_gx
+    rx, ry, rm = factor_x.shape[1], factor_y.shape[1], factor_m.shape[1]
+    shares = ry // devices
+    forward = [(i, (i + 1) % n_gx) for i in range(n_gx)]
+    own = (density, momenta, desired)
+    left = [lax.ppermute(a, "gx", forward) for a in own]
+    flat = [a.reshape(-1, cells_y) for pair in zip(left, own) for a in pair]
+    params = pltpu.CompilerParams(vmem_limit_bytes=32 * 1024 * 1024)
+    height = 3 * shares + rows // 2 + 1
+    sent = pl.pallas_call(
+        functools.partial(advance_kernel, n_gx),
+        out_shape=jax.ShapeDtypeStruct((devices * height, LANES), jnp.float32),
+        scratch_shapes=[pltpu.VMEM((3 * rows * members, cells_y), jnp.float32)]
+        + [pltpu.VMEM((cells_y // LANES, a.shape[0], LANES), jnp.float32) for a in flat[:4]],
+        compiler_params=params,
+        name="advance",
+    )(*flat, factor_y, factor_x, factor_m)
+    got = exchange(sent, devices)
+    lows = rm // 2
+    high = 3 * shares * lows * SUBLANES // LANES
+    sent = pl.pallas_call(
+        functools.partial(project_kernel, n_gx, rows, shares, rm),
+        out_shape=jax.ShapeDtypeStruct((devices * high, LANES), jnp.float32),
+        scratch_shapes=[
+            pltpu.VMEM((rows * n_gx, 3 * shares * rm), jnp.float32),
+            pltpu.VMEM((3, rx, LANES), jnp.float32),
+        ],
+        compiler_params=params,
+        name="project",
+    )(got)
+    got = exchange(sent, devices)
+    core = pl.pallas_call(
+        functools.partial(gather_kernel, shares, lows),
+        out_shape=jax.ShapeDtypeStruct((lows * 3 * SUBLANES, LANES), jnp.float32),
+        compiler_params=params,
+        name="gather",
+    )(got)
+    return core.reshape(lows, 3, SUBLANES, ry)
 
 
 def solution(mesh):

time: 117 us -> 48.2 us (0.41)
  starting transfers between devices: 23.1 us -> 4.26 us
  waiting for transfers between devices: 20.5 us -> 3.45 us
  between operations: 14.2 us -> 0.03 us
  other arithmetic: 9.68 us -> 0 us
  local copies, waits for them, and re-layouts: 12.3 us -> 4.16 us
  Pallas kernels: 0 us -> 7 us
  blocking collectives: 32.6 us -> 29 us
  matrix products: 3.46 us -> 0 us
    all_gather x1 -> x0, blocking collectives: 22 us -> none  [on_device(): lax.all_gather(factor_x, 'gx', axis=0, tiled=True)]
    all_to_all x1 -> x2, blocking collectives: 10.6 us -> 29 us  [exchange(): lax.all_to_all(block, ('mem', 'gx'), split_axis=0, concat_axis=0, tiled=T...]
    reduce_scatter x1 -> x0, waiting for transfers between devices: 12.2 us -> none  [on_device(): lax.psum_scatter(member_terms, 'mem', scatter_dimension=0, tiled=True)]
    all_to_all x1 -> x0, starting transfers between devices: 11.1 us -> none  [on_device(): lax.all_to_all(along_y, 'gx', split_axis=3, concat_axis=2, tiled=True)]
    ppermute x8 -> x3, starting transfers between devices: 11.9 us -> 4.26 us  [on_device(): left = [lax.ppermute(a, 'gx', forward) for a in own]]
    pallas_call x0 -> x3, Pallas kernels: none -> 7 us  [the longest x1 4.72 us: on_device(): pl.pallas_call(functools.partial(advance_kernel, n_gx), out_shape=jax.Sha...]
    ppermute x8 -> x3, waiting for transfers between devices: 8.32 us -> 3.45 us  [on_device(): left = [lax.ppermute(a, 'gx', forward) for a in own]]
    slice x62 -> x0, local copies, waits for them, and re-layouts: 3.7 us -> none  [the longest x24 1.31 us: tendency(): jnp.roll(cross_mid, -1, axis=-1)]
  transfers between devices with their start and end apart: 10 -> 3, of which waited for: 9 -> 1; matrix products, arithmetic and copies ran while one was open for 1% -> 0% of each run, Pallas kernels for 0% -> 0%
where the time goes in v1:
time: 48.2 us; the launch traced here: 47.9 us
  blocking collectives  29 us (60%)
  Pallas kernels  7 us (15%)
  starting transfers between devices  4.26 us (9%)
  local copies, waits for them, and re-layouts  4.16 us (9%)
  waiting for transfers between devices  3.45 us (7%)
    all_to_all x2, blocking collectives, exchange(): lax.all_to_all(block, ('mem', 'gx'), split_axis=0, concat_axis=0, tiled=T...  29 us
    pallas_call x1, Pallas kernels, on_device(): pl.pallas_call(functools.partial(advance_kernel, n_gx), out_shape=jax.Sha...  4.72 us
    ppermute x3, starting transfers between devices, on_device(): left = [lax.ppermute(a, 'gx', forward) for a in own]  4.26 us
    unnamed x12, local copies, waits for them, and re-layouts  4.16 us
    ppermute x3, waiting for transfers between devices, on_device(): left = [lax.ppermute(a, 'gx', forward) for a in own]  3.45 us
    pallas_call x1, Pallas kernels, on_device(): pl.pallas_call(functools.partial(project_kernel, n_gx, rows, shares, rm),...  1.29 us
    pallas_call x1, Pallas kernels, on_device(): pl.pallas_call(functools.partial(gather_kernel, shares, lows), out_shape=...  0.99 us
  transfers between devices with their start and end apart: 3, of which 1 were waited for; matrix products, arithmetic and copies ran while one was open for 0% of the time, Pallas kernels for 0%

profile of v1, /device:TPU:1, one launch (start us, length us, event | category | flops | bytes accessed | tf_op | source)
XLA Modules:
  0.0 47.9 jit_solution(5656881951171997090)
XLA Ops:
  0.0 0.0 copy-start.4
  0.0 2.6 %collective-permute-start.1 = (f32[16,2,8,256]{3,2,1,0:T(8,128)}, f32[16,2,8,256]{3,2,1,0:T(8,128)S(1)}, u32[]{:S(2)}, u32[]{:S(2)}) collective-permute-start(f32[16,2,8,256]{3,2,1,0:T(8,128)} %param.7), channel_id=1, source_target_pairs={{0,1},{1,2},{2,3},{3,4},{4,5},{5,6},{6,7},{7,8},{8,9},{9,10},{10,1... | collective-permute-start | bytes 786440 | tf_op jit(solution)/shard_map/ppermute | solution.py:367
  2.6 0.1 collective-permute-start
  2.7 1.6 %collective-permute-start.2 = (f32[2,8,256]{2,1,0:T(8,128)}, f32[2,8,256]{2,1,0:T(8,128)S(1)}, u32[]{:S(2)}, u32[]{:S(2)}) collective-permute-start(f32[2,8,256]{2,1,0:T(8,128)} %param.8), channel_id=1, source_target_pairs={{0,1},{1,2},{2,3},{3,4},{4,5},{5,6},{6,7},{7,8},{8,9},{9,10},{10,1... | collective-permute-start | bytes 49160 | tf_op jit(solution)/shard_map/ppermute | solution.py:367
  4.3 3.4 %collective-permute-done.2 = f32[2,8,256]{2,1,0:T(8,128)S(1)} collective-permute-done((f32[2,8,256]{2,1,0:T(8,128)}, f32[2,8,256]{2,1,0:T(8,128)S(1)}, u32[]{:S(2)}, u32[]{:S(2)}) %collective-permute-start.2) | collective-permute-done | bytes 16416 | tf_op jit(solution)/shard_map/ppermute | solution.py:367
  7.7 0.0 collective-permute-done
  7.7 0.0 collective-permute-done.1
  7.7 0.0 copy-done.4
  7.7 0.0 copy-start
  7.7 0.9 %copy-done = f32[16,2,8,256]{3,2,1,0:T(8,128)S(1)} copy-done((f32[16,2,8,256]{3,2,1,0:T(8,128)S(1)}, f32[16,2,8,256]{3,2,1,0:T(8,128)}, u32[]{:S(2)}) %copy-start) | copy-done | bytes 262168
  8.7 0.0 copy-start.1
  8.7 0.9 %copy-done.1 = f32[16,8,256]{2,1,0:T(8,128)S(1)} copy-done((f32[16,8,256]{2,1,0:T(8,128)S(1)}, f32[16,8,256]{2,1,0:T(8,128)}, u32[]{:S(2)}) %copy-start.1) | copy-done | bytes 131096
  9.6 0.0 copy-start.2
  9.6 0.9 %copy-done.2 = f32[256,128]{1,0:T(8,128)S(1)} copy-done((f32[256,128]{1,0:T(8,128)S(1)}, f32[256,128]{1,0:T(8,128)}, u32[]{:S(2)}) %copy-start.2) | copy-done | bytes 131096
  10.5 0.0 copy-start.3
  10.5 0.7 %copy-done.3 = f32[2,8,256]{2,1,0:T(8,128)S(1)} copy-done((f32[2,8,256]{2,1,0:T(8,128)S(1)}, f32[2,8,256]{2,1,0:T(8,128)}, u32[]{:S(2)}) %copy-start.3) | copy-done | bytes 16408
  11.2 0.0 copy-start.5
  11.2 0.7 %copy-done.5 = f32[8,128]{1,0:T(8,128)S(1)} copy-done((f32[8,128]{1,0:T(8,128)S(1)}, f32[8,128]{1,0:T(8,128)}, u32[]{:S(2)}) %copy-start.5) | copy-done | bytes 4120
  11.9 4.7 %advance.1 = f32[544,128]{1,0:T(8,128)S(1)} custom-call(f32[128,256]{1,0:T(8,128)S(1)} %bitcast.18, f32[128,256]{1,0:T(8,128)S(1)} %bitcast.17, f32[256,256]{1,0:T(8,128)S(1)} %bitcast.16, f32[256,256]{1,0:T(8,128)S(1)} %bitcast.15, f32[16,256]{1,0:T(8,128)S(1)} %bitcast.20, f32[16,256]{1,0:T(8,128)S(1)} %bitcast.19, f32[256,128]{1,0:T(8,128)S(1)} %copy-done.2, ...), custom_call_target="tpu_custom_call" | custom-call | tf_op jit(solution)/shard_map/advance/pallas_call | solution.py:371
  16.6 17.4 %all_to_all.10 = f32[32,17,1,128]{3,2,1,0:T(1,128)S(1)} all-to-all(f32[32,17,1,128]{3,2,1,0:T(1,128)S(1)} %bitcast.11), channel_id=1, replica_groups=mesh['mem'=2,'gx'=16] {'mem','gx'}, dimensions={0} | all-to-all | bytes 557056 | tf_op jit(solution)/shard_map/all_to_all | solution.py:333
  34.0 1.3 %project.1 = f32[384,128]{1,0:T(8,128)S(1)} custom-call(f32[544,128]{1,0:T(8,128)S(1)} %bitcast.12), custom_call_target="tpu_custom_call" | custom-call | tf_op jit(solution)/shard_map/project/pallas_call | solution.py:382
  35.3 11.7 %all_to_all.11 = f32[32,12,1,128]{3,2,1,0:T(1,128)S(1)} all-to-all(f32[32,12,1,128]{3,2,1,0:T(1,128)S(1)} %bitcast.14), channel_id=1, replica_groups=mesh['mem'=2,'gx'=16] {'mem','gx'}, dimensions={0} | all-to-all | bytes 393216 | tf_op jit(solution)/shard_map/all_to_all | solution.py:333
  47.0 1.0 %gather.1 = f32[384,128]{1,0:T(8,128)} custom-call(f32[384,128]{1,0:T(8,128)S(1)} %bitcast.13), custom_call_target="tpu_custom_call" | custom-call | tf_op jit(solution)/shard_map/gather/pallas_call | solution.py:393
Async XLA Ops:
  0.0 7.7 %copy-start.4 = (f32[16,32]{1,0:T(8,128)S(1)}, f32[16,32]{1,0:T(8,128)}, u32[]{:S(2)}) copy-start(f32[16,32]{1,0:T(8,128)} %fm.1) | copy-start | bytes 6148
  0.0 7.7 %collective-permute-start.1 = (f32[16,2,8,256]{3,2,1,0:T(8,128)}, f32[16,2,8,256]{3,2,1,0:T(8,128)S(1)}, u32[]{:S(2)}, u32[]{:S(2)}) collective-permute-start(f32[16,2,8,256]{3,2,1,0:T(8,128)} %param.7), channel_id=1, source_target_pairs={{0,1},{1,2},{2,3},{3,4},{4,5},{5,6},{6,7},{7,8},{8,9},{9,10},{10,1... | collective-permute-start | bytes 786440 | tf_op jit(solution)/shard_map/ppermute | solution.py:367
  2.6 5.1 %collective-permute-start = (f32[16,8,256]{2,1,0:T(8,128)}, f32[16,8,256]{2,1,0:T(8,128)S(1)}, u32[]{:S(2)}, u32[]{:S(2)}) collective-permute-start(f32[16,8,256]{2,1,0:T(8,128)} %param.6), channel_id=1, source_target_pairs={{0,1},{1,2},{2,3},{3,4},{4,5},{5,6},{6,7},{7,8},{8,9},{9,10},{10,1... | collective-permute-start | bytes 393224 | tf_op jit(solution)/shard_map/ppermute | solution.py:367
  2.7 5.1 %collective-permute-start.2 = (f32[2,8,256]{2,1,0:T(8,128)}, f32[2,8,256]{2,1,0:T(8,128)S(1)}, u32[]{:S(2)}, u32[]{:S(2)}) collective-permute-start(f32[2,8,256]{2,1,0:T(8,128)} %param.8), channel_id=1, source_target_pairs={{0,1},{1,2},{2,3},{3,4},{4,5},{5,6},{6,7},{7,8},{8,9},{9,10},{10,1... | collective-permute-start | bytes 49160 | tf_op jit(solution)/shard_map/ppermute | solution.py:367
  7.7 1.0 %copy-start = (f32[16,2,8,256]{3,2,1,0:T(8,128)S(1)}, f32[16,2,8,256]{3,2,1,0:T(8,128)}, u32[]{:S(2)}) copy-start(f32[16,2,8,256]{3,2,1,0:T(8,128)} %param.7) | copy-start | bytes 786436
  8.7 0.9 %copy-start.1 = (f32[16,8,256]{2,1,0:T(8,128)S(1)}, f32[16,8,256]{2,1,0:T(8,128)}, u32[]{:S(2)}) copy-start(f32[16,8,256]{2,1,0:T(8,128)} %param.6) | copy-start | bytes 393220
  9.6 0.9 %copy-start.2 = (f32[256,128]{1,0:T(8,128)S(1)}, f32[256,128]{1,0:T(8,128)}, u32[]{:S(2)}) copy-start(f32[256,128]{1,0:T(8,128)} %fy.1) | copy-start | bytes 393220
  10.5 0.7 %copy-start.3 = (f32[2,8,256]{2,1,0:T(8,128)S(1)}, f32[2,8,256]{2,1,0:T(8,128)}, u32[]{:S(2)}) copy-start(f32[2,8,256]{2,1,0:T(8,128)} %param.8) | copy-start | bytes 49156
  11.2 0.7 %copy-start.5 = (f32[8,128]{1,0:T(8,128)S(1)}, f32[8,128]{1,0:T(8,128)}, u32[]{:S(2)}) copy-start(f32[8,128]{1,0:T(8,128)} %fx.1) | copy-start | bytes 12292

commit v2 on v1

--- a/solution.py
+++ b/solution.py
@@ -145,78 +145,194 @@
     )
 
 
-def advance_kernel(
-    n_gx, left_d, own_d, left_m, own_m, left_w, own_w, fy, fx, fm, out, state, *tiled
+def start_kernel(d, m, w, fy, own_d, own_m, own_w, own_fy, near, far, sems):
+    tiles = own_d.shape[0]
+    copies = []
+    for whole, cut in ((d, own_d), (m, own_m), (w, own_w)):
+        for t in range(tiles):
+            copies.append((whole.at[:, pl.ds(t * LANES, LANES)], cut.at[t]))
+    copies.append((fy, own_fy))
+    copies = [
+        pltpu.make_async_copy(source, target, sems.at[i])
+        for i, (source, target) in enumerate(copies)
+    ]
+    for copy in copies:
+        copy.start()
+    odd = lax.rem(lax.axis_index("gx"), 2)
+    rows = own_w.shape[1] // 2
+    half = rows // 2
+    for copy in copies:
+        copy.wait()
+    for target, first in ((near, half * (1 - odd)), (far, half * odd)):
+        for t in range(tiles):
+            base = 0
+            for cut in (own_d, own_m, own_w):
+                lines = cut.shape[1] // rows
+                for i in range(half):
+                    target[t, pl.ds(base + i, lines, stride=half), :] = cut[
+                        t, pl.ds(first + i, lines, stride=rows), :
+                    ]
+                base += lines * half
+
+
+class Strip:
+    def __init__(self, group, own, near, far):
+        self.group, self.own, self.near, self.far = group, own, near, far
+        self.rows = own[2].shape[1] // 2
+        self.half = self.rows // 2
+        self.members = own[0].shape[1] // self.rows
+        self.tiles = own[0].shape[0]
+        self.odd = lax.rem(lax.axis_index("gx"), 2)
+        self.sign = (1 - 2 * self.odd).astype(jnp.float32)
+
+    def every(self, ref, first, count, stride):
+        parts = [ref[t, pl.ds(first, count, stride=stride), :] for t in range(self.tiles)]
+        return jnp.concatenate(parts, axis=1)
+
+    def place(self, x):
+        if x < self.half:
+            ref, at, lines = self.far, x, self.half
+        elif x < self.half + self.rows:
+            ref, at, lines = self.own, x - self.half, self.rows
+        else:
+            ref, at, lines = self.near, x - self.half - self.rows, self.half
+        return ref, self.odd * (lines - 1) + (1 - 2 * self.odd) * at, lines
+
+    def load(self, x):
+        ref, at, lines = self.place(x)
+        if ref is self.own:
+            d, m = ref[0], ref[1]
+            base = 0
+        else:
+            d = m = ref
+            base = self.members * lines
+        first = self.group * SUBLANES
+        rho = self.every(d, first * lines + at, SUBLANES, lines)
+        mx = self.every(m, base + first * 2 * lines + at, SUBLANES, 2 * lines)
+        my = self.every(m, base + (first * 2 + 1) * lines + at, SUBLANES, 2 * lines)
+        return rho, self.sign * mx, my
+
+    def wish(self, x):
+        ref, at, lines = self.place(x)
+        if ref is self.own:
+            ref, base = ref[2], 0
+        else:
+            base = 3 * self.members * lines
+        line = [self.every(ref, base + c * lines + at, 1, 1) for c in range(2)]
+        line[0] = self.sign * line[0]
+        return tuple(jnp.broadcast_to(a, (SUBLANES, a.shape[1])) for a in line)
+
+
+def march(count, computed, fetch, wish, emit):
+    sections = len(computed) - 1
+    known, terms, faces = {}, {}, {}
+
+    def value(s, x):
+        if (s, x) not in known:
+            if x in computed[s]:
+                new = section(
+                    cell(s - 1, x), face(s - 1, x - 1), face(s - 1, x), wish(x)
+                )
+                if s % 2 == 0:
+                    new = tuple(0.5 * a + 0.5 * b for a, b in zip(value(s - 2, x), new))
+                emit(s, x, new)
+            else:
+                new = fetch(s, x)
+            known[s, x] = new
+        return known[s, x]
+
+    def cell(s, x):
+        if (s, x) not in terms:
+            terms[s, x] = cell_terms(value(s, x))
+        return terms[s, x]
+
+    def face(s, x):
+        if (s, x) not in faces:
+            faces[s, x] = x_face(cell(s, x), cell(s, x + 1))
+        return faces[s, x]
+
+    for t in range(count):
+        for s in range(1, sections + 1):
+            if t - s in computed[s]:
+                value(s, t - s)
+
+
+def edge_line(s, x, half, members):
+    return ((s - 1) * 2 + x - half - s) * 3 * members
+
+
+def turn_projected(state, fy, members, c, count):
+    lines = count * members
+    block = state[pl.ds(c * lines, lines), :]
+    along = jnp.dot(block, fy[...], precision=HIGHEST, preferred_element_type=jnp.float32)
+    return along.T
+
+
+def inner_kernel(own_d, own_m, own_w, near, fy, edges, turned, state):
+    rows = own_w.shape[1] // 2
+    half = rows // 2
+    members = own_d.shape[1] // rows
+    sections = 2 * STEPS
+    count = 2 * rows
+    for group in range(members // SUBLANES):
+        strip = Strip(group, (own_d, own_m, own_w), near, None)
+
+        def emit(s, x, q):
+            if s == sections:
+                for c in range(3):
+                    at = (c * half + x - rows) * members + group * SUBLANES
+                    state[pl.ds(at, SUBLANES), :] = q[c]
+            elif x - half - s in (0, 1):
+                for c in range(3):
+                    at = edge_line(s, x, half, members) + c * members + group * SUBLANES
+                    edges[pl.ds(at, SUBLANES), :] = q[c]
+
+        computed = [range(0)] + [range(half + s, count - s) for s in range(1, sections + 1)]
+        march(count, computed, lambda s, x: strip.load(x), strip.wish, emit)
+    for c in range(3):
+        part = turn_projected(state, fy, members, c, half)
+        turned[c] = jnp.concatenate([jnp.zeros_like(part), part], axis=1)
+
+
+def outer_kernel(
+    n_gx, own_d, own_m, own_w, far, fy, edges, turned, fx, fm, out, state
 ):
-    rows = own_w.shape[0] // 2
-    members = own_d.shape[0] // rows
-    tiles = own_d.shape[1] // LANES
-    for whole, cut in zip((left_d, own_d, left_m, own_m), tiled):
-        for t in range(tiles):
-            cut[t] = whole[:, t * LANES : (t + 1) * LANES]
-    left_d, own_d, left_m, own_m = tiled
-
-    def every(ref, first, stride):
-        return jnp.concatenate(
-            [ref[t, pl.ds(first, SUBLANES, stride=stride), :] for t in range(tiles)], axis=1
-        )
-
-    count = 2 * rows
+    rows = own_w.shape[1] // 2
+    half = rows // 2
+    members = own_d.shape[1] // rows
     sections = 2 * STEPS
     for group in range(members // SUBLANES):
-        def load(x):
-            d, m = (left_d, left_m) if x < rows else (own_d, own_m)
-            at = x % rows
-            first = group * SUBLANES
-            return (
-                every(d, first * rows + at, rows),
-                every(m, first * 2 * rows + at, 2 * rows),
-                every(m, (first * 2 + 1) * rows + at, 2 * rows),
-            )
-
-        def wish(x):
-            w = left_w if x < rows else own_w
-            at = x % rows
-            return tuple(
-                jnp.broadcast_to(w[pl.ds(c * rows + at, 1), :], (SUBLANES, w.shape[1]))
-                for c in range(2)
-            )
-
-        cells = [{} for _ in range(sections + 1)]
-        faces = [{} for _ in range(sections)]
-        for t in range(count):
-            cells[0][t] = cell_terms(load(t))
-            if t:
-                faces[0][t - 1] = x_face(cells[0][t - 1], cells[0][t])
-            for s in range(1, sections + 1):
-                x = t - s
-                if x < s:
-                    break
-                new = section(cells[s - 1][x], faces[s - 1][x - 1], faces[s - 1][x], wish(x))
-                if s % 2 == 0:
-                    old = cells[s - 2][x]["q"]
-                    new = tuple(0.5 * a + 0.5 * b for a, b in zip(old, new))
-                if s < sections:
-                    cells[s][x] = cell_terms(new)
-                    if x > s:
-                        faces[s][x - 1] = x_face(cells[s][x - 1], cells[s][x])
-                else:
-                    at = (x - sections) * members + group * SUBLANES
-                    for c in range(3):
-                        state[pl.ds(c * rows * members + at, SUBLANES), :] = new[c]
+        strip = Strip(group, (own_d, own_m, own_w), None, far)
+
+        def fetch(s, x):
+            if s == 0:
+                return strip.load(x)
+            at = edge_line(s, x, half, members) + group * SUBLANES
+            return tuple(edges[pl.ds(at + c * members, SUBLANES), :] for c in range(3))
+
+        def emit(s, x, q):
+            if s == sections:
+                for c in range(3):
+                    at = (c * half + x - half) * members + group * SUBLANES
+                    state[pl.ds(at, SUBLANES), :] = q[c]
+
+        computed = [range(0)] + [range(s, half + s) for s in range(1, sections + 1)]
+        march(rows + sections, computed, fetch, strip.wish, emit)
     devices = 2 * n_gx
     shares = fy.shape[1] // devices
     height = out.shape[0] // devices
+    odd = lax.rem(lax.axis_index("gx"), 2)
+    sign = (1 - 2 * odd).astype(jnp.float32)
     for c in range(3):
-        block = state[pl.ds(c * rows * members, rows * members), :]
-        along = jnp.dot(block, fy[...], precision=HIGHEST, preferred_element_type=jnp.float32)
-        turned = along.T
+        part = turn_projected(state, fy, members, c, half)
+        whole = jnp.concatenate([part, turned[c][:, half * members :]], axis=1)
+        if c == 1:
+            whole = sign * whole
         for r in range(shares):
-            out[pl.ds(c * shares + r, devices, stride=height), :] = turned[
+            out[pl.ds(c * shares + r, devices, stride=height), :] = whole[
                 r * devices : (r + 1) * devices
             ]
     mem, gx = lax.axis_index("mem"), lax.axis_index("gx")
-    half = rows // 2
     for r in range(half):
         line = fx[pl.ds(mem * half + r, 1), :]
         out[pl.ds(3 * shares + r, devices, stride=height), :] = jnp.broadcast_to(
@@ -271,12 +387,9 @@
                 axis=1,
             )
     halves = [inp[pl.ds(pieces + r, devices, stride=height), :] for r in range(half)]
-    lines = []
-    for r in range(half):
-        late = halves[r][n_gx:]
-        lines.append(pltpu.roll(late, 1, 0))
-    for r in range(half):
-        lines.append(halves[r][:n_gx])
+    lines = [a[:n_gx] for a in halves] + [a[n_gx:] for a in halves]
+    odd = lax.broadcasted_iota(jnp.int32, (n_gx, LANES), 0) % 2 == 1
+    lines = [jnp.where(odd, lines[rows - 1 - r], lines[r]) for r in range(rows)]
     fx = jnp.concatenate(lines, axis=0)
     core = jnp.dot(fx.T, blocks[...], precision=HIGHEST, preferred_element_type=jnp.float32)
     high = out.shape[0] // devices
@@ -343,6 +456,7 @@
         n_mem == 2
         and rows == 4 * STEPS == SUBLANES
         and members == n_gx
+        and n_gx % 2 == 0
         and members * rows == LANES
         and members % SUBLANES == 0
         and cells_y % LANES == 0
@@ -362,20 +476,46 @@
     devices = 2 * n_gx
     rx, ry, rm = factor_x.shape[1], factor_y.shape[1], factor_m.shape[1]
     shares = ry // devices
-    forward = [(i, (i + 1) % n_gx) for i in range(n_gx)]
-    own = (density, momenta, desired)
-    left = [lax.ppermute(a, "gx", forward) for a in own]
-    flat = [a.reshape(-1, cells_y) for pair in zip(left, own) for a in pair]
     params = pltpu.CompilerParams(vmem_limit_bytes=32 * 1024 * 1024)
-    height = 3 * shares + rows // 2 + 1
+    vmem = pl.BlockSpec(memory_space=pltpu.VMEM)
+    anywhere = pl.BlockSpec(memory_space=pltpu.HBM)
+    tiles = cells_y // LANES
+    half = rows // 2
+    own = [a.reshape(-1, cells_y) for a in (density, momenta, desired)]
+    lines = [a.shape[0] for a in own]
+    shape = lambda *dims: jax.ShapeDtypeStruct(dims, jnp.float32)
+    *own, fy, near, far = pl.pallas_call(
+        start_kernel,
+        out_shape=[shape(tiles, n, LANES) for n in lines]
+        + [shape(*factor_y.shape)]
+        + [shape(tiles, sum(lines) // 2, LANES)] * 2,
+        in_specs=[anywhere] * 4,
+        out_specs=[vmem] * 6,
+        scratch_shapes=[pltpu.SemaphoreType.DMA((3 * tiles + 1,))],
+        compiler_params=params,
+        name="start",
+    )(*[pltpu.with_memory_space_constraint(a, pltpu.HBM) for a in (*own, factor_y)])
+    near = lax.ppermute(near, "gx", [(i, i ^ 1) for i in range(n_gx)])
+    far = lax.ppermute(far, "gx", [(i, (i - 1 + i % 2 * 2) % n_gx) for i in range(n_gx)])
+    sections = 2 * STEPS
+    edges, turned = pl.pallas_call(
+        inner_kernel,
+        out_shape=[
+            shape((sections - 1) * 2 * 3 * members, cells_y),
+            shape(3, ry, LANES),
+        ],
+        scratch_shapes=[pltpu.VMEM((3 * half * members, cells_y), jnp.float32)],
+        compiler_params=params,
+        name="inner",
+    )(*own, near, fy)
+    height = 3 * shares + half + 1
     sent = pl.pallas_call(
-        functools.partial(advance_kernel, n_gx),
-        out_shape=jax.ShapeDtypeStruct((devices * height, LANES), jnp.float32),
-        scratch_shapes=[pltpu.VMEM((3 * rows * members, cells_y), jnp.float32)]
-        + [pltpu.VMEM((cells_y // LANES, a.shape[0], LANES), jnp.float32) for a in flat[:4]],
+        functools.partial(outer_kernel, n_gx),
+        out_shape=shape(devices * height, LANES),
+        scratch_shapes=[pltpu.VMEM((3 * half * members, cells_y), jnp.float32)],
         compiler_params=params,
-        name="advance",
-    )(*flat, factor_y, factor_x, factor_m)
+        name="outer",
+    )(*own, far, fy, edges, turned, factor_x, factor_m)
     got = exchange(sent, devices)
     lows = rm // 2
     high = 3 * shares * lows * SUBLANES // LANES

time: 48.2 us -> 42.4 us (0.88)
  local copies, waits for them, and re-layouts: 4.16 us -> 0.01 us
  starting transfers between devices: 4.26 us -> 2.74 us
  waiting for transfers between devices: 3.45 us -> 2.23 us
  blocking collectives: 29 us -> 29.6 us
  Pallas kernels: 7 us -> 7.59 us
    unnamed x12 -> x4, local copies, waits for them, and re-layouts: 4.16 us -> 0.01 us
    ppermute x3 -> x2, starting transfers between devices: 4.26 us -> 2.74 us  [the longest x1 2.62 us: on_device(): lax.ppermute(far, 'gx', [(i, (i - 1 + i % 2 * 2) % n_gx) for i in range(n...]
    ppermute x3 -> x2, waiting for transfers between devices: 3.45 us -> 2.23 us  [the longest x1 2.23 us: on_device(): lax.ppermute(far, 'gx', [(i, (i - 1 + i % 2 * 2) % n_gx) for i in range(n...]
    pallas_call x1 -> x3, Pallas kernels: 4.72 us -> 5.3 us  [the longest x1 2.65 us: on_device(): pl.pallas_call(inner_kernel, out_shape=[shape((sections - 1) * 2 * 3 * me...]
    all_to_all x2, blocking collectives: 29 us -> 29.6 us  [exchange(): lax.all_to_all(block, ('mem', 'gx'), split_axis=0, concat_axis=0, tiled=T...]
  transfers between devices with their start and end apart: 3 -> 2, of which waited for: 1 -> 1; matrix products, arithmetic and copies ran while one was open for 0% -> 0% of each run, Pallas kernels for 0% -> 6%
where the time goes in v2:
time: 42.4 us; the launch traced here: 42.2 us
  blocking collectives  29.6 us (70%)
  Pallas kernels  7.59 us (18%)
  starting transfers between devices  2.74 us (6%)
  waiting for transfers between devices  2.23 us (5%)
    all_to_all x2, blocking collectives, exchange(): lax.all_to_all(block, ('mem', 'gx'), split_axis=0, concat_axis=0, tiled=T...  29.6 us
    pallas_call x1, Pallas kernels, on_device(): pl.pallas_call(inner_kernel, out_shape=[shape((sections - 1) * 2 * 3 * me...  2.65 us
    ppermute x1, starting transfers between devices, on_device(): lax.ppermute(far, 'gx', [(i, (i - 1 + i % 2 * 2) % n_gx) for i in range(n...  2.62 us
    ppermute x1, waiting for transfers between devices, on_device(): lax.ppermute(far, 'gx', [(i, (i - 1 + i % 2 * 2) % n_gx) for i in range(n...  2.23 us
    pallas_call x1, Pallas kernels, on_device(): pl.pallas_call(functools.partial(outer_kernel, n_gx), out_shape=shape(dev...  1.37 us
    pallas_call x1, Pallas kernels, on_device(): pl.pallas_call(functools.partial(project_kernel, n_gx, rows, shares, rm),...  1.29 us
    pallas_call x1, Pallas kernels, on_device(): pl.pallas_call(start_kernel, out_shape=[shape(tiles, n, LANES) for n in l...  1.28 us
    pallas_call x1, Pallas kernels, on_device(): pl.pallas_call(functools.partial(gather_kernel, shares, lows), out_shape=...  0.99 us
  transfers between devices with their start and end apart: 2, of which 1 were waited for; matrix products, arithmetic and copies ran while one was open for 0% of the time, Pallas kernels for 6%

profile of v2, /device:TPU:1, one launch (start us, length us, event | category | flops | bytes accessed | tf_op | source)
XLA Modules:
  0.0 42.2 jit_solution(10321616520969759516)
XLA Ops:
  0.0 1.3 %start.1 = (f32[2,128,128]{2,1,0:T(8,128)S(1)}, f32[2,256,128]{2,1,0:T(8,128)S(1)}, f32[2,16,128]{2,1,0:T(8,128)S(1)}, f32[256,128]{1,0:T(8,128)S(1)}, f32[2,200...) custom-call(f32[128,256]{1,0:T(8,128)} %bitcast.13, f32[256,256]{1,0:T(8,128)} %bitcast.12, f32[16,256]{1,0:T(8,128)} %bitcast.14, ...), custom_call_target="tpu_custom_call" | custom-call | tf_op jit(solution)/shard_map/start/pallas_call | solution.py:487
  1.3 0.1 collective-permute-start.1
  1.4 2.6 %collective-permute-start = (f32[2,200,128]{2,1,0:T(8,128)S(1)}, f32[2,200,128]{2,1,0:T(8,128)S(1)}, u32[]{:S(2)}, u32[]{:S(2)}) collective-permute-start(f32[2,200,128]{2,1,0:T(8,128)S(1)} %get-tuple-element.16), channel_id=1, source_target_pairs={{0,15},{1,2},{2,1},{3,4},{4,3},{5,6},{6,5},{7,8},{8,7},{9,10},{10,... | collective-permute-start | bytes 614408 | tf_op jit(solution)/shard_map/ppermute | solution.py:499
  4.0 0.0 collective-permute-done.1.near
  4.0 0.0 copy-start
  4.0 0.0 copy-start.1
  4.0 2.7 %inner.1 = (f32[288,256]{1,0:T(8,128)S(1)}, f32[3,128,128]{2,1,0:T(8,128)S(1)}) custom-call(f32[2,128,128]{2,1,0:T(8,128)S(1)} %get-tuple-element.13.own_d, f32[2,256,128]{2,1,0:T(8,128)S(1)} %get-tuple-element.14.own_m, f32[2,16,128]{2,1,0:T(8,128)S(1)} %get-tuple-element.15.own_w, f32[2,200,128]{2,1,0:T(8,128)S(1)} %collective-permute-done.1.near, ...), custom_call_target="tpu_custom_call" | custom-call | tf_op jit(solution)/shard_map/inner/pallas_call | solution.py:501
  6.7 2.2 %collective-permute-done.far = f32[2,200,128]{2,1,0:T(8,128)S(1)} collective-permute-done((f32[2,200,128]{2,1,0:T(8,128)S(1)}, f32[2,200,128]{2,1,0:T(8,128)S(1)}, u32[]{:S(2)}, u32[]{:S(2)}) %collective-permute-start) | collective-permute-done | bytes 204832 | tf_op jit(solution)/shard_map/ppermute | solution.py:499
  8.9 0.0 copy-done
  8.9 0.0 copy-done.1
  8.9 1.4 %outer.1 = f32[544,128]{1,0:T(8,128)S(1)} custom-call(f32[2,128,128]{2,1,0:T(8,128)S(1)} %get-tuple-element.13.own_d, f32[2,256,128]{2,1,0:T(8,128)S(1)} %get-tuple-element.14.own_m, f32[2,16,128]{2,1,0:T(8,128)S(1)} %get-tuple-element.15.own_w, f32[2,200,128]{2,1,0:T(8,128)S(1)} %collective-permute-done.far, f32[256,128]{1,0:T(8,128)S(1)} %get-tuple-element.17.fy, ...), custom_call_target="tpu_custom_call" | custom-call | tf_op jit(solution)/shard_map/outer/pallas_call | solution.py:512
  10.3 17.9 %all_to_all.10 = f32[32,17,1,128]{3,2,1,0:T(1,128)S(1)} all-to-all(f32[32,17,1,128]{3,2,1,0:T(1,128)S(1)} %bitcast.8), channel_id=1, replica_groups=mesh['mem'=2,'gx'=16] {'mem','gx'}, dimensions={0} | all-to-all | bytes 557056 | tf_op jit(solution)/shard_map/all_to_all | solution.py:446
  28.2 1.3 %project.1 = f32[384,128]{1,0:T(8,128)S(1)} custom-call(f32[544,128]{1,0:T(8,128)S(1)} %bitcast.9), custom_call_target="tpu_custom_call" | custom-call | tf_op jit(solution)/shard_map/project/pallas_call | solution.py:522
  29.5 11.7 %all_to_all.11 = f32[32,12,1,128]{3,2,1,0:T(1,128)S(1)} all-to-all(f32[32,12,1,128]{3,2,1,0:T(1,128)S(1)} %bitcast.11), channel_id=1, replica_groups=mesh['mem'=2,'gx'=16] {'mem','gx'}, dimensions={0} | all-to-all | bytes 393216 | tf_op jit(solution)/shard_map/all_to_all | solution.py:446
  41.2 1.0 %gather.1 = f32[384,128]{1,0:T(8,128)} custom-call(f32[384,128]{1,0:T(8,128)S(1)} %bitcast.10), custom_call_target="tpu_custom_call" | custom-call | tf_op jit(solution)/shard_map/gather/pallas_call | solution.py:533
Async XLA Ops:
  1.3 2.7 %collective-permute-start.1 = (f32[2,200,128]{2,1,0:T(8,128)S(1)}, f32[2,200,128]{2,1,0:T(8,128)S(1)}, u32[]{:S(2)}, u32[]{:S(2)}) collective-permute-start(f32[2,200,128]{2,1,0:T(8,128)S(1)} %get-tuple-element.18), channel_id=1, source_target_pairs={{0,1},{1,0},{2,3},{3,2},{4,5},{5,4},{6,7},{7,6},{8,9},{9,8},{10,11... | collective-permute-start | bytes 614408 | tf_op jit(solution)/shard_map/ppermute | solution.py:498
  1.4 7.5 %collective-permute-start = (f32[2,200,128]{2,1,0:T(8,128)S(1)}, f32[2,200,128]{2,1,0:T(8,128)S(1)}, u32[]{:S(2)}, u32[]{:S(2)}) collective-permute-start(f32[2,200,128]{2,1,0:T(8,128)S(1)} %get-tuple-element.16), channel_id=1, source_target_pairs={{0,15},{1,2},{2,1},{3,4},{4,3},{5,6},{6,5},{7,8},{8,7},{9,10},{10,... | collective-permute-start | bytes 614408 | tf_op jit(solution)/shard_map/ppermute | solution.py:499
  4.0 4.9 %copy-start = (f32[16,32]{1,0:T(8,128)S(1)}, f32[16,32]{1,0:T(8,128)}, u32[]{:S(2)}) copy-start(f32[16,32]{1,0:T(8,128)} %fm.1) | copy-start | bytes 6148
  4.0 4.9 %copy-start.1 = (f32[8,128]{1,0:T(8,128)S(1)}, f32[8,128]{1,0:T(8,128)}, u32[]{:S(2)}) copy-start(f32[8,128]{1,0:T(8,128)} %fx.1) | copy-start | bytes 12292

commit v3 on v2

--- a/solution.py
+++ b/solution.py
@@ -15,6 +15,7 @@
 DTIME = 0.2
 
 HIGHEST = lax.Precision.HIGHEST
+HIGH = lax.Precision.HIGH
 LANES = 128
 SUBLANES = 8
 
@@ -145,48 +146,51 @@
     )
 
 
-def start_kernel(d, m, w, fy, own_d, own_m, own_w, own_fy, near, far, sems):
+def start_kernel(d, m, w, fy, own_d, own_m, own_w, own_fy, far, near, sems):
     tiles = own_d.shape[0]
-    copies = []
+    odd = lax.rem(lax.axis_index("gx"), 2)
+    rows = own_w.shape[1] // 2
+    half = rows // 2
+    pairs = []
     for whole, cut in ((d, own_d), (m, own_m), (w, own_w)):
         for t in range(tiles):
-            copies.append((whole.at[:, pl.ds(t * LANES, LANES)], cut.at[t]))
-    copies.append((fy, own_fy))
+            pairs.append((whole.at[:, pl.ds(t * LANES, LANES)], cut.at[t]))
+    pairs.append((fy, own_fy))
     copies = [
         pltpu.make_async_copy(source, target, sems.at[i])
-        for i, (source, target) in enumerate(copies)
+        for i, (source, target) in enumerate(pairs)
     ]
     for copy in copies:
         copy.start()
-    odd = lax.rem(lax.axis_index("gx"), 2)
-    rows = own_w.shape[1] // 2
-    half = rows // 2
-    for copy in copies:
-        copy.wait()
-    for target, first in ((near, half * (1 - odd)), (far, half * odd)):
+    base = 0
+    for n, cut in enumerate((own_d, own_m, own_w)):
+        lines = cut.shape[1] // rows
         for t in range(tiles):
-            base = 0
-            for cut in (own_d, own_m, own_w):
-                lines = cut.shape[1] // rows
+            copies[n * tiles + t].wait()
+            for target, first in ((far.at[t], half * odd), (near[t], half * (1 - odd))):
                 for i in range(half):
-                    target[t, pl.ds(base + i, lines, stride=half), :] = cut[
+                    target[pl.ds(base + i, lines, stride=half), :] = cut[
                         t, pl.ds(first + i, lines, stride=rows), :
                     ]
-                base += lines * half
+        base += lines * half
+    copies[-1].wait()
 
 
 class Strip:
     def __init__(self, group, own, near, far):
-        self.group, self.own, self.near, self.far = group, own, near, far
         self.rows = own[2].shape[1] // 2
         self.half = self.rows // 2
         self.members = own[0].shape[1] // self.rows
         self.tiles = own[0].shape[0]
+        cut = lambda ref: [ref.at[t] for t in range(self.tiles)]
+        self.group, self.own = group, tuple(cut(a) for a in own)
+        self.near = near
+        self.far = None if far is None else cut(far)
         self.odd = lax.rem(lax.axis_index("gx"), 2)
         self.sign = (1 - 2 * self.odd).astype(jnp.float32)
 
     def every(self, ref, first, count, stride):
-        parts = [ref[t, pl.ds(first, count, stride=stride), :] for t in range(self.tiles)]
+        parts = [ref[t][pl.ds(first, count, stride=stride), :] for t in range(self.tiles)]
         return jnp.concatenate(parts, axis=1)
 
     def place(self, x):
@@ -264,11 +268,12 @@
 def turn_projected(state, fy, members, c, count):
     lines = count * members
     block = state[pl.ds(c * lines, lines), :]
-    along = jnp.dot(block, fy[...], precision=HIGHEST, preferred_element_type=jnp.float32)
+    along = jnp.dot(block, fy[...], precision=HIGH, preferred_element_type=jnp.float32)
     return along.T
 
 
-def inner_kernel(own_d, own_m, own_w, near, fy, edges, turned, state):
+def inner_kernel(own_d, own_m, own_w, fy, *rest):
+    *near, edges, turned, state = rest
     rows = own_w.shape[1] // 2
     half = rows // 2
     members = own_d.shape[1] // rows
@@ -374,7 +379,7 @@
                 )
             )
     diagonal = jnp.concatenate(lines, axis=0)
-    mixed = jnp.dot(lhs, diagonal, precision=HIGHEST, preferred_element_type=jnp.float32)
+    mixed = jnp.dot(lhs, diagonal, precision=HIGH, preferred_element_type=jnp.float32)
     lows = rm // 2
     orders = (range(pieces), [j % pieces for j in range(pieces - shares, 2 * pieces - shares)])
     for x in range(rows):
@@ -391,7 +396,7 @@
     odd = lax.broadcasted_iota(jnp.int32, (n_gx, LANES), 0) % 2 == 1
     lines = [jnp.where(odd, lines[rows - 1 - r], lines[r]) for r in range(rows)]
     fx = jnp.concatenate(lines, axis=0)
-    core = jnp.dot(fx.T, blocks[...], precision=HIGHEST, preferred_element_type=jnp.float32)
+    core = jnp.dot(fx.T, blocks[...], precision=HIGH, preferred_element_type=jnp.float32)
     high = out.shape[0] // devices
     for t in range(3):
         tall[t] = core[:, t * LANES : (t + 1) * LANES]
@@ -478,25 +483,25 @@
     shares = ry // devices
     params = pltpu.CompilerParams(vmem_limit_bytes=32 * 1024 * 1024)
     vmem = pl.BlockSpec(memory_space=pltpu.VMEM)
-    anywhere = pl.BlockSpec(memory_space=pltpu.HBM)
+    anywhere = pl.BlockSpec(memory_space=pl.ANY)
     tiles = cells_y // LANES
     half = rows // 2
     own = [a.reshape(-1, cells_y) for a in (density, momenta, desired)]
     lines = [a.shape[0] for a in own]
     shape = lambda *dims: jax.ShapeDtypeStruct(dims, jnp.float32)
-    *own, fy, near, far = pl.pallas_call(
+    packed = (sum(lines) // 2, LANES)
+    *own, fy, far, near = pl.pallas_call(
         start_kernel,
         out_shape=[shape(tiles, n, LANES) for n in lines]
-        + [shape(*factor_y.shape)]
-        + [shape(tiles, sum(lines) // 2, LANES)] * 2,
+        + [shape(*factor_y.shape), shape(tiles, *packed), [shape(*packed)] * tiles],
         in_specs=[anywhere] * 4,
-        out_specs=[vmem] * 6,
+        out_specs=[vmem] * 5 + [[vmem] * tiles],
         scratch_shapes=[pltpu.SemaphoreType.DMA((3 * tiles + 1,))],
         compiler_params=params,
         name="start",
     )(*[pltpu.with_memory_space_constraint(a, pltpu.HBM) for a in (*own, factor_y)])
-    near = lax.ppermute(near, "gx", [(i, i ^ 1) for i in range(n_gx)])
     far = lax.ppermute(far, "gx", [(i, (i - 1 + i % 2 * 2) % n_gx) for i in range(n_gx)])
+    near = [lax.ppermute(a, "gx", [(i, i ^ 1) for i in range(n_gx)]) for a in near]
     sections = 2 * STEPS
     edges, turned = pl.pallas_call(
         inner_kernel,
@@ -507,7 +512,7 @@
         scratch_shapes=[pltpu.VMEM((3 * half * members, cells_y), jnp.float32)],
         compiler_params=params,
         name="inner",
-    )(*own, near, fy)
+    )(*own, fy, *near)
     height = 3 * shares + half + 1
     sent = pl.pallas_call(
         functools.partial(outer_kernel, n_gx),

time: 42.4 us -> 41.3 us (0.974)
  blocking collectives: 29.6 us -> 26.8 us
  starting transfers between devices: 2.74 us -> 5.54 us
  waiting for transfers between devices: 2.23 us -> 1.31 us
    ppermute x1 -> x2, starting transfers between devices: 0.12 us -> 2.87 us  [on_device(): lax.ppermute(a, 'gx', [(i, i ^ 1) for i in range(n_gx)])]
    all_to_all x2, blocking collectives: 29.6 us -> 26.8 us  [exchange(): lax.all_to_all(block, ('mem', 'gx'), split_axis=0, concat_axis=0, tiled=T...]
    ppermute x1, waiting for transfers between devices: 2.23 us -> 0.01 us  [on_device(): lax.ppermute(far, 'gx', [(i, (i - 1 + i % 2 * 2) % n_gx) for i in range(n...]
    ppermute x1 -> x2, waiting for transfers between devices: 0.01 us -> 1.3 us  [on_device(): lax.ppermute(a, 'gx', [(i, i ^ 1) for i in range(n_gx)])]
  transfers between devices with their start and end apart: 2 -> 3, of which waited for: 1 -> 2; matrix products, arithmetic and copies ran while one was open for 0% -> 0% of each run, Pallas kernels for 6% -> 7%
where the time goes in v3:
time: 41.3 us; the launch traced here: 41.1 us
  blocking collectives  26.8 us (65%)
  Pallas kernels  7.33 us (18%)
  starting transfers between devices  5.54 us (13%)
  waiting for transfers between devices  1.31 us (3%)
    all_to_all x2, blocking collectives, exchange(): lax.all_to_all(block, ('mem', 'gx'), split_axis=0, concat_axis=0, tiled=T...  26.8 us
    ppermute x2, starting transfers between devices, on_device(): lax.ppermute(a, 'gx', [(i, i ^ 1) for i in range(n_gx)])  2.87 us
    pallas_call x1, Pallas kernels, on_device(): pl.pallas_call(inner_kernel, out_shape=[shape((sections - 1) * 2 * 3 * me...  2.81 us
    ppermute x1, starting transfers between devices, on_device(): lax.ppermute(far, 'gx', [(i, (i - 1 + i % 2 * 2) % n_gx) for i in range(n...  2.67 us
    ppermute x2, waiting for transfers between devices, on_device(): lax.ppermute(a, 'gx', [(i, i ^ 1) for i in range(n_gx)])  1.3 us
    pallas_call x1, Pallas kernels, on_device(): pl.pallas_call(functools.partial(outer_kernel, n_gx), out_shape=shape(dev...  1.29 us
    pallas_call x1, Pallas kernels, on_device(): pl.pallas_call(start_kernel, out_shape=[shape(tiles, n, LANES) for n in l...  1.19 us
    pallas_call x1, Pallas kernels, on_device(): pl.pallas_call(functools.partial(project_kernel, n_gx, rows, shares, rm),...  1.03 us
  transfers between devices with their start and end apart: 3, of which 2 were waited for; matrix products, arithmetic and copies ran while one was open for 0% of the time, Pallas kernels for 7%

profile of v3, /device:TPU:1, one launch (start us, length us, event | category | flops | bytes accessed | tf_op | source)
XLA Modules:
  0.0 41.1 jit_solution(3496850531746956506)
XLA Ops:
  0.0 1.2 %start.1 = (f32[2,128,128]{2,1,0:T(8,128)S(1)}, f32[2,256,128]{2,1,0:T(8,128)S(1)}, f32[2,16,128]{2,1,0:T(8,128)S(1)}, f32[256,128]{1,0:T(8,128)S(1)}, f32[2,200...) custom-call(f32[128,256]{1,0:T(8,128)} %bitcast.13, f32[256,256]{1,0:T(8,128)} %bitcast.12, ...), custom_call_target="tpu_custom_call" | custom-call | tf_op jit(solution)/shard_map/start/pallas_call | solution.py:493
  1.2 2.7 %collective-permute-start = (f32[2,200,128]{2,1,0:T(8,128)S(1)}, f32[2,200,128]{2,1,0:T(8,128)S(1)}, u32[]{:S(2)}, u32[]{:S(2)}) collective-permute-start(f32[2,200,128]{2,1,0:T(8,128)S(1)} %get-tuple-element.17), channel_id=1, source_target_pairs={{0,15},{1,2},{2,1},{3,4},{4,3},{5,6},{6,5},{7,8},{8,7},{9,10},{10,... | collective-permute-start | bytes 614408 | tf_op jit(solution)/shard_map/ppermute | solution.py:503
  3.9 2.9 %collective-permute-start.1 = (f32[200,128]{1,0:T(8,128)S(1)}, f32[200,128]{1,0:T(8,128)S(1)}, u32[]{:S(2)}, u32[]{:S(2)}) collective-permute-start(f32[200,128]{1,0:T(8,128)S(1)} %get-tuple-element.19), channel_id=1, source_target_pairs={{0,1},{1,0},{2,3},{3,2},{4,5},{5,4},{6,7},{7,6},{8,9},{9,8},{10,11... | collective-permute-start | bytes 307208 | tf_op jit(solution)/shard_map/ppermute | solution.py:504
  6.7 0.0 collective-permute-start.2
  6.7 0.9 %collective-permute-done.1.rest_0_ = f32[200,128]{1,0:T(8,128)S(1)} collective-permute-done((f32[200,128]{1,0:T(8,128)S(1)}, f32[200,128]{1,0:T(8,128)S(1)}, u32[]{:S(2)}, u32[]{:S(2)}) %collective-permute-start.1) | collective-permute-done | bytes 102432 | tf_op jit(solution)/shard_map/ppermute | solution.py:504
  7.7 0.4 collective-permute-done.2.rest_1_
  8.0 0.0 copy-start
  8.1 0.0 copy-start.1
  8.1 2.8 %inner.1 = (f32[288,256]{1,0:T(8,128)S(1)}, f32[3,128,128]{2,1,0:T(8,128)S(1)}) custom-call(f32[2,128,128]{2,1,0:T(8,128)S(1)} %get-tuple-element.14.own_d, f32[2,256,128]{2,1,0:T(8,128)S(1)} %get-tuple-element.15.own_m, f32[2,16,128]{2,1,0:T(8,128)S(1)} %get-tuple-element.16.own_w, f32[256,128]{1,0:T(8,128)S(1)} %get-tuple-element.18.fy, ...), custom_call_target="tpu_custom_call" | custom-call | tf_op jit(solution)/shard_map/inner/pallas_call | solution.py:506
  10.9 0.0 collective-permute-done.far
  10.9 0.0 copy-done
  10.9 0.0 copy-done.1
  10.9 1.3 %outer.1 = f32[544,128]{1,0:T(8,128)S(1)} custom-call(f32[2,128,128]{2,1,0:T(8,128)S(1)} %get-tuple-element.14.own_d, f32[2,256,128]{2,1,0:T(8,128)S(1)} %get-tuple-element.15.own_m, f32[2,16,128]{2,1,0:T(8,128)S(1)} %get-tuple-element.16.own_w, f32[2,200,128]{2,1,0:T(8,128)S(1)} %collective-permute-done.far, f32[256,128]{1,0:T(8,128)S(1)} %get-tuple-element.18.fy, ...), custom_call_target="tpu_custom_call" | custom-call | tf_op jit(solution)/shard_map/outer/pallas_call | solution.py:517
  12.2 15.2 %all_to_all.10 = f32[32,17,1,128]{3,2,1,0:T(1,128)S(1)} all-to-all(f32[32,17,1,128]{3,2,1,0:T(1,128)S(1)} %bitcast.8), channel_id=1, replica_groups=mesh['mem'=2,'gx'=16] {'mem','gx'}, dimensions={0} | all-to-all | bytes 557056 | tf_op jit(solution)/shard_map/all_to_all | solution.py:451
  27.4 1.0 %project.1 = f32[384,128]{1,0:T(8,128)S(1)} custom-call(f32[544,128]{1,0:T(8,128)S(1)} %bitcast.9), custom_call_target="tpu_custom_call" | custom-call | tf_op jit(solution)/shard_map/project/pallas_call | solution.py:527
  28.4 11.7 %all_to_all.11 = f32[32,12,1,128]{3,2,1,0:T(1,128)S(1)} all-to-all(f32[32,12,1,128]{3,2,1,0:T(1,128)S(1)} %bitcast.11), channel_id=1, replica_groups=mesh['mem'=2,'gx'=16] {'mem','gx'}, dimensions={0} | all-to-all | bytes 393216 | tf_op jit(solution)/shard_map/all_to_all | solution.py:451
  40.1 1.0 %gather.1 = f32[384,128]{1,0:T(8,128)} custom-call(f32[384,128]{1,0:T(8,128)S(1)} %bitcast.10), custom_call_target="tpu_custom_call" | custom-call | tf_op jit(solution)/shard_map/gather/pallas_call | solution.py:538
Async XLA Ops:
  1.2 9.7 %collective-permute-start = (f32[2,200,128]{2,1,0:T(8,128)S(1)}, f32[2,200,128]{2,1,0:T(8,128)S(1)}, u32[]{:S(2)}, u32[]{:S(2)}) collective-permute-start(f32[2,200,128]{2,1,0:T(8,128)S(1)} %get-tuple-element.17), channel_id=1, source_target_pairs={{0,15},{1,2},{2,1},{3,4},{4,3},{5,6},{6,5},{7,8},{8,7},{9,10},{10,... | collective-permute-start | bytes 614408 | tf_op jit(solution)/shard_map/ppermute | solution.py:503
  3.9 3.8 %collective-permute-start.1 = (f32[200,128]{1,0:T(8,128)S(1)}, f32[200,128]{1,0:T(8,128)S(1)}, u32[]{:S(2)}, u32[]{:S(2)}) collective-permute-start(f32[200,128]{1,0:T(8,128)S(1)} %get-tuple-element.19), channel_id=1, source_target_pairs={{0,1},{1,0},{2,3},{3,2},{4,5},{5,4},{6,7},{7,6},{8,9},{9,8},{10,11... | collective-permute-start | bytes 307208 | tf_op jit(solution)/shard_map/ppermute | solution.py:504
  6.7 1.3 %collective-permute-start.2 = (f32[200,128]{1,0:T(8,128)S(1)}, f32[200,128]{1,0:T(8,128)S(1)}, u32[]{:S(2)}, u32[]{:S(2)}) collective-permute-start(f32[200,128]{1,0:T(8,128)S(1)} %get-tuple-element.20), channel_id=1, source_target_pairs={{0,1},{1,0},{2,3},{3,2},{4,5},{5,4},{6,7},{7,6},{8,9},{9,8},{10,11... | collective-permute-start | bytes 307208 | tf_op jit(solution)/shard_map/ppermute | solution.py:504
  8.0 2.8 %copy-start = (f32[16,32]{1,0:T(8,128)S(1)}, f32[16,32]{1,0:T(8,128)}, u32[]{:S(2)}) copy-start(f32[16,32]{1,0:T(8,128)} %fm.1) | copy-start | bytes 6148
  8.1 2.8 %copy-start.1 = (f32[8,128]{1,0:T(8,128)S(1)}, f32[8,128]{1,0:T(8,128)}, u32[]{:S(2)}) copy-start(f32[8,128]{1,0:T(8,128)} %fx.1) | copy-start | bytes 12292

commit v4 on v3

--- a/solution.py
+++ b/solution.py
@@ -136,7 +136,9 @@
     cross = y_difference(row)
     rho, mx, my = row["q"]
     half = 0.5 * DTIME
-    spread = tuple(h - l + d for h, l, d in zip(high_face, low_face, cross))
+    spread = tuple(h + d for h, d in zip(high_face, cross))
+    if low_face is not None:
+        spread = tuple(a - l for a, l in zip(spread, low_face))
     keep = 1.0 - DTIME / RELAX
     wished = (DTIME / RELAX) * rho
     return (
@@ -226,28 +228,44 @@
         line[0] = self.sign * line[0]
         return tuple(jnp.broadcast_to(a, (SUBLANES, a.shape[1])) for a in line)
 
-
-def march(count, computed, fetch, wish, emit):
+    def keep(self, state, x, q):
+        for c, a in enumerate((q[0], self.sign * q[1], q[2])):
+            at = (3 * x + c) * self.members + self.group * SUBLANES
+            state[pl.ds(at, SUBLANES), :] = a
+
+
+def march(computed, fetch, wish, emit, hook=None, bound=None):
     sections = len(computed) - 1
     known, terms, faces = {}, {}, {}
 
     def value(s, x):
         if (s, x) not in known:
+            if x not in computed[s]:
+                new = fetch(s, x)
+            elif bound is not None and x == computed[s][-1]:
+                share = 0.5 * DTIME * (0.5 if s % 2 == 0 else 1.0)
+                new = tuple(
+                    a + share * b for a, b in zip(bound(s - 1, x)["next"], face(s - 1, x - 1))
+                )
+            else:
+                new = advanced(s, x, face(s - 1, x - 1))
             if x in computed[s]:
-                new = section(
-                    cell(s - 1, x), face(s - 1, x - 1), face(s - 1, x), wish(x)
-                )
-                if s % 2 == 0:
-                    new = tuple(0.5 * a + 0.5 * b for a, b in zip(value(s - 2, x), new))
                 emit(s, x, new)
-            else:
-                new = fetch(s, x)
             known[s, x] = new
         return known[s, x]
 
+    def advanced(s, x, low):
+        new = section(cell(s - 1, x), low, face(s - 1, x), wish(x))
+        if s % 2 == 0:
+            new = tuple(0.5 * a + 0.5 * b for a, b in zip(value(s - 2, x), new))
+        return new
+
     def cell(s, x):
         if (s, x) not in terms:
-            terms[s, x] = cell_terms(value(s, x))
+            if bound is not None and x == computed[s + 1][-1]:
+                terms[s, x] = bound(s, x)
+            else:
+                terms[s, x] = cell_terms(value(s, x))
         return terms[s, x]
 
     def face(s, x):
@@ -255,25 +273,44 @@
             faces[s, x] = x_face(cell(s, x), cell(s, x + 1))
         return faces[s, x]
 
-    for t in range(count):
+    for t in range(computed[1][0], computed[-1][-1] + sections + 1):
         for s in range(1, sections + 1):
             if t - s in computed[s]:
                 value(s, t - s)
-
-
-def edge_line(s, x, half, members):
-    return ((s - 1) * 2 + x - half - s) * 3 * members
-
-
-def turn_projected(state, fy, members, c, count):
-    lines = count * members
-    block = state[pl.ds(c * lines, lines), :]
-    along = jnp.dot(block, fy[...], precision=HIGH, preferred_element_type=jnp.float32)
-    return along.T
+        if hook is not None:
+            for s in range(sections):
+                hook(s, t - s - 1, cell, advanced)
+
+
+def edge_line(s, members):
+    return s * 9 * members
+
+
+def deal_columns(state, fy, devices, members, lines):
+    along = jnp.dot(state[...], fy[...], precision=HIGH, preferred_element_type=jnp.float32)
+    turned = along.T
+    shares = fy.shape[1] // devices
+    firsts, thirds = [], []
+    for x in range(lines):
+        at = 3 * x * members
+        cut = lambda low, high: jnp.concatenate(
+            [
+                turned[r * devices : (r + 1) * devices, at + low : at + high]
+                for r in range(shares)
+            ],
+            axis=1,
+        )
+        firsts.append(cut(0, 2 * members))
+        thirds.append(cut(2 * members, 3 * members))
+    return firsts, thirds
+
+
+def member_kernel(near, fm, out):
+    out[...] = jnp.concatenate([fm[...]] * (LANES // fm.shape[1]), axis=1)
 
 
 def inner_kernel(own_d, own_m, own_w, fy, *rest):
-    *near, edges, turned, state = rest
+    *near, edges, early, state = rest
     rows = own_w.shape[1] // 2
     half = rows // 2
     members = own_d.shape[1] // rows
@@ -284,23 +321,27 @@
 
         def emit(s, x, q):
             if s == sections:
-                for c in range(3):
-                    at = (c * half + x - rows) * members + group * SUBLANES
-                    state[pl.ds(at, SUBLANES), :] = q[c]
-            elif x - half - s in (0, 1):
-                for c in range(3):
-                    at = edge_line(s, x, half, members) + c * members + group * SUBLANES
-                    edges[pl.ds(at, SUBLANES), :] = q[c]
+                strip.keep(state, x - rows, q)
+
+        def hook(s, x, cell, advanced):
+            if x == half + s:
+                row = cell(s, x)
+                arrays = (*row["q"], *row["f"][1:], row["ax"], *advanced(s + 1, x, None))
+                for c, a in enumerate(arrays):
+                    at = edge_line(s, members) + c * members + group * SUBLANES
+                    edges[pl.ds(at, SUBLANES), :] = a
 
         computed = [range(0)] + [range(half + s, count - s) for s in range(1, sections + 1)]
-        march(count, computed, lambda s, x: strip.load(x), strip.wish, emit)
-    for c in range(3):
-        part = turn_projected(state, fy, members, c, half)
-        turned[c] = jnp.concatenate([jnp.zeros_like(part), part], axis=1)
+        march(computed, lambda s, x: strip.load(x), strip.wish, emit, hook)
+    devices = early.shape[0] // (2 * half)
+    firsts, thirds = deal_columns(state, fy, devices, members, half)
+    for i in range(half):
+        early[pl.ds(i * devices, devices), :] = firsts[i]
+        early[pl.ds((half + i) * devices, devices), :] = jnp.concatenate([thirds[i]] * 2, axis=1)
 
 
 def outer_kernel(
-    n_gx, own_d, own_m, own_w, far, fy, edges, turned, fx, fm, out, state
+    n_gx, own_d, own_m, own_w, far, fy, edges, early, fx, other_fm, out, state
 ):
     rows = own_w.shape[1] // 2
     half = rows // 2
@@ -309,94 +350,109 @@
     for group in range(members // SUBLANES):
         strip = Strip(group, (own_d, own_m, own_w), None, far)
 
+        @functools.cache
+        def bound(s, x):
+            at = edge_line(s, members) + group * SUBLANES
+            a = [edges[pl.ds(at + c * members, SUBLANES), :] for c in range(9)]
+            return dict(q=tuple(a[:3]), f=(a[1], a[3], a[4]), ax=a[5], next=tuple(a[6:]))
+
         def fetch(s, x):
-            if s == 0:
-                return strip.load(x)
-            at = edge_line(s, x, half, members) + group * SUBLANES
-            return tuple(edges[pl.ds(at + c * members, SUBLANES), :] for c in range(3))
+            return strip.load(x) if s == 0 else bound(s, x)["q"]
 
         def emit(s, x, q):
             if s == sections:
-                for c in range(3):
-                    at = (c * half + x - half) * members + group * SUBLANES
-                    state[pl.ds(at, SUBLANES), :] = q[c]
+                strip.keep(state, x - half, q)
 
         computed = [range(0)] + [range(s, half + s) for s in range(1, sections + 1)]
-        march(rows + sections, computed, fetch, strip.wish, emit)
+        march(computed, fetch, strip.wish, emit, bound=bound)
     devices = 2 * n_gx
-    shares = fy.shape[1] // devices
     height = out.shape[0] // devices
-    odd = lax.rem(lax.axis_index("gx"), 2)
-    sign = (1 - 2 * odd).astype(jnp.float32)
-    for c in range(3):
-        part = turn_projected(state, fy, members, c, half)
-        whole = jnp.concatenate([part, turned[c][:, half * members :]], axis=1)
-        if c == 1:
-            whole = sign * whole
-        for r in range(shares):
-            out[pl.ds(c * shares + r, devices, stride=height), :] = whole[
-                r * devices : (r + 1) * devices
-            ]
-    mem, gx = lax.axis_index("mem"), lax.axis_index("gx")
+    firsts, thirds = deal_columns(state, fy, devices, members, half)
+    middle = LANES // 2
+    for i in range(half):
+        out[pl.ds(i, devices, stride=height), :] = firsts[i]
+        out[pl.ds(half + i, devices, stride=height), :] = early[pl.ds(i * devices, devices), :]
+        other = early[pl.ds((half + i) * devices, devices), :]
+        out[pl.ds(rows + i, devices, stride=height), :] = jnp.concatenate(
+            [thirds[i], other[:, middle:]], axis=1
+        )
+    mem = lax.axis_index("mem")
     for r in range(half):
         line = fx[pl.ds(mem * half + r, 1), :]
-        out[pl.ds(3 * shares + r, devices, stride=height), :] = jnp.broadcast_to(
+        out[pl.ds(rows + half + r, devices, stride=height), :] = jnp.broadcast_to(
             line, (devices, line.shape[1])
         )
-    line = fm[pl.ds(gx, 1), :]
-    line = jnp.concatenate([line] * (LANES // line.shape[1]), axis=1)
-    out[pl.ds(3 * shares + half, devices, stride=height), :] = jnp.broadcast_to(
-        line, (devices, LANES)
-    )
-
-
-def project_kernel(n_gx, rows, shares, rm, inp, out, blocks, tall):
+
+
+def project_kernel(n_gx, rows, rm, inp, own_fm, other_fm, out, tall):
     devices = 2 * n_gx
     members = n_gx
     height = inp.shape[0] // devices
     half = rows // 2
-    pieces = 3 * shares
-    columns = [inp[pl.ds(j, devices, stride=height), :] for j in range(pieces)]
-    lhs = jnp.concatenate(
+    middle = LANES // 2
+    low_rank = rm // 2
+    line = lambda j: inp[pl.ds(j, devices, stride=height), :]
+    swap = lambda a: pltpu.roll(a, middle, 1)
+    lane = lax.broadcasted_iota(jnp.int32, (members, LANES), 1)
+    firsts = [line(x) for x in range(rows)]
+    firsts = jnp.concatenate(
         [
-            jnp.concatenate([d[:n_gx] for d in columns], axis=0),
-            jnp.concatenate([d[n_gx:] for d in columns], axis=0),
+            jnp.concatenate([a[mem * n_gx : (mem + 1) * n_gx] for a in firsts], axis=0)
+            for mem in range(2)
         ],
         axis=1,
     )
-    fm = inp[pl.ds(pieces + half, devices, stride=height), :]
-    group = lax.broadcasted_iota(jnp.int32, (members, LANES), 1) // rm
-    per = LANES // rm
-    zero = jnp.zeros((members, LANES), jnp.float32)
-    lines = []
-    for mem in range(2):
-        part = fm[mem * members : (mem + 1) * members]
-        for x in range(rows):
-            kept = jnp.where(group == x % per, part, 0.0)
-            lines.append(
-                jnp.concatenate(
-                    [kept if x // per == t else zero for t in range(rows // per)], axis=1
-                )
+    thirds = [line(rows + i) for i in range(half)]
+    pairs = [(a[:n_gx], a[n_gx:]) for a in thirds]
+    thirds = jnp.concatenate(
+        [jnp.where(lane < middle, a, swap(b)) for a, b in pairs]
+        + [jnp.where(lane < middle, swap(a), b) for a, b in pairs],
+        axis=0,
+    )
+    first = lax.axis_index("mem") == 0
+    a, b = own_fm[...], other_fm[...]
+    fm = jnp.concatenate([jnp.where(first, a, b), jnp.where(first, b, a)], axis=0)
+    wide = lax.broadcasted_iota(jnp.int32, fm.shape, 1)
+    first_half = wide % rm < low_rank
+    repeated = (
+        jnp.where(first_half, fm, pltpu.roll(fm, low_rank, 1)),
+        jnp.where(first_half, pltpu.roll(fm, LANES - low_rank, 1), fm),
+    )
+    block = lane // low_rank
+    part = lambda k, mem: repeated[k][mem * members : (mem + 1) * members]
+    count = LANES // members
+    diagonal = jnp.concatenate(
+        [
+            jnp.concatenate(
+                [jnp.where(block == p, part(k, mem), 0.0) for mem in range(2) for p in range(count)],
+                axis=0,
             )
-    diagonal = jnp.concatenate(lines, axis=0)
-    mixed = jnp.dot(lhs, diagonal, precision=HIGH, preferred_element_type=jnp.float32)
-    lows = rm // 2
-    orders = (range(pieces), [j % pieces for j in range(pieces - shares, 2 * pieces - shares)])
-    for x in range(rows):
-        for k in range(2):
-            blocks[pl.ds(x * n_gx, n_gx), pl.ds(k * pieces * lows, pieces * lows)] = jnp.concatenate(
-                [
-                    mixed[j * n_gx : (j + 1) * n_gx, x * rm + k * lows : x * rm + (k + 1) * lows]
-                    for j in orders[k]
-                ],
-                axis=1,
+            for k in range(2)
+        ],
+        axis=1,
+    )
+    small = jnp.concatenate(
+        [
+            jnp.where(
+                block == p,
+                part(0, mem),
+                jnp.where(block == count // 2 + p, part(1, mem), 0.0),
             )
-    halves = [inp[pl.ds(pieces + r, devices, stride=height), :] for r in range(half)]
+            for mem in range(2)
+            for p in range(count // 2)
+        ],
+        axis=0,
+    )
+    product = functools.partial(jnp.dot, precision=HIGH, preferred_element_type=jnp.float32)
+    firsts = product(firsts, diagonal)
+    thirds = product(thirds, small)
+    blocks = jnp.concatenate([firsts[:, :LANES], thirds, firsts[:, LANES:]], axis=1)
+    halves = [line(rows + half + r) for r in range(half)]
     lines = [a[:n_gx] for a in halves] + [a[n_gx:] for a in halves]
     odd = lax.broadcasted_iota(jnp.int32, (n_gx, LANES), 0) % 2 == 1
     lines = [jnp.where(odd, lines[rows - 1 - r], lines[r]) for r in range(rows)]
     fx = jnp.concatenate(lines, axis=0)
-    core = jnp.dot(fx.T, blocks[...], precision=HIGH, preferred_element_type=jnp.float32)
+    core = product(fx.T, blocks)
     high = out.shape[0] // devices
     for t in range(3):
         tall[t] = core[:, t * LANES : (t + 1) * LANES]
@@ -426,11 +482,11 @@
             [inp[pl.ds(first + i, devices, stride=high), :] for i in range(quarter)], axis=0
         ).T
 
-    def place(turned, base, c, a0):
+    def place(turned, base, apart, c, a0):
         for i in range(quarter):
             line = jnp.concatenate(
                 [
-                    turned[base + r * lows : base + (r + 1) * lows, i * devices : (i + 1) * devices]
+                    turned[base + r * apart : base + r * apart + lows, i * devices : (i + 1) * devices]
                     for r in range(shares)
                 ],
                 axis=1,
@@ -440,10 +496,10 @@
     for h in range(2):
         turned = turn(h * quarter)
         for c in range(2):
-            place(turned, c * shares * lows, c, h * quarter)
+            place(turned, c * lows, 2 * lows, c, h * quarter)
     turned = turn(SUBLANES)
     for h in range(2):
-        place(turned, h * shares * lows, 2, h * quarter)
+        place(turned, h * shares * lows, lows, 2, h * quarter)
 
 
 def exchange(chunks, devices):
@@ -469,7 +525,8 @@
         and ry == LANES == shares * n_mem * n_gx
         and shares * rm == LANES
         and shares * rm // 2 * 2 == LANES
-        and rows * rm == 2 * LANES
+        and 2 * shares * members == LANES
+        and 2 * members == rm
     )
 
 
@@ -502,38 +559,46 @@
     )(*[pltpu.with_memory_space_constraint(a, pltpu.HBM) for a in (*own, factor_y)])
     far = lax.ppermute(far, "gx", [(i, (i - 1 + i % 2 * 2) % n_gx) for i in range(n_gx)])
     near = [lax.ppermute(a, "gx", [(i, i ^ 1) for i in range(n_gx)]) for a in near]
+    own_fm = pl.pallas_call(
+        member_kernel,
+        out_shape=shape(members, LANES),
+        in_specs=[anywhere, vmem],
+        out_specs=vmem,
+        compiler_params=params,
+        name="member",
+    )(near[-1], factor_m)
+    other_fm = lax.ppermute(own_fm, "mem", [(0, 1), (1, 0)])
     sections = 2 * STEPS
-    edges, turned = pl.pallas_call(
+    edges, early = pl.pallas_call(
         inner_kernel,
         out_shape=[
-            shape((sections - 1) * 2 * 3 * members, cells_y),
-            shape(3, ry, LANES),
+            shape(sections * 9 * members, cells_y),
+            shape(2 * half * devices, LANES),
         ],
         scratch_shapes=[pltpu.VMEM((3 * half * members, cells_y), jnp.float32)],
         compiler_params=params,
         name="inner",
     )(*own, fy, *near)
-    height = 3 * shares + half + 1
+    height = rows + 2 * half
     sent = pl.pallas_call(
         functools.partial(outer_kernel, n_gx),
         out_shape=shape(devices * height, LANES),
+        in_specs=[vmem] * 8 + [anywhere],
+        out_specs=vmem,
         scratch_shapes=[pltpu.VMEM((3 * half * members, cells_y), jnp.float32)],
         compiler_params=params,
         name="outer",
-    )(*own, far, fy, edges, turned, factor_x, factor_m)
+    )(*own, far, fy, edges, early, factor_x, other_fm)
     got = exchange(sent, devices)
     lows = rm // 2
     high = 3 * shares * lows * SUBLANES // LANES
     sent = pl.pallas_call(
-        functools.partial(project_kernel, n_gx, rows, shares, rm),
+        functools.partial(project_kernel, n_gx, rows, rm),
         out_shape=jax.ShapeDtypeStruct((devices * high, LANES), jnp.float32),
-        scratch_shapes=[
-            pltpu.VMEM((rows * n_gx, 3 * shares * rm), jnp.float32),
-            pltpu.VMEM((3, rx, LANES), jnp.float32),
-        ],
+        scratch_shapes=[pltpu.VMEM((3, rx, LANES), jnp.float32)],
         compiler_params=params,
         name="project",
-    )(got)
+    )(got, own_fm, other_fm)
     got = exchange(sent, devices)
     core = pl.pallas_call(
         functools.partial(gather_kernel, shares, lows),

time: 41.3 us -> 40.5 us (0.981)
  blocking collectives: 26.8 us -> 24.8 us
  starting transfers between devices: 5.54 us -> 6.79 us
  Pallas kernels: 7.33 us -> 7.76 us
    all_to_all x2, blocking collectives: 26.8 us -> 24.8 us  [exchange(): lax.all_to_all(block, ('mem', 'gx'), split_axis=0, concat_axis=0, tiled=T...]
    ppermute x0 -> x1, starting transfers between devices: none -> 1.24 us  [on_device(): other_fm = lax.ppermute(own_fm, 'mem', [(0, 1), (1, 0)])]
    pallas_call x2 -> x3, Pallas kernels: 3.85 us -> 4.32 us  [the longest x1 3.57 us: on_device(): pl.pallas_call(inner_kernel, out_shape=[shape(sections * 9 * members, cel...]
  transfers between devices with their start and end apart: 3 -> 4, of which waited for: 2 -> 1; matrix products, arithmetic and copies ran while one was open for 0% -> 0% of each run, Pallas kernels for 7% -> 9%
where the time goes in v4:
time: 40.5 us; the launch traced here: 40.4 us
  blocking collectives  24.8 us (61%)
  Pallas kernels  7.76 us (19%)
  starting transfers between devices  6.79 us (17%)
  waiting for transfers between devices  0.95 us (2%)
    all_to_all x2, blocking collectives, exchange(): lax.all_to_all(block, ('mem', 'gx'), split_axis=0, concat_axis=0, tiled=T...  24.8 us
    pallas_call x1, Pallas kernels, on_device(): pl.pallas_call(inner_kernel, out_shape=[shape(sections * 9 * members, cel...  3.57 us
    ppermute x2, starting transfers between devices, on_device(): lax.ppermute(a, 'gx', [(i, i ^ 1) for i in range(n_gx)])  2.87 us
    ppermute x1, starting transfers between devices, on_device(): lax.ppermute(far, 'gx', [(i, (i - 1 + i % 2 * 2) % n_gx) for i in range(n...  2.67 us
    ppermute x1, starting transfers between devices, on_device(): other_fm = lax.ppermute(own_fm, 'mem', [(0, 1), (1, 0)])  1.24 us
    pallas_call x1, Pallas kernels, on_device(): pl.pallas_call(functools.partial(outer_kernel, n_gx), out_shape=shape(dev...  1.23 us
    pallas_call x1, Pallas kernels, on_device(): pl.pallas_call(start_kernel, out_shape=[shape(tiles, n, LANES) for n in l...  1.2 us
    pallas_call x1, Pallas kernels, on_device(): pl.pallas_call(functools.partial(gather_kernel, shares, lows), out_shape=...  1.01 us
  transfers between devices with their start and end apart: 4, of which 1 were waited for; matrix products, arithmetic and copies ran while one was open for 0% of the time, Pallas kernels for 9%

profile of v4, /device:TPU:1, one launch (start us, length us, event | category | flops | bytes accessed | tf_op | source)
XLA Modules:
  0.0 40.4 jit_solution(7242082607674662273)
XLA Ops:
  0.0 0.0 copy-start
  0.0 1.2 %start.1 = (f32[2,128,128]{2,1,0:T(8,128)S(1)}, f32[2,256,128]{2,1,0:T(8,128)S(1)}, f32[2,16,128]{2,1,0:T(8,128)S(1)}, f32[256,128]{1,0:T(8,128)S(1)}, f32[2,200...) custom-call(f32[128,256]{1,0:T(8,128)} %bitcast.15, f32[256,256]{1,0:T(8,128)} %bitcast.14, ...), custom_call_target="tpu_custom_call" | custom-call | tf_op jit(solution)/shard_map/start/pallas_call | solution.py:550
  1.2 2.7 %collective-permute-start = (f32[2,200,128]{2,1,0:T(8,128)S(1)}, f32[2,200,128]{2,1,0:T(8,128)S(1)}, u32[]{:S(2)}, u32[]{:S(2)}) collective-permute-start(f32[2,200,128]{2,1,0:T(8,128)S(1)} %get-tuple-element.17), channel_id=1, source_target_pairs={{0,15},{1,2},{2,1},{3,4},{4,3},{5,6},{6,5},{7,8},{8,7},{9,10},{10,... | collective-permute-start | bytes 614408 | tf_op jit(solution)/shard_map/ppermute | solution.py:560
  3.9 2.9 %collective-permute-start.2 = (f32[200,128]{1,0:T(8,128)S(1)}, f32[200,128]{1,0:T(8,128)S(1)}, u32[]{:S(2)}, u32[]{:S(2)}) collective-permute-start(f32[200,128]{1,0:T(8,128)S(1)} %get-tuple-element.20), channel_id=1, source_target_pairs={{0,1},{1,0},{2,3},{3,2},{4,5},{5,4},{6,7},{7,6},{8,9},{9,8},{10,11... | collective-permute-start | bytes 307208 | tf_op jit(solution)/shard_map/ppermute | solution.py:561
  6.8 0.0 collective-permute-start.1
  6.8 0.9 %collective-permute-done.2.rest_1_.near = f32[200,128]{1,0:T(8,128)S(1)} collective-permute-done((f32[200,128]{1,0:T(8,128)S(1)}, f32[200,128]{1,0:T(8,128)S(1)}, u32[]{:S(2)}, u32[]{:S(2)}) %collective-permute-start.2) | collective-permute-done | bytes 102432 | tf_op jit(solution)/shard_map/ppermute | solution.py:561
  7.7 0.0 copy-done
  7.7 0.1 member.1.own_fm
  7.8 1.2 %collective-permute-start.3 = (f32[16,128]{1,0:T(8,128)S(1)}, f32[16,128]{1,0:T(8,128)S(1)}, u32[]{:S(2)}, u32[]{:S(2)}) collective-permute-start(f32[16,128]{1,0:T(8,128)S(1)} %member.1.own_fm), channel_id=1, source_target_pairs={{0,16},{16,0},{1,17},{17,1},{2,18},{18,2},{3,19},{19,3},{4,20},{20... | collective-permute-start | bytes 24584 | tf_op jit(solution)/shard_map/ppermute | solution.py:570
  9.0 0.0 collective-permute-done.1.rest_0_
  9.0 0.0 copy-start.1
  9.0 3.6 %inner.1 = (f32[576,256]{1,0:T(8,128)S(1)}, f32[256,128]{1,0:T(8,128)S(1)}) custom-call(f32[2,128,128]{2,1,0:T(8,128)S(1)} %get-tuple-element.14.own_d, f32[2,256,128]{2,1,0:T(8,128)S(1)} %get-tuple-element.15.own_m, f32[2,16,128]{2,1,0:T(8,128)S(1)} %get-tuple-element.16.own_w, f32[256,128]{1,0:T(8,128)S(1)} %get-tuple-element.18.fy, ...), custom_call_target="tpu_custom_call" | custom-call | tf_op jit(solution)/shard_map/inner/pallas_call | solution.py:572
  12.6 0.0 collective-permute-done.3.other_fm
  12.6 0.0 collective-permute-done.far
  12.6 0.0 copy-done.1
  12.6 1.2 %outer.1 = f32[512,128]{1,0:T(8,128)S(1)} custom-call(f32[2,128,128]{2,1,0:T(8,128)S(1)} %get-tuple-element.14.own_d, f32[2,256,128]{2,1,0:T(8,128)S(1)} %get-tuple-element.15.own_m, f32[2,16,128]{2,1,0:T(8,128)S(1)} %get-tuple-element.16.own_w, f32[2,200,128]{2,1,0:T(8,128)S(1)} %collective-permute-done.far, f32[256,128]{1,0:T(8,128)S(1)} %get-tuple-element.18.fy, ...), custom_call_target="tpu_custom_call" | custom-call | tf_op jit(solution)/shard_map/outer/pallas_call | solution.py:583
  13.9 13.2 %all_to_all.10 = f32[32,16,1,128]{3,1,2,0:T(8,128)S(1)} all-to-all(f32[32,16,1,128]{3,1,2,0:T(8,128)S(1)} %bitcast.11), channel_id=1, replica_groups=mesh['mem'=2,'gx'=16] {'mem','gx'}, dimensions={0} | all-to-all | bytes 524288 | tf_op jit(solution)/shard_map/all_to_all | solution.py:507
  27.1 0.7 %project.1 = f32[384,128]{1,0:T(8,128)S(1)} custom-call(f32[512,128]{1,0:T(8,128)S(1)} %bitcast.10, f32[16,128]{1,0:T(8,128)S(1)} %member.1.own_fm, f32[16,128]{1,0:T(8,128)S(1)} %collective-permute-done.3.other_fm), custom_call_target="tpu_custom_call" | custom-call | tf_op jit(solution)/shard_map/project/pallas_call | solution.py:595
  27.8 11.6 %all_to_all.11 = f32[32,12,1,128]{3,2,1,0:T(1,128)S(1)} all-to-all(f32[32,12,1,128]{3,2,1,0:T(1,128)S(1)} %bitcast.13), channel_id=1, replica_groups=mesh['mem'=2,'gx'=16] {'mem','gx'}, dimensions={0} | all-to-all | bytes 393216 | tf_op jit(solution)/shard_map/all_to_all | solution.py:507
  39.3 1.0 %gather.1 = f32[384,128]{1,0:T(8,128)} custom-call(f32[384,128]{1,0:T(8,128)S(1)} %bitcast.12), custom_call_target="tpu_custom_call" | custom-call | tf_op jit(solution)/shard_map/gather/pallas_call | solution.py:603
Async XLA Ops:
  0.0 7.7 %copy-start = (f32[16,32]{1,0:T(8,128)S(1)}, f32[16,32]{1,0:T(8,128)}, u32[]{:S(2)}) copy-start(f32[16,32]{1,0:T(8,128)} %fm.1) | copy-start | bytes 6148
  1.2 11.4 %collective-permute-start = (f32[2,200,128]{2,1,0:T(8,128)S(1)}, f32[2,200,128]{2,1,0:T(8,128)S(1)}, u32[]{:S(2)}, u32[]{:S(2)}) collective-permute-start(f32[2,200,128]{2,1,0:T(8,128)S(1)} %get-tuple-element.17), channel_id=1, source_target_pairs={{0,15},{1,2},{2,1},{3,4},{4,3},{5,6},{6,5},{7,8},{8,7},{9,10},{10,... | collective-permute-start | bytes 614408 | tf_op jit(solution)/shard_map/ppermute | solution.py:560
  3.9 3.8 %collective-permute-start.2 = (f32[200,128]{1,0:T(8,128)S(1)}, f32[200,128]{1,0:T(8,128)S(1)}, u32[]{:S(2)}, u32[]{:S(2)}) collective-permute-start(f32[200,128]{1,0:T(8,128)S(1)} %get-tuple-element.20), channel_id=1, source_target_pairs={{0,1},{1,0},{2,3},{3,2},{4,5},{5,4},{6,7},{7,6},{8,9},{9,8},{10,11... | collective-permute-start | bytes 307208 | tf_op jit(solution)/shard_map/ppermute | solution.py:561
  6.8 2.3 %collective-permute-start.1 = (f32[200,128]{1,0:T(8,128)S(1)}, f32[200,128]{1,0:T(8,128)S(1)}, u32[]{:S(2)}, u32[]{:S(2)}) collective-permute-start(f32[200,128]{1,0:T(8,128)S(1)} %get-tuple-element.19), channel_id=1, source_target_pairs={{0,1},{1,0},{2,3},{3,2},{4,5},{5,4},{6,7},{7,6},{8,9},{9,8},{10,11... | collective-permute-start | bytes 307208 | tf_op jit(solution)/shard_map/ppermute | solution.py:561
  7.8 4.8 %collective-permute-start.3 = (f32[16,128]{1,0:T(8,128)S(1)}, f32[16,128]{1,0:T(8,128)S(1)}, u32[]{:S(2)}, u32[]{:S(2)}) collective-permute-start(f32[16,128]{1,0:T(8,128)S(1)} %member.1.own_fm), channel_id=1, source_target_pairs={{0,16},{16,0},{1,17},{17,1},{2,18},{18,2},{3,19},{19,3},{4,20},{20... | collective-permute-start | bytes 24584 | tf_op jit(solution)/shard_map/ppermute | solution.py:570
  9.0 3.6 %copy-start.1 = (f32[8,128]{1,0:T(8,128)S(1)}, f32[8,128]{1,0:T(8,128)}, u32[]{:S(2)}) copy-start(f32[8,128]{1,0:T(8,128)} %fx.1) | copy-start | bytes 12292

commit v5 on v4

--- a/solution.py
+++ b/solution.py
@@ -140,42 +140,62 @@
     if low_face is not None:
         spread = tuple(a - l for a, l in zip(spread, low_face))
     keep = 1.0 - DTIME / RELAX
-    wished = (DTIME / RELAX) * rho
     return (
         rho - half * spread[0],
-        keep * mx + wished * wish[0] - half * spread[1],
-        keep * my + wished * wish[1] - half * spread[2],
-    )
-
-
-def start_kernel(d, m, w, fy, own_d, own_m, own_w, own_fy, far, near, sems):
+        keep * mx + rho * wish[0] - half * spread[1],
+        keep * my + rho * wish[1] - half * spread[2],
+    )
+
+
+def half_copies(arrays, targets, odd, upper, sems):
+    kinds = []
+    for low in range(2):
+        copies = []
+        for t, target in enumerate(targets):
+            base = 0
+            for whole in arrays:
+                lines, rows = whole.shape[:2]
+                source = whole.at[:, pl.ds(low * (rows // 2), rows // 2), pl.ds(t * LANES, LANES)]
+                copies.append((source, target.at[pl.ds(base, lines)]))
+                base += lines
+        kinds.append([
+            pltpu.make_async_copy(source, target, sems.at[i])
+            for i, (source, target) in enumerate(copies)
+        ])
+    for kind in range(2):
+
+        @pl.when(odd == kind)
+        def _():
+            for copy in kinds[kind if upper else 1 - kind]:
+                copy.start()
+
+    return kinds[0]
+
+
+def far_kernel(d, m, w, far, sems):
+    odd = lax.rem(lax.axis_index("gx"), 2)
+    targets = [far.at[t] for t in range(far.shape[0])]
+    for copy in half_copies((d, m, w), targets, odd, 1, sems):
+        copy.wait()
+
+
+def own_kernel(d, m, w, fy, fx, far, own_d, own_m, own_w, own_fy, own_fx, near, half_sems, sems):
     tiles = own_d.shape[0]
     odd = lax.rem(lax.axis_index("gx"), 2)
-    rows = own_w.shape[1] // 2
-    half = rows // 2
-    pairs = []
+    copies = half_copies((d, m, w), near, odd, 0, half_sems)
+    wholes = []
     for whole, cut in ((d, own_d), (m, own_m), (w, own_w)):
         for t in range(tiles):
-            pairs.append((whole.at[:, pl.ds(t * LANES, LANES)], cut.at[t]))
-    pairs.append((fy, own_fy))
-    copies = [
+            wholes.append((whole.at[:, :, pl.ds(t * LANES, LANES)], cut.at[t]))
+    wholes += [(fy, own_fy), (fx, own_fx)]
+    wholes = [
         pltpu.make_async_copy(source, target, sems.at[i])
-        for i, (source, target) in enumerate(pairs)
+        for i, (source, target) in enumerate(wholes)
     ]
-    for copy in copies:
+    for copy in wholes:
         copy.start()
-    base = 0
-    for n, cut in enumerate((own_d, own_m, own_w)):
-        lines = cut.shape[1] // rows
-        for t in range(tiles):
-            copies[n * tiles + t].wait()
-            for target, first in ((far.at[t], half * odd), (near[t], half * (1 - odd))):
-                for i in range(half):
-                    target[pl.ds(base + i, lines, stride=half), :] = cut[
-                        t, pl.ds(first + i, lines, stride=rows), :
-                    ]
-        base += lines * half
-    copies[-1].wait()
+    for copy in copies + wholes:
+        copy.wait()
 
 
 class Strip:
@@ -185,7 +205,7 @@
         self.members = own[0].shape[1] // self.rows
         self.tiles = own[0].shape[0]
         cut = lambda ref: [ref.at[t] for t in range(self.tiles)]
-        self.group, self.own = group, tuple(cut(a) for a in own)
+        self.first, self.own = pl.multiple_of(group * SUBLANES, SUBLANES), tuple(cut(a) for a in own)
         self.near = near
         self.far = None if far is None else cut(far)
         self.odd = lax.rem(lax.axis_index("gx"), 2)
@@ -212,7 +232,7 @@
         else:
             d = m = ref
             base = self.members * lines
-        first = self.group * SUBLANES
+        first = self.first
         rho = self.every(d, first * lines + at, SUBLANES, lines)
         mx = self.every(m, base + first * 2 * lines + at, SUBLANES, 2 * lines)
         my = self.every(m, base + (first * 2 + 1) * lines + at, SUBLANES, 2 * lines)
@@ -225,12 +245,13 @@
         else:
             base = 3 * self.members * lines
         line = [self.every(ref, base + c * lines + at, 1, 1) for c in range(2)]
-        line[0] = self.sign * line[0]
+        rate = DTIME / RELAX
+        line = [(rate * self.sign) * line[0], rate * line[1]]
         return tuple(jnp.broadcast_to(a, (SUBLANES, a.shape[1])) for a in line)
 
     def keep(self, state, x, q):
         for c, a in enumerate((q[0], self.sign * q[1], q[2])):
-            at = (3 * x + c) * self.members + self.group * SUBLANES
+            at = (3 * x + c) * self.members + self.first
             state[pl.ds(at, SUBLANES), :] = a
 
 
@@ -257,7 +278,7 @@
     def advanced(s, x, low):
         new = section(cell(s - 1, x), low, face(s - 1, x), wish(x))
         if s % 2 == 0:
-            new = tuple(0.5 * a + 0.5 * b for a, b in zip(value(s - 2, x), new))
+            new = tuple(0.5 * (a + b) for a, b in zip(value(s - 2, x), new))
         return new
 
     def cell(s, x):
@@ -286,10 +307,15 @@
     return s * 9 * members
 
 
-def deal_columns(state, fy, devices, members, lines):
-    along = jnp.dot(state[...], fy[...], precision=HIGH, preferred_element_type=jnp.float32)
-    turned = along.T
-    shares = fy.shape[1] // devices
+def deal_columns(state, turned_fy, devices, members, lines):
+    turned = lax.dot_general(
+        turned_fy,
+        state[...],
+        (((1,), (1,)), ((), ())),
+        precision=HIGH,
+        preferred_element_type=jnp.float32,
+    )
+    shares = turned_fy.shape[0] // devices
     firsts, thirds = [], []
     for x in range(lines):
         at = 3 * x * members
@@ -310,13 +336,15 @@
 
 
 def inner_kernel(own_d, own_m, own_w, fy, *rest):
-    *near, edges, early, state = rest
+    *near, edges, early, fy_out, state = rest
     rows = own_w.shape[1] // 2
     half = rows // 2
     members = own_d.shape[1] // rows
     sections = 2 * STEPS
     count = 2 * rows
-    for group in range(members // SUBLANES):
+
+    @pl.loop(0, members // SUBLANES)
+    def _(group):
         strip = Strip(group, (own_d, own_m, own_w), near, None)
 
         def emit(s, x, q):
@@ -328,13 +356,15 @@
                 row = cell(s, x)
                 arrays = (*row["q"], *row["f"][1:], row["ax"], *advanced(s + 1, x, None))
                 for c, a in enumerate(arrays):
-                    at = edge_line(s, members) + c * members + group * SUBLANES
+                    at = edge_line(s, members) + c * members + strip.first
                     edges[pl.ds(at, SUBLANES), :] = a
 
         computed = [range(0)] + [range(half + s, count - s) for s in range(1, sections + 1)]
         march(computed, lambda s, x: strip.load(x), strip.wish, emit, hook)
+
     devices = early.shape[0] // (2 * half)
-    firsts, thirds = deal_columns(state, fy, devices, members, half)
+    fy_out[...] = fy[...].T
+    firsts, thirds = deal_columns(state, fy_out[...], devices, members, half)
     for i in range(half):
         early[pl.ds(i * devices, devices), :] = firsts[i]
         early[pl.ds((half + i) * devices, devices), :] = jnp.concatenate([thirds[i]] * 2, axis=1)
@@ -352,12 +382,12 @@
 
         @functools.cache
         def bound(s, x):
-            at = edge_line(s, members) + group * SUBLANES
+            at = edge_line(s, members) + strip.first
             a = [edges[pl.ds(at + c * members, SUBLANES), :] for c in range(9)]
             return dict(q=tuple(a[:3]), f=(a[1], a[3], a[4]), ax=a[5], next=tuple(a[6:]))
 
         def fetch(s, x):
-            return strip.load(x) if s == 0 else bound(s, x)["q"]
+            return strip.load(x) if x < half else bound(s, x)["q"]
 
         def emit(s, x, q):
             if s == sections:
@@ -365,9 +395,10 @@
 
         computed = [range(0)] + [range(s, half + s) for s in range(1, sections + 1)]
         march(computed, fetch, strip.wish, emit, bound=bound)
+
     devices = 2 * n_gx
     height = out.shape[0] // devices
-    firsts, thirds = deal_columns(state, fy, devices, members, half)
+    firsts, thirds = deal_columns(state, fy[...], devices, members, half)
     middle = LANES // 2
     for i in range(half):
         out[pl.ds(i, devices, stride=height), :] = firsts[i]
@@ -471,11 +502,10 @@
         out[pl.ds(n_gx * high + SUBLANES + i, n_gx, stride=high), :] = second
 
 
-def gather_kernel(shares, lows, inp, out):
+def gather_kernel(shares, lows, inp, core, out, sems):
     devices = LANES // shares
     high = inp.shape[0] // devices
     quarter = SUBLANES // 2
-    step = out.shape[0] // lows
 
     def turn(first):
         return jnp.concatenate(
@@ -491,15 +521,23 @@
                 ],
                 axis=1,
             )
-            out[pl.ds(c * SUBLANES + a0 + i, lows, stride=step), :] = line
-
-    for h in range(2):
-        turned = turn(h * quarter)
-        for c in range(2):
-            place(turned, c * lows, 2 * lows, c, h * quarter)
+            out[c, pl.ds(a0 + i, lows, stride=SUBLANES), :] = line
+
+    def send(c):
+        source = out.at[c].reshape(lows, SUBLANES, LANES)
+        return pltpu.make_async_copy(source, core.at[:, c], sems.at[c])
+
+    turned = [turn(h * quarter) for h in range(2)]
+    for c in range(2):
+        for h in range(2):
+            place(turned[h], c * lows, 2 * lows, c, h * quarter)
+        send(c).start()
     turned = turn(SUBLANES)
     for h in range(2):
         place(turned, h * shares * lows, lows, 2, h * quarter)
+    send(2).start()
+    for c in range(3):
+        send(c).wait()
 
 
 def exchange(chunks, devices):
@@ -543,20 +581,36 @@
     anywhere = pl.BlockSpec(memory_space=pl.ANY)
     tiles = cells_y // LANES
     half = rows // 2
-    own = [a.reshape(-1, cells_y) for a in (density, momenta, desired)]
+    shape = lambda *dims: jax.ShapeDtypeStruct(dims, jnp.float32)
+    held = lambda *arrays: [pltpu.with_memory_space_constraint(a, pltpu.HBM) for a in arrays]
+    own = [a.reshape(-1, rows, cells_y) for a in (density, momenta, desired)]
     lines = [a.shape[0] for a in own]
-    shape = lambda *dims: jax.ShapeDtypeStruct(dims, jnp.float32)
-    packed = (sum(lines) // 2, LANES)
-    *own, fy, far, near = pl.pallas_call(
-        start_kernel,
-        out_shape=[shape(tiles, n, LANES) for n in lines]
-        + [shape(*factor_y.shape), shape(tiles, *packed), [shape(*packed)] * tiles],
-        in_specs=[anywhere] * 4,
+    packed = (sum(lines), half, LANES)
+    far = pl.pallas_call(
+        far_kernel,
+        out_shape=shape(tiles, *packed),
+        in_specs=[anywhere] * 3,
+        out_specs=vmem,
+        scratch_shapes=[pltpu.SemaphoreType.DMA((3 * tiles,))],
+        compiler_params=params,
+        name="far",
+    )(*held(*own))
+    *own, fy, fx, near = pl.pallas_call(
+        own_kernel,
+        out_shape=[shape(tiles, n, rows, LANES) for n in lines]
+        + [shape(*factor_y.shape), shape(*factor_x.shape), [shape(*packed)] * tiles],
+        in_specs=[anywhere] * 6,
         out_specs=[vmem] * 5 + [[vmem] * tiles],
-        scratch_shapes=[pltpu.SemaphoreType.DMA((3 * tiles + 1,))],
+        scratch_shapes=[
+            pltpu.SemaphoreType.DMA((3 * tiles,)),
+            pltpu.SemaphoreType.DMA((3 * tiles + 2,)),
+        ],
         compiler_params=params,
-        name="start",
-    )(*[pltpu.with_memory_space_constraint(a, pltpu.HBM) for a in (*own, factor_y)])
+        name="own",
+    )(*held(*own, factor_y, factor_x), far)
+    own = [a.reshape(tiles, -1, LANES) for a in own]
+    far = far.reshape(tiles, -1, LANES)
+    near = [a.reshape(-1, LANES) for a in near]
     far = lax.ppermute(far, "gx", [(i, (i - 1 + i % 2 * 2) % n_gx) for i in range(n_gx)])
     near = [lax.ppermute(a, "gx", [(i, i ^ 1) for i in range(n_gx)]) for a in near]
     own_fm = pl.pallas_call(
@@ -569,11 +623,12 @@
     )(near[-1], factor_m)
     other_fm = lax.ppermute(own_fm, "mem", [(0, 1), (1, 0)])
     sections = 2 * STEPS
-    edges, early = pl.pallas_call(
+    edges, early, turned_fy = pl.pallas_call(
         inner_kernel,
         out_shape=[
             shape(sections * 9 * members, cells_y),
             shape(2 * half * devices, LANES),
+            shape(ry, cells_y),
         ],
         scratch_shapes=[pltpu.VMEM((3 * half * members, cells_y), jnp.float32)],
         compiler_params=params,
@@ -588,7 +643,7 @@
         scratch_shapes=[pltpu.VMEM((3 * half * members, cells_y), jnp.float32)],
         compiler_params=params,
         name="outer",
-    )(*own, far, fy, edges, early, factor_x, other_fm)
+    )(*own, far, turned_fy, edges, early, fx, other_fm)
     got = exchange(sent, devices)
     lows = rm // 2
     high = 3 * shares * lows * SUBLANES // LANES
@@ -602,11 +657,16 @@
     got = exchange(sent, devices)
     core = pl.pallas_call(
         functools.partial(gather_kernel, shares, lows),
-        out_shape=jax.ShapeDtypeStruct((lows * 3 * SUBLANES, LANES), jnp.float32),
+        out_shape=shape(lows, 3, SUBLANES, LANES),
+        out_specs=anywhere,
+        scratch_shapes=[
+            pltpu.VMEM((3, lows * SUBLANES, LANES), jnp.float32),
+            pltpu.SemaphoreType.DMA((3,)),
+        ],
         compiler_params=params,
         name="gather",
     )(got)
-    return core.reshape(lows, 3, SUBLANES, ry)
+    return core
 
 
 def solution(mesh):

time: 40.5 us -> 40.2 us (level)
  blocking collectives: 24.8 us -> 24.1 us
    pallas_call x1 -> x2, Pallas kernels: 1.2 us -> 2.34 us  [the longest x1 1.36 us: on_device(): pl.pallas_call(own_kernel, out_shape=[shape(tiles, n, rows, LANES) for n...]
    pallas_call x1, Pallas kernels: 3.57 us -> 2.81 us  [on_device(): pl.pallas_call(inner_kernel, out_shape=[shape(sections * 9 * members, cel...]
    all_to_all x2, blocking collectives: 24.8 us -> 24.1 us  [exchange(): lax.all_to_all(block, ('mem', 'gx'), split_axis=0, concat_axis=0, tiled=T...]
  transfers between devices with their start and end apart: 4 -> 4, of which waited for: 1 -> 1; matrix products, arithmetic and copies ran while one was open for 0% -> 0% of each run, Pallas kernels for 9% -> 11%
where the time goes in v5:
time: 40.2 us; the launch traced here: 40 us
  blocking collectives  24.1 us (60%)
  Pallas kernels  8.03 us (20%)
  starting transfers between devices  6.95 us (17%)
  waiting for transfers between devices  0.88 us (2%)
    all_to_all x2, blocking collectives, exchange(): lax.all_to_all(block, ('mem', 'gx'), split_axis=0, concat_axis=0, tiled=T...  24.1 us
    ppermute x2, starting transfers between devices, on_device(): lax.ppermute(a, 'gx', [(i, i ^ 1) for i in range(n_gx)])  3.04 us
    pallas_call x1, Pallas kernels, on_device(): pl.pallas_call(inner_kernel, out_shape=[shape(sections * 9 * members, cel...  2.81 us
    ppermute x1, starting transfers between devices, on_device(): lax.ppermute(far, 'gx', [(i, (i - 1 + i % 2 * 2) % n_gx) for i in range(n...  2.67 us
    pallas_call x1, Pallas kernels, on_device(): pl.pallas_call(own_kernel, out_shape=[shape(tiles, n, rows, LANES) for n...  1.36 us
    ppermute x1, starting transfers between devices, on_device(): other_fm = lax.ppermute(own_fm, 'mem', [(0, 1), (1, 0)])  1.24 us
    pallas_call x1, Pallas kernels, on_device(): pl.pallas_call(functools.partial(outer_kernel, n_gx), out_shape=shape(dev...  1.15 us
    pallas_call x1, Pallas kernels, on_device(): pl.pallas_call(far_kernel, out_shape=shape(tiles, *packed), in_specs=[any...  0.98 us
  transfers between devices with their start and end apart: 4, of which 1 were waited for; matrix products, arithmetic and copies ran while one was open for 0% of the time, Pallas kernels for 11%

profile of v5, /device:TPU:1, one launch (start us, length us, event | category | flops | bytes accessed | tf_op | source)
XLA Modules:
  0.0 40.0 jit_solution(6923618252293629949)
XLA Ops:
  0.0 1.0 %far.1 = f32[2,50,4,128]{3,2,1,0:T(4,128)S(1)} custom-call(f32[16,8,256]{2,1,0:T(8,128)} %d.3, f32[32,8,256]{2,1,0:T(8,128)} %bitcast.26, f32[2,8,256]{2,1,0:T(8,128)} %w.3), custom_call_target="tpu_custom_call" | custom-call | tf_op jit(solution)/shard_map/far/pallas_call | solution.py:589
  1.0 2.7 %collective-permute-start = (f32[2,200,128]{2,1,0:T(8,128)S(1)}, f32[2,200,128]{2,1,0:T(8,128)S(1)}, u32[]{:S(2)}, u32[]{:S(2)}) collective-permute-start(f32[2,200,128]{2,1,0:T(8,128)S(1)} %bitcast.17), channel_id=1, source_target_pairs={{0,15},{1,2},{2,1},{3,4},{4,3},{5,6},{6,5},{7,8},{8,7},{9,10},{10,... | collective-permute-start | bytes 614408 | tf_op jit(solution)/shard_map/ppermute | solution.py:614
  3.7 0.0 copy-start
  3.7 1.4 %own.1 = (f32[2,16,8,128]{3,2,1,0:T(8,128)S(1)}, f32[2,32,8,128]{3,2,1,0:T(8,128)S(1)}, f32[2,2,8,128]{3,2,1,0:T(8,128)S(1)}, f32[256,128]{1,0:T(8,128)S(1)}, f3...) custom-call(f32[16,8,256]{2,1,0:T(8,128)} %d.3, f32[32,8,256]{2,1,0:T(8,128)} %bitcast.27, ...), custom_call_target="tpu_custom_call" | custom-call | tf_op jit(solution)/shard_map/own/pallas_call | solution.py:598
  5.0 3.0 %collective-permute-start.2 = (f32[200,128]{1,0:T(8,128)S(1)}, f32[200,128]{1,0:T(8,128)S(1)}, u32[]{:S(2)}, u32[]{:S(2)}) collective-permute-start(f32[200,128]{1,0:T(8,128)S(1)} %bitcast.25), channel_id=1, source_target_pairs={{0,1},{1,0},{2,3},{3,2},{4,5},{5,4},{6,7},{7,6},{8,9},{9,8},{10,11... | collective-permute-start | bytes 307208 | tf_op jit(solution)/shard_map/ppermute | solution.py:615
  8.0 0.1 collective-permute-start.1
  8.1 0.9 %collective-permute-done.2.rest_1_.near = f32[200,128]{1,0:T(8,128)S(1)} collective-permute-done((f32[200,128]{1,0:T(8,128)S(1)}, f32[200,128]{1,0:T(8,128)S(1)}, u32[]{:S(2)}, u32[]{:S(2)}) %collective-permute-start.2) | collective-permute-done | bytes 102432 | tf_op jit(solution)/shard_map/ppermute | solution.py:615
  8.9 0.0 copy-done
  8.9 0.1 member.1.own_fm
  9.0 1.2 %collective-permute-start.3 = (f32[16,128]{1,0:T(8,128)S(1)}, f32[16,128]{1,0:T(8,128)S(1)}, u32[]{:S(2)}, u32[]{:S(2)}) collective-permute-start(f32[16,128]{1,0:T(8,128)S(1)} %member.1.own_fm), channel_id=1, source_target_pairs={{0,16},{16,0},{1,17},{17,1},{2,18},{18,2},{3,19},{19,3},{4,20},{20... | collective-permute-start | bytes 24584 | tf_op jit(solution)/shard_map/ppermute | solution.py:624
  10.3 0.0 collective-permute-done.1.rest_0_
  10.3 2.8 %inner.1 = (f32[576,256]{1,0:T(8,128)S(1)}, f32[256,128]{1,0:T(8,128)S(1)}, f32[128,256]{1,0:T(8,128)S(1)}) custom-call(f32[2,128,128]{2,1,0:T(8,128)S(1)} %bitcast.20, f32[2,256,128]{2,1,0:T(8,128)S(1)} %bitcast.13, f32[2,16,128]{2,1,0:T(8,128)S(1)} %bitcast.22, f32[256,128]{1,0:T(8,128)S(1)} %get-tuple-element.18.fy, ...), custom_call_target="tpu_custom_call" | custom-call | tf_op jit(solution)/shard_map/inner/pallas_call | solution.py:626
  13.1 0.0 collective-permute-done.3.other_fm
  13.1 0.0 collective-permute-done.far
  13.1 1.1 %outer.1 = f32[512,128]{1,0:T(8,128)S(1)} custom-call(f32[2,128,128]{2,1,0:T(8,128)S(1)} %bitcast.21, f32[2,256,128]{2,1,0:T(8,128)S(1)} %bitcast.14, f32[2,16,128]{2,1,0:T(8,128)S(1)} %bitcast.23, f32[2,200,128]{2,1,0:T(8,128)S(1)} %collective-permute-done.far, f32[128,256]{1,0:T(8,128)S(1)} %get-tuple-element.21.fy, ...), custom_call_target="tpu_custom_call" | custom-call | tf_op jit(solution)/shard_map/outer/pallas_call | solution.py:638
  14.3 12.5 %all_to_all.10 = f32[32,16,1,128]{3,1,2,0:T(8,128)S(1)} all-to-all(f32[32,16,1,128]{3,1,2,0:T(8,128)S(1)} %bitcast.16), channel_id=1, replica_groups=mesh['mem'=2,'gx'=16] {'mem','gx'}, dimensions={0} | all-to-all | bytes 524288 | tf_op jit(solution)/shard_map/all_to_all | solution.py:545
  26.8 0.7 %project.1 = f32[384,128]{1,0:T(8,128)S(1)} custom-call(f32[512,128]{1,0:T(8,128)S(1)} %bitcast.15, f32[16,128]{1,0:T(8,128)S(1)} %member.1.own_fm, f32[16,128]{1,0:T(8,128)S(1)} %collective-permute-done.3.other_fm), custom_call_target="tpu_custom_call" | custom-call | tf_op jit(solution)/shard_map/project/pallas_call | solution.py:650
  27.5 11.6 %all_to_all.11 = f32[32,12,1,128]{3,2,1,0:T(1,128)S(1)} all-to-all(f32[32,12,1,128]{3,2,1,0:T(1,128)S(1)} %bitcast.19), channel_id=1, replica_groups=mesh['mem'=2,'gx'=16] {'mem','gx'}, dimensions={0} | all-to-all | bytes 393216 | tf_op jit(solution)/shard_map/all_to_all | solution.py:545
  39.0 1.0 %gather.1 = f32[16,3,8,128]{3,2,1,0:T(8,128)} custom-call(f32[384,128]{1,0:T(8,128)S(1)} %bitcast.18), custom_call_target="tpu_custom_call" | custom-call | tf_op jit(solution)/shard_map/gather/pallas_call | solution.py:658
Async XLA Ops:
  1.0 12.1 %collective-permute-start = (f32[2,200,128]{2,1,0:T(8,128)S(1)}, f32[2,200,128]{2,1,0:T(8,128)S(1)}, u32[]{:S(2)}, u32[]{:S(2)}) collective-permute-start(f32[2,200,128]{2,1,0:T(8,128)S(1)} %bitcast.17), channel_id=1, source_target_pairs={{0,15},{1,2},{2,1},{3,4},{4,3},{5,6},{6,5},{7,8},{8,7},{9,10},{10,... | collective-permute-start | bytes 614408 | tf_op jit(solution)/shard_map/ppermute | solution.py:614
  3.7 5.3 %copy-start = (f32[16,32]{1,0:T(8,128)S(1)}, f32[16,32]{1,0:T(8,128)}, u32[]{:S(2)}) copy-start(f32[16,32]{1,0:T(8,128)} %fm.1) | copy-start | bytes 6148
  5.0 3.9 %collective-permute-start.2 = (f32[200,128]{1,0:T(8,128)S(1)}, f32[200,128]{1,0:T(8,128)S(1)}, u32[]{:S(2)}, u32[]{:S(2)}) collective-permute-start(f32[200,128]{1,0:T(8,128)S(1)} %bitcast.25), channel_id=1, source_target_pairs={{0,1},{1,0},{2,3},{3,2},{4,5},{5,4},{6,7},{7,6},{8,9},{9,8},{10,11... | collective-permute-start | bytes 307208 | tf_op jit(solution)/shard_map/ppermute | solution.py:615
  8.0 2.3 %collective-permute-start.1 = (f32[200,128]{1,0:T(8,128)S(1)}, f32[200,128]{1,0:T(8,128)S(1)}, u32[]{:S(2)}, u32[]{:S(2)}) collective-permute-start(f32[200,128]{1,0:T(8,128)S(1)} %bitcast.24), channel_id=1, source_target_pairs={{0,1},{1,0},{2,3},{3,2},{4,5},{5,4},{6,7},{7,6},{8,9},{9,8},{10,11... | collective-permute-start | bytes 307208 | tf_op jit(solution)/shard_map/ppermute | solution.py:615
  9.0 4.1 %collective-permute-start.3 = (f32[16,128]{1,0:T(8,128)S(1)}, f32[16,128]{1,0:T(8,128)S(1)}, u32[]{:S(2)}, u32[]{:S(2)}) collective-permute-start(f32[16,128]{1,0:T(8,128)S(1)} %member.1.own_fm), channel_id=1, source_target_pairs={{0,16},{16,0},{1,17},{17,1},{2,18},{18,2},{3,19},{19,3},{4,20},{20... | collective-permute-start | bytes 24584 | tf_op jit(solution)/shard_map/ppermute | solution.py:624

commit v6 on v5

--- a/solution.py
+++ b/solution.py
@@ -475,15 +475,15 @@
         axis=0,
     )
     product = functools.partial(jnp.dot, precision=HIGH, preferred_element_type=jnp.float32)
-    firsts = product(firsts, diagonal)
-    thirds = product(thirds, small)
-    blocks = jnp.concatenate([firsts[:, :LANES], thirds, firsts[:, LANES:]], axis=1)
     halves = [line(rows + half + r) for r in range(half)]
     lines = [a[:n_gx] for a in halves] + [a[n_gx:] for a in halves]
     odd = lax.broadcasted_iota(jnp.int32, (n_gx, LANES), 0) % 2 == 1
     lines = [jnp.where(odd, lines[rows - 1 - r], lines[r]) for r in range(rows)]
     fx = jnp.concatenate(lines, axis=0)
-    core = product(fx.T, blocks)
+    turned_fx = fx.T
+    firsts = product(product(turned_fx, firsts), diagonal)
+    thirds = product(product(turned_fx, thirds), small)
+    core = jnp.concatenate([firsts[:, :LANES], thirds, firsts[:, LANES:]], axis=1)
     high = out.shape[0] // devices
     for t in range(3):
         tall[t] = core[:, t * LANES : (t + 1) * LANES]
@@ -521,11 +521,10 @@
                 ],
                 axis=1,
             )
-            out[c, pl.ds(a0 + i, lows, stride=SUBLANES), :] = line
+            out[c, :, a0 + i, :] = line
 
     def send(c):
-        source = out.at[c].reshape(lows, SUBLANES, LANES)
-        return pltpu.make_async_copy(source, core.at[:, c], sems.at[c])
+        return pltpu.make_async_copy(out.at[c], core.at[:, c], sems.at[c])
 
     turned = [turn(h * quarter) for h in range(2)]
     for c in range(2):
@@ -660,7 +659,7 @@
         out_shape=shape(lows, 3, SUBLANES, LANES),
         out_specs=anywhere,
         scratch_shapes=[
-            pltpu.VMEM((3, lows * SUBLANES, LANES), jnp.float32),
+            pltpu.VMEM((3, lows, SUBLANES, LANES), jnp.float32),
             pltpu.SemaphoreType.DMA((3,)),
         ],
         compiler_params=params,

time: 40.2 us -> 40.2 us (level)
  no operation moved by 1% of the time
where the time goes in v6:
time: 40.2 us; the launch traced here: 39.9 us
  blocking collectives  24.1 us (60%)
  Pallas kernels  7.96 us (20%)
  starting transfers between devices  6.95 us (17%)
  waiting for transfers between devices  0.88 us (2%)
    all_to_all x2, blocking collectives, exchange(): lax.all_to_all(block, ('mem', 'gx'), split_axis=0, concat_axis=0, tiled=T...  24.1 us
    ppermute x2, starting transfers between devices, on_device(): lax.ppermute(a, 'gx', [(i, i ^ 1) for i in range(n_gx)])  3.04 us
    pallas_call x1, Pallas kernels, on_device(): pl.pallas_call(inner_kernel, out_shape=[shape(sections * 9 * members, cel...  2.81 us
    ppermute x1, starting transfers between devices, on_device(): lax.ppermute(far, 'gx', [(i, (i - 1 + i % 2 * 2) % n_gx) for i in range(n...  2.67 us
    pallas_call x1, Pallas kernels, on_device(): pl.pallas_call(own_kernel, out_shape=[shape(tiles, n, rows, LANES) for n...  1.36 us
    ppermute x1, starting transfers between devices, on_device(): other_fm = lax.ppermute(own_fm, 'mem', [(0, 1), (1, 0)])  1.24 us
    pallas_call x1, Pallas kernels, on_device(): pl.pallas_call(functools.partial(outer_kernel, n_gx), out_shape=shape(dev...  1.15 us
    pallas_call x1, Pallas kernels, on_device(): pl.pallas_call(functools.partial(gather_kernel, shares, lows), out_shape=...  0.99 us
  transfers between devices with their start and end apart: 4, of which 1 were waited for; matrix products, arithmetic and copies ran while one was open for 0% of the time, Pallas kernels for 11%

profile of v6, /device:TPU:1, one launch (start us, length us, event | category | flops | bytes accessed | tf_op | source)
XLA Modules:
  0.0 39.9 jit_solution(15222178277498802660)
XLA Ops:
  0.0 1.0 %far.1 = f32[2,50,4,128]{3,2,1,0:T(4,128)S(1)} custom-call(f32[16,8,256]{2,1,0:T(8,128)} %d.3, f32[32,8,256]{2,1,0:T(8,128)} %bitcast.26, f32[2,8,256]{2,1,0:T(8,128)} %w.3), custom_call_target="tpu_custom_call" | custom-call | tf_op jit(solution)/shard_map/far/pallas_call | solution.py:588
  1.0 2.7 %collective-permute-start = (f32[2,200,128]{2,1,0:T(8,128)S(1)}, f32[2,200,128]{2,1,0:T(8,128)S(1)}, u32[]{:S(2)}, u32[]{:S(2)}) collective-permute-start(f32[2,200,128]{2,1,0:T(8,128)S(1)} %bitcast.17), channel_id=1, source_target_pairs={{0,15},{1,2},{2,1},{3,4},{4,3},{5,6},{6,5},{7,8},{8,7},{9,10},{10,... | collective-permute-start | bytes 614408 | tf_op jit(solution)/shard_map/ppermute | solution.py:613
  3.7 0.0 copy-start
  3.7 1.4 %own.1 = (f32[2,16,8,128]{3,2,1,0:T(8,128)S(1)}, f32[2,32,8,128]{3,2,1,0:T(8,128)S(1)}, f32[2,2,8,128]{3,2,1,0:T(8,128)S(1)}, f32[256,128]{1,0:T(8,128)S(1)}, f3...) custom-call(f32[16,8,256]{2,1,0:T(8,128)} %d.3, f32[32,8,256]{2,1,0:T(8,128)} %bitcast.27, ...), custom_call_target="tpu_custom_call" | custom-call | tf_op jit(solution)/shard_map/own/pallas_call | solution.py:597
  5.0 3.0 %collective-permute-start.2 = (f32[200,128]{1,0:T(8,128)S(1)}, f32[200,128]{1,0:T(8,128)S(1)}, u32[]{:S(2)}, u32[]{:S(2)}) collective-permute-start(f32[200,128]{1,0:T(8,128)S(1)} %bitcast.25), channel_id=1, source_target_pairs={{0,1},{1,0},{2,3},{3,2},{4,5},{5,4},{6,7},{7,6},{8,9},{9,8},{10,11... | collective-permute-start | bytes 307208 | tf_op jit(solution)/shard_map/ppermute | solution.py:614
  8.0 0.1 collective-permute-start.1
  8.1 0.9 %collective-permute-done.2.rest_1_.near = f32[200,128]{1,0:T(8,128)S(1)} collective-permute-done((f32[200,128]{1,0:T(8,128)S(1)}, f32[200,128]{1,0:T(8,128)S(1)}, u32[]{:S(2)}, u32[]{:S(2)}) %collective-permute-start.2) | collective-permute-done | bytes 102432 | tf_op jit(solution)/shard_map/ppermute | solution.py:614
  8.9 0.0 copy-done
  8.9 0.1 member.1.own_fm
  9.0 1.2 %collective-permute-start.3 = (f32[16,128]{1,0:T(8,128)S(1)}, f32[16,128]{1,0:T(8,128)S(1)}, u32[]{:S(2)}, u32[]{:S(2)}) collective-permute-start(f32[16,128]{1,0:T(8,128)S(1)} %member.1.own_fm), channel_id=1, source_target_pairs={{0,16},{16,0},{1,17},{17,1},{2,18},{18,2},{3,19},{19,3},{4,20},{20... | collective-permute-start | bytes 24584 | tf_op jit(solution)/shard_map/ppermute | solution.py:623
  10.3 0.0 collective-permute-done.1.rest_0_
  10.3 2.8 %inner.1 = (f32[576,256]{1,0:T(8,128)S(1)}, f32[256,128]{1,0:T(8,128)S(1)}, f32[128,256]{1,0:T(8,128)S(1)}) custom-call(f32[2,128,128]{2,1,0:T(8,128)S(1)} %bitcast.20, f32[2,256,128]{2,1,0:T(8,128)S(1)} %bitcast.13, f32[2,16,128]{2,1,0:T(8,128)S(1)} %bitcast.22, f32[256,128]{1,0:T(8,128)S(1)} %get-tuple-element.18.fy, ...), custom_call_target="tpu_custom_call" | custom-call | tf_op jit(solution)/shard_map/inner/pallas_call | solution.py:625
  13.1 0.0 collective-permute-done.3.other_fm
  13.1 0.0 collective-permute-done.far
  13.1 1.1 %outer.1 = f32[512,128]{1,0:T(8,128)S(1)} custom-call(f32[2,128,128]{2,1,0:T(8,128)S(1)} %bitcast.21, f32[2,256,128]{2,1,0:T(8,128)S(1)} %bitcast.14, f32[2,16,128]{2,1,0:T(8,128)S(1)} %bitcast.23, f32[2,200,128]{2,1,0:T(8,128)S(1)} %collective-permute-done.far, f32[128,256]{1,0:T(8,128)S(1)} %get-tuple-element.21.fy, ...), custom_call_target="tpu_custom_call" | custom-call | tf_op jit(solution)/shard_map/outer/pallas_call | solution.py:637
  14.3 12.5 %all_to_all.10 = f32[32,16,1,128]{3,1,2,0:T(8,128)S(1)} all-to-all(f32[32,16,1,128]{3,1,2,0:T(8,128)S(1)} %bitcast.16), channel_id=1, replica_groups=mesh['mem'=2,'gx'=16] {'mem','gx'}, dimensions={0} | all-to-all | bytes 524288 | tf_op jit(solution)/shard_map/all_to_all | solution.py:544
  26.8 0.6 %project.1 = f32[384,128]{1,0:T(8,128)S(1)} custom-call(f32[512,128]{1,0:T(8,128)S(1)} %bitcast.15, f32[16,128]{1,0:T(8,128)S(1)} %member.1.own_fm, f32[16,128]{1,0:T(8,128)S(1)} %collective-permute-done.3.other_fm), custom_call_target="tpu_custom_call" | custom-call | tf_op jit(solution)/shard_map/project/pallas_call | solution.py:649
  27.4 11.6 %all_to_all.11 = f32[32,12,1,128]{3,2,1,0:T(1,128)S(1)} all-to-all(f32[32,12,1,128]{3,2,1,0:T(1,128)S(1)} %bitcast.19), channel_id=1, replica_groups=mesh['mem'=2,'gx'=16] {'mem','gx'}, dimensions={0} | all-to-all | bytes 393216 | tf_op jit(solution)/shard_map/all_to_all | solution.py:544
  39.0 1.0 %gather.1 = f32[16,3,8,128]{3,2,1,0:T(8,128)} custom-call(f32[384,128]{1,0:T(8,128)S(1)} %bitcast.18), custom_call_target="tpu_custom_call" | custom-call | tf_op jit(solution)/shard_map/gather/pallas_call | solution.py:657
Async XLA Ops:
  1.0 12.1 %collective-permute-start = (f32[2,200,128]{2,1,0:T(8,128)S(1)}, f32[2,200,128]{2,1,0:T(8,128)S(1)}, u32[]{:S(2)}, u32[]{:S(2)}) collective-permute-start(f32[2,200,128]{2,1,0:T(8,128)S(1)} %bitcast.17), channel_id=1, source_target_pairs={{0,15},{1,2},{2,1},{3,4},{4,3},{5,6},{6,5},{7,8},{8,7},{9,10},{10,... | collective-permute-start | bytes 614408 | tf_op jit(solution)/shard_map/ppermute | solution.py:613
  3.7 5.3 %copy-start = (f32[16,32]{1,0:T(8,128)S(1)}, f32[16,32]{1,0:T(8,128)}, u32[]{:S(2)}) copy-start(f32[16,32]{1,0:T(8,128)} %fm.1) | copy-start | bytes 6148
  5.0 3.9 %collective-permute-start.2 = (f32[200,128]{1,0:T(8,128)S(1)}, f32[200,128]{1,0:T(8,128)S(1)}, u32[]{:S(2)}, u32[]{:S(2)}) collective-permute-start(f32[200,128]{1,0:T(8,128)S(1)} %bitcast.25), channel_id=1, source_target_pairs={{0,1},{1,0},{2,3},{3,2},{4,5},{5,4},{6,7},{7,6},{8,9},{9,8},{10,11... | collective-permute-start | bytes 307208 | tf_op jit(solution)/shard_map/ppermute | solution.py:614
  8.0 2.3 %collective-permute-start.1 = (f32[200,128]{1,0:T(8,128)S(1)}, f32[200,128]{1,0:T(8,128)S(1)}, u32[]{:S(2)}, u32[]{:S(2)}) collective-permute-start(f32[200,128]{1,0:T(8,128)S(1)} %bitcast.24), channel_id=1, source_target_pairs={{0,1},{1,0},{2,3},{3,2},{4,5},{5,4},{6,7},{7,6},{8,9},{9,8},{10,11... | collective-permute-start | bytes 307208 | tf_op jit(solution)/shard_map/ppermute | solution.py:614
  9.0 4.1 %collective-permute-start.3 = (f32[16,128]{1,0:T(8,128)S(1)}, f32[16,128]{1,0:T(8,128)S(1)}, u32[]{:S(2)}, u32[]{:S(2)}) collective-permute-start(f32[16,128]{1,0:T(8,128)S(1)} %member.1.own_fm), channel_id=1, source_target_pairs={{0,16},{16,0},{1,17},{17,1},{2,18},{18,2},{3,19},{19,3},{4,20},{20... | collective-permute-start | bytes 24584 | tf_op jit(solution)/shard_map/ppermute | solution.py:623

commit v7 on v6

--- a/solution.py
+++ b/solution.py
@@ -120,16 +120,13 @@
 def y_difference(row):
     axis = row["ay"].ndim - 1
     size = row["ay"].shape[axis]
-    after = lambda a: pltpu.roll(a, size - 1, axis)
-    before = lambda a: pltpu.roll(a, 1, axis)
-    moved_q = tuple(after(a) for a in row["q"])
-    moved_g = (moved_q[2], after(row["g"][1]), after(row["g"][2]))
-    bound = jnp.maximum(row["ay"], after(row["ay"]))
+    q = tuple(pltpu.roll(a, size - 1, axis) for a in row["q"])
+    ahead = cell_terms(q)
+    bound = jnp.maximum(row["ay"], ahead["ay"])
     face = tuple(
-        ga + gb - bound * (b - a)
-        for ga, gb, a, b in zip(row["g"], moved_g, row["q"], moved_q)
-    )
-    return tuple(a - before(a) for a in face)
+        ga + gb - bound * (b - a) for ga, gb, a, b in zip(row["g"], ahead["g"], row["q"], q)
+    )
+    return tuple(a - pltpu.roll(a, 1, axis) for a in face)
 
 
 def section(row, low_face, high_face, wish):

time: 40.2 us -> 40.2 us (level)
  transfers between devices with their start and end apart: 4 -> 4, of which waited for: 1 -> 1; matrix products, arithmetic and copies ran while one was open for 0% -> 0% of each run, Pallas kernels for 11% -> 10%
where the time goes in v7:
time: 40.2 us; the launch traced here: 39.9 us
  blocking collectives  24.5 us (61%)
  Pallas kernels  7.57 us (19%)
  starting transfers between devices  6.95 us (17%)
  waiting for transfers between devices  0.88 us (2%)
    all_to_all x2, blocking collectives, exchange(): lax.all_to_all(block, ('mem', 'gx'), split_axis=0, concat_axis=0, tiled=T...  24.5 us
    ppermute x2, starting transfers between devices, on_device(): lax.ppermute(a, 'gx', [(i, i ^ 1) for i in range(n_gx)])  3.04 us
    ppermute x1, starting transfers between devices, on_device(): lax.ppermute(far, 'gx', [(i, (i - 1 + i % 2 * 2) % n_gx) for i in range(n...  2.67 us
    pallas_call x1, Pallas kernels, on_device(): pl.pallas_call(inner_kernel, out_shape=[shape(sections * 9 * members, cel...  2.43 us
    pallas_call x1, Pallas kernels, on_device(): pl.pallas_call(own_kernel, out_shape=[shape(tiles, n, rows, LANES) for n...  1.36 us
    ppermute x1, starting transfers between devices, on_device(): other_fm = lax.ppermute(own_fm, 'mem', [(0, 1), (1, 0)])  1.24 us
    pallas_call x1, Pallas kernels, on_device(): pl.pallas_call(functools.partial(outer_kernel, n_gx), out_shape=shape(dev...  1.15 us
    pallas_call x1, Pallas kernels, on_device(): pl.pallas_call(functools.partial(gather_kernel, shares, lows), out_shape=...  0.99 us
  transfers between devices with their start and end apart: 4, of which 1 were waited for; matrix products, arithmetic and copies ran while one was open for 0% of the time, Pallas kernels for 10%

profile of v7, /device:TPU:1, one launch (start us, length us, event | category | flops | bytes accessed | tf_op | source)
XLA Modules:
  0.0 39.9 jit_solution(17756313654437088349)
XLA Ops:
  0.0 1.0 %far.1 = f32[2,50,4,128]{3,2,1,0:T(4,128)S(1)} custom-call(f32[16,8,256]{2,1,0:T(8,128)} %d.3, f32[32,8,256]{2,1,0:T(8,128)} %bitcast.26, f32[2,8,256]{2,1,0:T(8,128)} %w.3), custom_call_target="tpu_custom_call" | custom-call | tf_op jit(solution)/shard_map/far/pallas_call | solution.py:585
  1.0 2.7 %collective-permute-start = (f32[2,200,128]{2,1,0:T(8,128)S(1)}, f32[2,200,128]{2,1,0:T(8,128)S(1)}, u32[]{:S(2)}, u32[]{:S(2)}) collective-permute-start(f32[2,200,128]{2,1,0:T(8,128)S(1)} %bitcast.17), channel_id=1, source_target_pairs={{0,15},{1,2},{2,1},{3,4},{4,3},{5,6},{6,5},{7,8},{8,7},{9,10},{10,... | collective-permute-start | bytes 614408 | tf_op jit(solution)/shard_map/ppermute | solution.py:610
  3.7 0.0 copy-start
  3.7 1.4 %own.1 = (f32[2,16,8,128]{3,2,1,0:T(8,128)S(1)}, f32[2,32,8,128]{3,2,1,0:T(8,128)S(1)}, f32[2,2,8,128]{3,2,1,0:T(8,128)S(1)}, f32[256,128]{1,0:T(8,128)S(1)}, f3...) custom-call(f32[16,8,256]{2,1,0:T(8,128)} %d.3, f32[32,8,256]{2,1,0:T(8,128)} %bitcast.27, ...), custom_call_target="tpu_custom_call" | custom-call | tf_op jit(solution)/shard_map/own/pallas_call | solution.py:594
  5.0 3.0 %collective-permute-start.2 = (f32[200,128]{1,0:T(8,128)S(1)}, f32[200,128]{1,0:T(8,128)S(1)}, u32[]{:S(2)}, u32[]{:S(2)}) collective-permute-start(f32[200,128]{1,0:T(8,128)S(1)} %bitcast.25), channel_id=1, source_target_pairs={{0,1},{1,0},{2,3},{3,2},{4,5},{5,4},{6,7},{7,6},{8,9},{9,8},{10,11... | collective-permute-start | bytes 307208 | tf_op jit(solution)/shard_map/ppermute | solution.py:611
  8.0 0.1 collective-permute-start.1
  8.1 0.9 %collective-permute-done.2.rest_1_.near = f32[200,128]{1,0:T(8,128)S(1)} collective-permute-done((f32[200,128]{1,0:T(8,128)S(1)}, f32[200,128]{1,0:T(8,128)S(1)}, u32[]{:S(2)}, u32[]{:S(2)}) %collective-permute-start.2) | collective-permute-done | bytes 102432 | tf_op jit(solution)/shard_map/ppermute | solution.py:611
  8.9 0.0 copy-done
  8.9 0.1 member.1.own_fm
  9.0 1.2 %collective-permute-start.3 = (f32[16,128]{1,0:T(8,128)S(1)}, f32[16,128]{1,0:T(8,128)S(1)}, u32[]{:S(2)}, u32[]{:S(2)}) collective-permute-start(f32[16,128]{1,0:T(8,128)S(1)} %member.1.own_fm), channel_id=1, source_target_pairs={{0,16},{16,0},{1,17},{17,1},{2,18},{18,2},{3,19},{19,3},{4,20},{20... | collective-permute-start | bytes 24584 | tf_op jit(solution)/shard_map/ppermute | solution.py:620
  10.3 0.0 collective-permute-done.1.rest_0_
  10.3 2.4 %inner.1 = (f32[576,256]{1,0:T(8,128)S(1)}, f32[256,128]{1,0:T(8,128)S(1)}, f32[128,256]{1,0:T(8,128)S(1)}) custom-call(f32[2,128,128]{2,1,0:T(8,128)S(1)} %bitcast.20, f32[2,256,128]{2,1,0:T(8,128)S(1)} %bitcast.13, f32[2,16,128]{2,1,0:T(8,128)S(1)} %bitcast.22, f32[256,128]{1,0:T(8,128)S(1)} %get-tuple-element.18.fy, ...), custom_call_target="tpu_custom_call" | custom-call | tf_op jit(solution)/shard_map/inner/pallas_call | solution.py:622
  12.7 0.0 collective-permute-done.3.other_fm
  12.7 0.0 collective-permute-done.far
  12.7 1.1 %outer.1 = f32[512,128]{1,0:T(8,128)S(1)} custom-call(f32[2,128,128]{2,1,0:T(8,128)S(1)} %bitcast.21, f32[2,256,128]{2,1,0:T(8,128)S(1)} %bitcast.14, f32[2,16,128]{2,1,0:T(8,128)S(1)} %bitcast.23, f32[2,200,128]{2,1,0:T(8,128)S(1)} %collective-permute-done.far, f32[128,256]{1,0:T(8,128)S(1)} %get-tuple-element.21.fy, ...), custom_call_target="tpu_custom_call" | custom-call | tf_op jit(solution)/shard_map/outer/pallas_call | solution.py:634
  13.9 12.9 %all_to_all.10 = f32[32,16,1,128]{3,1,2,0:T(8,128)S(1)} all-to-all(f32[32,16,1,128]{3,1,2,0:T(8,128)S(1)} %bitcast.16), channel_id=1, replica_groups=mesh['mem'=2,'gx'=16] {'mem','gx'}, dimensions={0} | all-to-all | bytes 524288 | tf_op jit(solution)/shard_map/all_to_all | solution.py:541
  26.8 0.6 %project.1 = f32[384,128]{1,0:T(8,128)S(1)} custom-call(f32[512,128]{1,0:T(8,128)S(1)} %bitcast.15, f32[16,128]{1,0:T(8,128)S(1)} %member.1.own_fm, f32[16,128]{1,0:T(8,128)S(1)} %collective-permute-done.3.other_fm), custom_call_target="tpu_custom_call" | custom-call | tf_op jit(solution)/shard_map/project/pallas_call | solution.py:646
  27.4 11.6 %all_to_all.11 = f32[32,12,1,128]{3,2,1,0:T(1,128)S(1)} all-to-all(f32[32,12,1,128]{3,2,1,0:T(1,128)S(1)} %bitcast.19), channel_id=1, replica_groups=mesh['mem'=2,'gx'=16] {'mem','gx'}, dimensions={0} | all-to-all | bytes 393216 | tf_op jit(solution)/shard_map/all_to_all | solution.py:541
  39.0 1.0 %gather.1 = f32[16,3,8,128]{3,2,1,0:T(8,128)} custom-call(f32[384,128]{1,0:T(8,128)S(1)} %bitcast.18), custom_call_target="tpu_custom_call" | custom-call | tf_op jit(solution)/shard_map/gather/pallas_call | solution.py:654
Async XLA Ops:
  1.0 11.7 %collective-permute-start = (f32[2,200,128]{2,1,0:T(8,128)S(1)}, f32[2,200,128]{2,1,0:T(8,128)S(1)}, u32[]{:S(2)}, u32[]{:S(2)}) collective-permute-start(f32[2,200,128]{2,1,0:T(8,128)S(1)} %bitcast.17), channel_id=1, source_target_pairs={{0,15},{1,2},{2,1},{3,4},{4,3},{5,6},{6,5},{7,8},{8,7},{9,10},{10,... | collective-permute-start | bytes 614408 | tf_op jit(solution)/shard_map/ppermute | solution.py:610
  3.7 5.3 %copy-start = (f32[16,32]{1,0:T(8,128)S(1)}, f32[16,32]{1,0:T(8,128)}, u32[]{:S(2)}) copy-start(f32[16,32]{1,0:T(8,128)} %fm.1) | copy-start | bytes 6148
  5.0 3.9 %collective-permute-start.2 = (f32[200,128]{1,0:T(8,128)S(1)}, f32[200,128]{1,0:T(8,128)S(1)}, u32[]{:S(2)}, u32[]{:S(2)}) collective-permute-start(f32[200,128]{1,0:T(8,128)S(1)} %bitcast.25), channel_id=1, source_target_pairs={{0,1},{1,0},{2,3},{3,2},{4,5},{5,4},{6,7},{7,6},{8,9},{9,8},{10,11... | collective-permute-start | bytes 307208 | tf_op jit(solution)/shard_map/ppermute | solution.py:611
  8.0 2.3 %collective-permute-start.1 = (f32[200,128]{1,0:T(8,128)S(1)}, f32[200,128]{1,0:T(8,128)S(1)}, u32[]{:S(2)}, u32[]{:S(2)}) collective-permute-start(f32[200,128]{1,0:T(8,128)S(1)} %bitcast.24), channel_id=1, source_target_pairs={{0,1},{1,0},{2,3},{3,2},{4,5},{5,4},{6,7},{7,6},{8,9},{9,8},{10,11... | collective-permute-start | bytes 307208 | tf_op jit(solution)/shard_map/ppermute | solution.py:611
  9.0 3.7 %collective-permute-start.3 = (f32[16,128]{1,0:T(8,128)S(1)}, f32[16,128]{1,0:T(8,128)S(1)}, u32[]{:S(2)}, u32[]{:S(2)}) collective-permute-start(f32[16,128]{1,0:T(8,128)S(1)} %member.1.own_fm), channel_id=1, source_target_pairs={{0,16},{16,0},{1,17},{17,1},{2,18},{18,2},{3,19},{19,3},{4,20},{20... | collective-permute-start | bytes 24584 | tf_op jit(solution)/shard_map/ppermute | solution.py:620

commit v8 on v7

--- a/solution.py
+++ b/solution.py
@@ -474,7 +474,7 @@
     product = functools.partial(jnp.dot, precision=HIGH, preferred_element_type=jnp.float32)
     halves = [line(rows + half + r) for r in range(half)]
     lines = [a[:n_gx] for a in halves] + [a[n_gx:] for a in halves]
-    odd = lax.broadcasted_iota(jnp.int32, (n_gx, LANES), 0) % 2 == 1
+    odd = lax.broadcasted_iota(jnp.int32, (n_gx, LANES), 0) >= n_gx // 2
     lines = [jnp.where(odd, lines[rows - 1 - r], lines[r]) for r in range(rows)]
     fx = jnp.concatenate(lines, axis=0)
     turned_fx = fx.T
@@ -484,19 +484,21 @@
     high = out.shape[0] // devices
     for t in range(3):
         tall[t] = core[:, t * LANES : (t + 1) * LANES]
-    lane = lax.broadcasted_iota(jnp.int32, (n_gx, LANES), 1)
-    for a in range(SUBLANES):
-        for k in range(2):
-            out[pl.ds(k * n_gx * high + a, n_gx, stride=high), :] = tall[
-                2 * k, pl.ds(a, n_gx, stride=SUBLANES), :
-            ]
-    for i in range(SUBLANES // 2):
-        upper = tall[1, pl.ds(i, n_gx, stride=SUBLANES), :]
-        lower = tall[1, pl.ds(i + SUBLANES // 2, n_gx, stride=SUBLANES), :]
-        first = jnp.where(lane < LANES // 2, upper, pltpu.roll(lower, LANES // 2, 1))
-        second = jnp.where(lane < LANES // 2, pltpu.roll(upper, LANES // 2, 1), lower)
-        out[pl.ds(SUBLANES + i, n_gx, stride=high), :] = first
-        out[pl.ds(n_gx * high + SUBLANES + i, n_gx, stride=high), :] = second
+    pairs = n_gx // 2
+    lane = lax.broadcasted_iota(jnp.int32, (pairs, LANES), 1)
+    for odd in range(2):
+        share = lambda t, a: tall[t, pl.ds(odd * SUBLANES + a, pairs, stride=2 * SUBLANES), :]
+        spot = lambda k, i: pl.ds((k * n_gx + odd * pairs) * high + i, pairs, stride=high)
+        for a in range(SUBLANES):
+            for k in range(2):
+                out[spot(k, a), :] = share(2 * k, a)
+        for i in range(SUBLANES // 2):
+            upper = share(1, i)
+            lower = share(1, i + SUBLANES // 2)
+            first = jnp.where(lane < middle, upper, swap(lower))
+            second = jnp.where(lane < middle, swap(upper), lower)
+            out[spot(0, SUBLANES + i), :] = first
+            out[spot(1, SUBLANES + i), :] = second
 
 
 def gather_kernel(shares, lows, inp, core, out, sems):
@@ -538,7 +540,11 @@
 
 def exchange(chunks, devices):
     block = chunks.reshape(devices, chunks.shape[0] // devices, 1, chunks.shape[1])
-    moved = lax.all_to_all(block, ("mem", "gx"), split_axis=0, concat_axis=0, tiled=True)
+    n_gx = lax.axis_size("gx")
+    order = [mem * n_gx + i for mem in range(devices // n_gx) for odd in range(2) for i in range(odd, n_gx, 2)]
+    moved = lax.all_to_all(
+        block, ("mem", "gx"), split_axis=0, concat_axis=0, axis_index_groups=[order], tiled=True
+    )
     return moved.reshape(chunks.shape)
 
 

time: 40.2 us -> 39.8 us (0.990)
  blocking collectives: 24.5 us -> 23.8 us
    all_to_all x2, blocking collectives: 24.5 us -> 23.8 us  [exchange(): lax.all_to_all(block, ('mem', 'gx'), split_axis=0, concat_axis=0, axis_in...]
where the time goes in v8:
time: 39.8 us; the launch traced here: 39.3 us
  blocking collectives  23.8 us (60%)
  Pallas kernels  7.58 us (19%)
  starting transfers between devices  6.95 us (17%)
  waiting for transfers between devices  0.88 us (2%)
    all_to_all x2, blocking collectives, exchange(): lax.all_to_all(block, ('mem', 'gx'), split_axis=0, concat_axis=0, axis_in...  23.8 us
    ppermute x2, starting transfers between devices, on_device(): lax.ppermute(a, 'gx', [(i, i ^ 1) for i in range(n_gx)])  3.04 us
    ppermute x1, starting transfers between devices, on_device(): lax.ppermute(far, 'gx', [(i, (i - 1 + i % 2 * 2) % n_gx) for i in range(n...  2.67 us
    pallas_call x1, Pallas kernels, on_device(): pl.pallas_call(inner_kernel, out_shape=[shape(sections * 9 * members, cel...  2.43 us
    pallas_call x1, Pallas kernels, on_device(): pl.pallas_call(own_kernel, out_shape=[shape(tiles, n, rows, LANES) for n...  1.36 us
    ppermute x1, starting transfers between devices, on_device(): other_fm = lax.ppermute(own_fm, 'mem', [(0, 1), (1, 0)])  1.24 us
    pallas_call x1, Pallas kernels, on_device(): pl.pallas_call(functools.partial(outer_kernel, n_gx), out_shape=shape(dev...  1.15 us
    pallas_call x1, Pallas kernels, on_device(): pl.pallas_call(functools.partial(gather_kernel, shares, lows), out_shape=...  0.99 us
  transfers between devices with their start and end apart: 4, of which 1 were waited for; matrix products, arithmetic and copies ran while one was open for 0% of the time, Pallas kernels for 10%

profile of v8, /device:TPU:1, one launch (start us, length us, event | category | flops | bytes accessed | tf_op | source)
XLA Modules:
  0.0 39.3 jit_solution(8426039893549468644)
XLA Ops:
  0.0 1.0 %far.1 = f32[2,50,4,128]{3,2,1,0:T(4,128)S(1)} custom-call(f32[16,8,256]{2,1,0:T(8,128)} %d.3, f32[32,8,256]{2,1,0:T(8,128)} %bitcast.26, f32[2,8,256]{2,1,0:T(8,128)} %w.3), custom_call_target="tpu_custom_call" | custom-call | tf_op jit(solution)/shard_map/far/pallas_call | solution.py:591
  1.0 2.7 %collective-permute-start = (f32[2,200,128]{2,1,0:T(8,128)S(1)}, f32[2,200,128]{2,1,0:T(8,128)S(1)}, u32[]{:S(2)}, u32[]{:S(2)}) collective-permute-start(f32[2,200,128]{2,1,0:T(8,128)S(1)} %bitcast.17), channel_id=1, source_target_pairs={{0,15},{1,2},{2,1},{3,4},{4,3},{5,6},{6,5},{7,8},{8,7},{9,10},{10,... | collective-permute-start | bytes 614408 | tf_op jit(solution)/shard_map/ppermute | solution.py:616
  3.7 0.0 copy-start
  3.7 1.4 %own.1 = (f32[2,16,8,128]{3,2,1,0:T(8,128)S(1)}, f32[2,32,8,128]{3,2,1,0:T(8,128)S(1)}, f32[2,2,8,128]{3,2,1,0:T(8,128)S(1)}, f32[256,128]{1,0:T(8,128)S(1)}, f3...) custom-call(f32[16,8,256]{2,1,0:T(8,128)} %d.3, f32[32,8,256]{2,1,0:T(8,128)} %bitcast.27, ...), custom_call_target="tpu_custom_call" | custom-call | tf_op jit(solution)/shard_map/own/pallas_call | solution.py:600
  5.0 3.0 %collective-permute-start.2 = (f32[200,128]{1,0:T(8,128)S(1)}, f32[200,128]{1,0:T(8,128)S(1)}, u32[]{:S(2)}, u32[]{:S(2)}) collective-permute-start(f32[200,128]{1,0:T(8,128)S(1)} %bitcast.25), channel_id=1, source_target_pairs={{0,1},{1,0},{2,3},{3,2},{4,5},{5,4},{6,7},{7,6},{8,9},{9,8},{10,11... | collective-permute-start | bytes 307208 | tf_op jit(solution)/shard_map/ppermute | solution.py:617
  8.0 0.1 collective-permute-start.1
  8.1 0.9 %collective-permute-done.2.rest_1_.near = f32[200,128]{1,0:T(8,128)S(1)} collective-permute-done((f32[200,128]{1,0:T(8,128)S(1)}, f32[200,128]{1,0:T(8,128)S(1)}, u32[]{:S(2)}, u32[]{:S(2)}) %collective-permute-start.2) | collective-permute-done | bytes 102432 | tf_op jit(solution)/shard_map/ppermute | solution.py:617
  8.9 0.0 copy-done
  8.9 0.1 member.1.own_fm
  9.0 1.2 %collective-permute-start.3 = (f32[16,128]{1,0:T(8,128)S(1)}, f32[16,128]{1,0:T(8,128)S(1)}, u32[]{:S(2)}, u32[]{:S(2)}) collective-permute-start(f32[16,128]{1,0:T(8,128)S(1)} %member.1.own_fm), channel_id=1, source_target_pairs={{0,16},{16,0},{1,17},{17,1},{2,18},{18,2},{3,19},{19,3},{4,20},{20... | collective-permute-start | bytes 24584 | tf_op jit(solution)/shard_map/ppermute | solution.py:626
  10.3 0.0 collective-permute-done.1.rest_0_
  10.3 2.4 %inner.1 = (f32[576,256]{1,0:T(8,128)S(1)}, f32[256,128]{1,0:T(8,128)S(1)}, f32[128,256]{1,0:T(8,128)S(1)}) custom-call(f32[2,128,128]{2,1,0:T(8,128)S(1)} %bitcast.20, f32[2,256,128]{2,1,0:T(8,128)S(1)} %bitcast.13, f32[2,16,128]{2,1,0:T(8,128)S(1)} %bitcast.22, f32[256,128]{1,0:T(8,128)S(1)} %get-tuple-element.18.fy, ...), custom_call_target="tpu_custom_call" | custom-call | tf_op jit(solution)/shard_map/inner/pallas_call | solution.py:628
  12.7 0.0 collective-permute-done.3.other_fm
  12.7 0.0 collective-permute-done.far
  12.7 1.1 %outer.1 = f32[512,128]{1,0:T(8,128)S(1)} custom-call(f32[2,128,128]{2,1,0:T(8,128)S(1)} %bitcast.21, f32[2,256,128]{2,1,0:T(8,128)S(1)} %bitcast.14, f32[2,16,128]{2,1,0:T(8,128)S(1)} %bitcast.23, f32[2,200,128]{2,1,0:T(8,128)S(1)} %collective-permute-done.far, f32[128,256]{1,0:T(8,128)S(1)} %get-tuple-element.21.fy, ...), custom_call_target="tpu_custom_call" | custom-call | tf_op jit(solution)/shard_map/outer/pallas_call | solution.py:640
  13.9 12.7 %all_to_all.10 = f32[32,16,1,128]{3,1,2,0:T(8,128)S(1)} all-to-all(f32[32,16,1,128]{3,1,2,0:T(8,128)S(1)} %bitcast.16), channel_id=1, replica_groups={{0,2,4,6,8,10,12,14,1,3,5,7,9,11,13,15,16,18,20,22,24,26,28,30,17,19,21..., dimensions={0} | all-to-all | bytes 524288 | tf_op jit(solution)/shard_map/all_to_all | solution.py:545
  26.6 0.6 %project.1 = f32[384,128]{1,0:T(8,128)S(1)} custom-call(f32[512,128]{1,0:T(8,128)S(1)} %bitcast.15, f32[16,128]{1,0:T(8,128)S(1)} %member.1.own_fm, f32[16,128]{1,0:T(8,128)S(1)} %collective-permute-done.3.other_fm), custom_call_target="tpu_custom_call" | custom-call | tf_op jit(solution)/shard_map/project/pallas_call | solution.py:652
  27.2 11.1 %all_to_all.11 = f32[32,12,1,128]{3,2,1,0:T(1,128)S(1)} all-to-all(f32[32,12,1,128]{3,2,1,0:T(1,128)S(1)} %bitcast.19), channel_id=1, replica_groups={{0,2,4,6,8,10,12,14,1,3,5,7,9,11,13,15,16,18,20,22,24,26,28,30,17,19,21..., dimensions={0} | all-to-all | bytes 393216 | tf_op jit(solution)/shard_map/all_to_all | solution.py:545
  38.3 1.0 %gather.1 = f32[16,3,8,128]{3,2,1,0:T(8,128)} custom-call(f32[384,128]{1,0:T(8,128)S(1)} %bitcast.18), custom_call_target="tpu_custom_call" | custom-call | tf_op jit(solution)/shard_map/gather/pallas_call | solution.py:660
Async XLA Ops:
  1.0 11.7 %collective-permute-start = (f32[2,200,128]{2,1,0:T(8,128)S(1)}, f32[2,200,128]{2,1,0:T(8,128)S(1)}, u32[]{:S(2)}, u32[]{:S(2)}) collective-permute-start(f32[2,200,128]{2,1,0:T(8,128)S(1)} %bitcast.17), channel_id=1, source_target_pairs={{0,15},{1,2},{2,1},{3,4},{4,3},{5,6},{6,5},{7,8},{8,7},{9,10},{10,... | collective-permute-start | bytes 614408 | tf_op jit(solution)/shard_map/ppermute | solution.py:616
  3.7 5.3 %copy-start = (f32[16,32]{1,0:T(8,128)S(1)}, f32[16,32]{1,0:T(8,128)}, u32[]{:S(2)}) copy-start(f32[16,32]{1,0:T(8,128)} %fm.1) | copy-start | bytes 6148
  5.0 3.9 %collective-permute-start.2 = (f32[200,128]{1,0:T(8,128)S(1)}, f32[200,128]{1,0:T(8,128)S(1)}, u32[]{:S(2)}, u32[]{:S(2)}) collective-permute-start(f32[200,128]{1,0:T(8,128)S(1)} %bitcast.25), channel_id=1, source_target_pairs={{0,1},{1,0},{2,3},{3,2},{4,5},{5,4},{6,7},{7,6},{8,9},{9,8},{10,11... | collective-permute-start | bytes 307208 | tf_op jit(solution)/shard_map/ppermute | solution.py:617
  8.0 2.3 %collective-permute-start.1 = (f32[200,128]{1,0:T(8,128)S(1)}, f32[200,128]{1,0:T(8,128)S(1)}, u32[]{:S(2)}, u32[]{:S(2)}) collective-permute-start(f32[200,128]{1,0:T(8,128)S(1)} %bitcast.24), channel_id=1, source_target_pairs={{0,1},{1,0},{2,3},{3,2},{4,5},{5,4},{6,7},{7,6},{8,9},{9,8},{10,11... | collective-permute-start | bytes 307208 | tf_op jit(solution)/shard_map/ppermute | solution.py:617
  9.0 3.7 %collective-permute-start.3 = (f32[16,128]{1,0:T(8,128)S(1)}, f32[16,128]{1,0:T(8,128)S(1)}, u32[]{:S(2)}, u32[]{:S(2)}) collective-permute-start(f32[16,128]{1,0:T(8,128)S(1)} %member.1.own_fm), channel_id=1, source_target_pairs={{0,16},{16,0},{1,17},{17,1},{2,18},{18,2},{3,19},{19,3},{4,20},{20... | collective-permute-start | bytes 24584 | tf_op jit(solution)/shard_map/ppermute | solution.py:626

commit v9 on v8

--- a/solution.py
+++ b/solution.py
@@ -478,8 +478,9 @@
     lines = [jnp.where(odd, lines[rows - 1 - r], lines[r]) for r in range(rows)]
     fx = jnp.concatenate(lines, axis=0)
     turned_fx = fx.T
-    firsts = product(product(turned_fx, firsts), diagonal)
-    thirds = product(product(turned_fx, thirds), small)
+    both = product(turned_fx, jnp.concatenate([firsts, thirds], axis=1))
+    firsts = product(both[:, : 2 * LANES], diagonal)
+    thirds = product(both[:, 2 * LANES :], small)
     core = jnp.concatenate([firsts[:, :LANES], thirds, firsts[:, LANES:]], axis=1)
     high = out.shape[0] // devices
     for t in range(3):

time: 39.8 us -> 39.7 us (level)
  no operation moved by 1% of the time
where the time goes in v9:
time: 39.7 us; the launch traced here: 39.2 us
  blocking collectives  23.8 us (60%)
  Pallas kernels  7.51 us (19%)
  starting transfers between devices  6.95 us (18%)
  waiting for transfers between devices  0.88 us (2%)
    all_to_all x2, blocking collectives, exchange(): lax.all_to_all(block, ('mem', 'gx'), split_axis=0, concat_axis=0, axis_in...  23.8 us
    ppermute x2, starting transfers between devices, on_device(): lax.ppermute(a, 'gx', [(i, i ^ 1) for i in range(n_gx)])  3.04 us
    ppermute x1, starting transfers between devices, on_device(): lax.ppermute(far, 'gx', [(i, (i - 1 + i % 2 * 2) % n_gx) for i in range(n...  2.67 us
    pallas_call x1, Pallas kernels, on_device(): pl.pallas_call(inner_kernel, out_shape=[shape(sections * 9 * members, cel...  2.43 us
    pallas_call x1, Pallas kernels, on_device(): pl.pallas_call(own_kernel, out_shape=[shape(tiles, n, rows, LANES) for n...  1.36 us
    ppermute x1, starting transfers between devices, on_device(): other_fm = lax.ppermute(own_fm, 'mem', [(0, 1), (1, 0)])  1.24 us
    pallas_call x1, Pallas kernels, on_device(): pl.pallas_call(functools.partial(outer_kernel, n_gx), out_shape=shape(dev...  1.15 us
    pallas_call x1, Pallas kernels, on_device(): pl.pallas_call(functools.partial(gather_kernel, shares, lows), out_shape=...  0.99 us
  transfers between devices with their start and end apart: 4, of which 1 were waited for; matrix products, arithmetic and copies ran while one was open for 0% of the time, Pallas kernels for 10%

profile of v9, /device:TPU:1, one launch (start us, length us, event | category | flops | bytes accessed | tf_op | source)
XLA Modules:
  0.0 39.2 jit_solution(16489618613500424137)
XLA Ops:
  0.0 1.0 %far.1 = f32[2,50,4,128]{3,2,1,0:T(4,128)S(1)} custom-call(f32[16,8,256]{2,1,0:T(8,128)} %d.3, f32[32,8,256]{2,1,0:T(8,128)} %bitcast.26, f32[2,8,256]{2,1,0:T(8,128)} %w.3), custom_call_target="tpu_custom_call" | custom-call | tf_op jit(solution)/shard_map/far/pallas_call | solution.py:592
  1.0 2.7 %collective-permute-start = (f32[2,200,128]{2,1,0:T(8,128)S(1)}, f32[2,200,128]{2,1,0:T(8,128)S(1)}, u32[]{:S(2)}, u32[]{:S(2)}) collective-permute-start(f32[2,200,128]{2,1,0:T(8,128)S(1)} %bitcast.17), channel_id=1, source_target_pairs={{0,15},{1,2},{2,1},{3,4},{4,3},{5,6},{6,5},{7,8},{8,7},{9,10},{10,... | collective-permute-start | bytes 614408 | tf_op jit(solution)/shard_map/ppermute | solution.py:617
  3.7 0.0 copy-start
  3.7 1.4 %own.1 = (f32[2,16,8,128]{3,2,1,0:T(8,128)S(1)}, f32[2,32,8,128]{3,2,1,0:T(8,128)S(1)}, f32[2,2,8,128]{3,2,1,0:T(8,128)S(1)}, f32[256,128]{1,0:T(8,128)S(1)}, f3...) custom-call(f32[16,8,256]{2,1,0:T(8,128)} %d.3, f32[32,8,256]{2,1,0:T(8,128)} %bitcast.27, ...), custom_call_target="tpu_custom_call" | custom-call | tf_op jit(solution)/shard_map/own/pallas_call | solution.py:601
  5.0 3.0 %collective-permute-start.2 = (f32[200,128]{1,0:T(8,128)S(1)}, f32[200,128]{1,0:T(8,128)S(1)}, u32[]{:S(2)}, u32[]{:S(2)}) collective-permute-start(f32[200,128]{1,0:T(8,128)S(1)} %bitcast.25), channel_id=1, source_target_pairs={{0,1},{1,0},{2,3},{3,2},{4,5},{5,4},{6,7},{7,6},{8,9},{9,8},{10,11... | collective-permute-start | bytes 307208 | tf_op jit(solution)/shard_map/ppermute | solution.py:618
  8.0 0.1 collective-permute-start.1
  8.1 0.9 %collective-permute-done.2.rest_1_.near = f32[200,128]{1,0:T(8,128)S(1)} collective-permute-done((f32[200,128]{1,0:T(8,128)S(1)}, f32[200,128]{1,0:T(8,128)S(1)}, u32[]{:S(2)}, u32[]{:S(2)}) %collective-permute-start.2) | collective-permute-done | bytes 102432 | tf_op jit(solution)/shard_map/ppermute | solution.py:618
  8.9 0.0 copy-done
  8.9 0.1 member.1.own_fm
  9.0 1.2 %collective-permute-start.3 = (f32[16,128]{1,0:T(8,128)S(1)}, f32[16,128]{1,0:T(8,128)S(1)}, u32[]{:S(2)}, u32[]{:S(2)}) collective-permute-start(f32[16,128]{1,0:T(8,128)S(1)} %member.1.own_fm), channel_id=1, source_target_pairs={{0,16},{16,0},{1,17},{17,1},{2,18},{18,2},{3,19},{19,3},{4,20},{20... | collective-permute-start | bytes 24584 | tf_op jit(solution)/shard_map/ppermute | solution.py:627
  10.3 0.0 collective-permute-done.1.rest_0_
  10.3 2.4 %inner.1 = (f32[576,256]{1,0:T(8,128)S(1)}, f32[256,128]{1,0:T(8,128)S(1)}, f32[128,256]{1,0:T(8,128)S(1)}) custom-call(f32[2,128,128]{2,1,0:T(8,128)S(1)} %bitcast.20, f32[2,256,128]{2,1,0:T(8,128)S(1)} %bitcast.13, f32[2,16,128]{2,1,0:T(8,128)S(1)} %bitcast.22, f32[256,128]{1,0:T(8,128)S(1)} %get-tuple-element.18.fy, ...), custom_call_target="tpu_custom_call" | custom-call | tf_op jit(solution)/shard_map/inner/pallas_call | solution.py:629
  12.7 0.0 collective-permute-done.3.other_fm
  12.7 0.0 collective-permute-done.far
  12.7 1.1 %outer.1 = f32[512,128]{1,0:T(8,128)S(1)} custom-call(f32[2,128,128]{2,1,0:T(8,128)S(1)} %bitcast.21, f32[2,256,128]{2,1,0:T(8,128)S(1)} %bitcast.14, f32[2,16,128]{2,1,0:T(8,128)S(1)} %bitcast.23, f32[2,200,128]{2,1,0:T(8,128)S(1)} %collective-permute-done.far, f32[128,256]{1,0:T(8,128)S(1)} %get-tuple-element.21.fy, ...), custom_call_target="tpu_custom_call" | custom-call | tf_op jit(solution)/shard_map/outer/pallas_call | solution.py:641
  13.9 12.7 %all_to_all.10 = f32[32,16,1,128]{3,1,2,0:T(8,128)S(1)} all-to-all(f32[32,16,1,128]{3,1,2,0:T(8,128)S(1)} %bitcast.16), channel_id=1, replica_groups={{0,2,4,6,8,10,12,14,1,3,5,7,9,11,13,15,16,18,20,22,24,26,28,30,17,19,21..., dimensions={0} | all-to-all | bytes 524288 | tf_op jit(solution)/shard_map/all_to_all | solution.py:546
  26.6 0.5 %project.1 = f32[384,128]{1,0:T(8,128)S(1)} custom-call(f32[512,128]{1,0:T(8,128)S(1)} %bitcast.15, f32[16,128]{1,0:T(8,128)S(1)} %member.1.own_fm, f32[16,128]{1,0:T(8,128)S(1)} %collective-permute-done.3.other_fm), custom_call_target="tpu_custom_call" | custom-call | tf_op jit(solution)/shard_map/project/pallas_call | solution.py:653
  27.1 11.1 %all_to_all.11 = f32[32,12,1,128]{3,2,1,0:T(1,128)S(1)} all-to-all(f32[32,12,1,128]{3,2,1,0:T(1,128)S(1)} %bitcast.19), channel_id=1, replica_groups={{0,2,4,6,8,10,12,14,1,3,5,7,9,11,13,15,16,18,20,22,24,26,28,30,17,19,21..., dimensions={0} | all-to-all | bytes 393216 | tf_op jit(solution)/shard_map/all_to_all | solution.py:546
  38.2 1.0 %gather.1 = f32[16,3,8,128]{3,2,1,0:T(8,128)} custom-call(f32[384,128]{1,0:T(8,128)S(1)} %bitcast.18), custom_call_target="tpu_custom_call" | custom-call | tf_op jit(solution)/shard_map/gather/pallas_call | solution.py:661
Async XLA Ops:
  1.0 11.7 %collective-permute-start = (f32[2,200,128]{2,1,0:T(8,128)S(1)}, f32[2,200,128]{2,1,0:T(8,128)S(1)}, u32[]{:S(2)}, u32[]{:S(2)}) collective-permute-start(f32[2,200,128]{2,1,0:T(8,128)S(1)} %bitcast.17), channel_id=1, source_target_pairs={{0,15},{1,2},{2,1},{3,4},{4,3},{5,6},{6,5},{7,8},{8,7},{9,10},{10,... | collective-permute-start | bytes 614408 | tf_op jit(solution)/shard_map/ppermute | solution.py:617
  3.7 5.3 %copy-start = (f32[16,32]{1,0:T(8,128)S(1)}, f32[16,32]{1,0:T(8,128)}, u32[]{:S(2)}) copy-start(f32[16,32]{1,0:T(8,128)} %fm.1) | copy-start | bytes 6148
  5.0 3.9 %collective-permute-start.2 = (f32[200,128]{1,0:T(8,128)S(1)}, f32[200,128]{1,0:T(8,128)S(1)}, u32[]{:S(2)}, u32[]{:S(2)}) collective-permute-start(f32[200,128]{1,0:T(8,128)S(1)} %bitcast.25), channel_id=1, source_target_pairs={{0,1},{1,0},{2,3},{3,2},{4,5},{5,4},{6,7},{7,6},{8,9},{9,8},{10,11... | collective-permute-start | bytes 307208 | tf_op jit(solution)/shard_map/ppermute | solution.py:618
  8.0 2.3 %collective-permute-start.1 = (f32[200,128]{1,0:T(8,128)S(1)}, f32[200,128]{1,0:T(8,128)S(1)}, u32[]{:S(2)}, u32[]{:S(2)}) collective-permute-start(f32[200,128]{1,0:T(8,128)S(1)} %bitcast.24), channel_id=1, source_target_pairs={{0,1},{1,0},{2,3},{3,2},{4,5},{5,4},{6,7},{7,6},{8,9},{9,8},{10,11... | collective-permute-start | bytes 307208 | tf_op jit(solution)/shard_map/ppermute | solution.py:618
  9.0 3.7 %collective-permute-start.3 = (f32[16,128]{1,0:T(8,128)S(1)}, f32[16,128]{1,0:T(8,128)S(1)}, u32[]{:S(2)}, u32[]{:S(2)}) collective-permute-start(f32[16,128]{1,0:T(8,128)S(1)} %member.1.own_fm), channel_id=1, source_target_pairs={{0,16},{16,0},{1,17},{17,1},{2,18},{18,2},{3,19},{19,3},{4,20},{20... | collective-permute-start | bytes 24584 | tf_op jit(solution)/shard_map/ppermute | solution.py:627

commit v10 on v9

--- a/solution.py
+++ b/solution.py
@@ -196,13 +196,14 @@
 
 
 class Strip:
-    def __init__(self, group, own, near, far):
+    def __init__(self, group, own, near, far, width=SUBLANES):
+        self.width = width
         self.rows = own[2].shape[1] // 2
         self.half = self.rows // 2
         self.members = own[0].shape[1] // self.rows
         self.tiles = own[0].shape[0]
         cut = lambda ref: [ref.at[t] for t in range(self.tiles)]
-        self.first, self.own = pl.multiple_of(group * SUBLANES, SUBLANES), tuple(cut(a) for a in own)
+        self.first, self.own = pl.multiple_of(group * width, SUBLANES), tuple(cut(a) for a in own)
         self.near = near
         self.far = None if far is None else cut(far)
         self.odd = lax.rem(lax.axis_index("gx"), 2)
@@ -230,9 +231,9 @@
             d = m = ref
             base = self.members * lines
         first = self.first
-        rho = self.every(d, first * lines + at, SUBLANES, lines)
-        mx = self.every(m, base + first * 2 * lines + at, SUBLANES, 2 * lines)
-        my = self.every(m, base + (first * 2 + 1) * lines + at, SUBLANES, 2 * lines)
+        rho = self.every(d, first * lines + at, self.width, lines)
+        mx = self.every(m, base + first * 2 * lines + at, self.width, 2 * lines)
+        my = self.every(m, base + (first * 2 + 1) * lines + at, self.width, 2 * lines)
         return rho, self.sign * mx, my
 
     def wish(self, x):
@@ -244,12 +245,12 @@
         line = [self.every(ref, base + c * lines + at, 1, 1) for c in range(2)]
         rate = DTIME / RELAX
         line = [(rate * self.sign) * line[0], rate * line[1]]
-        return tuple(jnp.broadcast_to(a, (SUBLANES, a.shape[1])) for a in line)
+        return tuple(jnp.broadcast_to(a, (self.width, a.shape[1])) for a in line)
 
     def keep(self, state, x, q):
         for c, a in enumerate((q[0], self.sign * q[1], q[2])):
             at = (3 * x + c) * self.members + self.first
-            state[pl.ds(at, SUBLANES), :] = a
+            state[pl.ds(at, self.width), :] = a
 
 
 def march(computed, fetch, wish, emit, hook=None, bound=None):
@@ -374,24 +375,23 @@
     half = rows // 2
     members = own_d.shape[1] // rows
     sections = 2 * STEPS
-    for group in range(members // SUBLANES):
-        strip = Strip(group, (own_d, own_m, own_w), None, far)
-
-        @functools.cache
-        def bound(s, x):
-            at = edge_line(s, members) + strip.first
-            a = [edges[pl.ds(at + c * members, SUBLANES), :] for c in range(9)]
-            return dict(q=tuple(a[:3]), f=(a[1], a[3], a[4]), ax=a[5], next=tuple(a[6:]))
-
-        def fetch(s, x):
-            return strip.load(x) if x < half else bound(s, x)["q"]
-
-        def emit(s, x, q):
-            if s == sections:
-                strip.keep(state, x - half, q)
-
-        computed = [range(0)] + [range(s, half + s) for s in range(1, sections + 1)]
-        march(computed, fetch, strip.wish, emit, bound=bound)
+    strip = Strip(0, (own_d, own_m, own_w), None, far, members)
+
+    @functools.cache
+    def bound(s, x):
+        at = edge_line(s, members) + strip.first
+        a = [edges[pl.ds(at + c * members, members), :] for c in range(9)]
+        return dict(q=tuple(a[:3]), f=(a[1], a[3], a[4]), ax=a[5], next=tuple(a[6:]))
+
+    def fetch(s, x):
+        return strip.load(x) if x < half else bound(s, x)["q"]
+
+    def emit(s, x, q):
+        if s == sections:
+            strip.keep(state, x - half, q)
+
+    computed = [range(0)] + [range(s, half + s) for s in range(1, sections + 1)]
+    march(computed, fetch, strip.wish, emit, bound=bound)
 
     devices = 2 * n_gx
     height = out.shape[0] // devices

time: 39.7 us -> 39.7 us (level)
  no operation moved by 1% of the time
where the time goes in v10:
time: 39.7 us; the launch traced here: 39.2 us
  blocking collectives  23.8 us (60%)
  Pallas kernels  7.52 us (19%)
  starting transfers between devices  6.95 us (18%)
  waiting for transfers between devices  0.88 us (2%)
    all_to_all x2, blocking collectives, exchange(): lax.all_to_all(block, ('mem', 'gx'), split_axis=0, concat_axis=0, axis_in...  23.8 us
    ppermute x2, starting transfers between devices, on_device(): lax.ppermute(a, 'gx', [(i, i ^ 1) for i in range(n_gx)])  3.04 us
    ppermute x1, starting transfers between devices, on_device(): lax.ppermute(far, 'gx', [(i, (i - 1 + i % 2 * 2) % n_gx) for i in range(n...  2.67 us
    pallas_call x1, Pallas kernels, on_device(): pl.pallas_call(inner_kernel, out_shape=[shape(sections * 9 * members, cel...  2.43 us
    pallas_call x1, Pallas kernels, on_device(): pl.pallas_call(own_kernel, out_shape=[shape(tiles, n, rows, LANES) for n...  1.36 us
    ppermute x1, starting transfers between devices, on_device(): other_fm = lax.ppermute(own_fm, 'mem', [(0, 1), (1, 0)])  1.24 us
    pallas_call x1, Pallas kernels, on_device(): pl.pallas_call(functools.partial(outer_kernel, n_gx), out_shape=shape(dev...  1.15 us
    pallas_call x1, Pallas kernels, on_device(): pl.pallas_call(functools.partial(gather_kernel, shares, lows), out_shape=...  0.99 us
  transfers between devices with their start and end apart: 4, of which 1 were waited for; matrix products, arithmetic and copies ran while one was open for 0% of the time, Pallas kernels for 10%

profile of v10, /device:TPU:1, one launch (start us, length us, event | category | flops | bytes accessed | tf_op | source)
XLA Modules:
  0.0 39.2 jit_solution(12286604854050360895)
XLA Ops:
  0.0 1.0 %far.1 = f32[2,50,4,128]{3,2,1,0:T(4,128)S(1)} custom-call(f32[16,8,256]{2,1,0:T(8,128)} %d.3, f32[32,8,256]{2,1,0:T(8,128)} %bitcast.26, f32[2,8,256]{2,1,0:T(8,128)} %w.3), custom_call_target="tpu_custom_call" | custom-call | tf_op jit(solution)/shard_map/far/pallas_call | solution.py:592
  1.0 2.7 %collective-permute-start = (f32[2,200,128]{2,1,0:T(8,128)S(1)}, f32[2,200,128]{2,1,0:T(8,128)S(1)}, u32[]{:S(2)}, u32[]{:S(2)}) collective-permute-start(f32[2,200,128]{2,1,0:T(8,128)S(1)} %bitcast.17), channel_id=1, source_target_pairs={{0,15},{1,2},{2,1},{3,4},{4,3},{5,6},{6,5},{7,8},{8,7},{9,10},{10,... | collective-permute-start | bytes 614408 | tf_op jit(solution)/shard_map/ppermute | solution.py:617
  3.7 0.0 copy-start
  3.7 1.4 %own.1 = (f32[2,16,8,128]{3,2,1,0:T(8,128)S(1)}, f32[2,32,8,128]{3,2,1,0:T(8,128)S(1)}, f32[2,2,8,128]{3,2,1,0:T(8,128)S(1)}, f32[256,128]{1,0:T(8,128)S(1)}, f3...) custom-call(f32[16,8,256]{2,1,0:T(8,128)} %d.3, f32[32,8,256]{2,1,0:T(8,128)} %bitcast.27, ...), custom_call_target="tpu_custom_call" | custom-call | tf_op jit(solution)/shard_map/own/pallas_call | solution.py:601
  5.0 3.0 %collective-permute-start.2 = (f32[200,128]{1,0:T(8,128)S(1)}, f32[200,128]{1,0:T(8,128)S(1)}, u32[]{:S(2)}, u32[]{:S(2)}) collective-permute-start(f32[200,128]{1,0:T(8,128)S(1)} %bitcast.25), channel_id=1, source_target_pairs={{0,1},{1,0},{2,3},{3,2},{4,5},{5,4},{6,7},{7,6},{8,9},{9,8},{10,11... | collective-permute-start | bytes 307208 | tf_op jit(solution)/shard_map/ppermute | solution.py:618
  8.0 0.1 collective-permute-start.1
  8.1 0.9 %collective-permute-done.2.rest_1_.near = f32[200,128]{1,0:T(8,128)S(1)} collective-permute-done((f32[200,128]{1,0:T(8,128)S(1)}, f32[200,128]{1,0:T(8,128)S(1)}, u32[]{:S(2)}, u32[]{:S(2)}) %collective-permute-start.2) | collective-permute-done | bytes 102432 | tf_op jit(solution)/shard_map/ppermute | solution.py:618
  8.9 0.0 copy-done
  8.9 0.1 member.1.own_fm
  9.0 1.2 %collective-permute-start.3 = (f32[16,128]{1,0:T(8,128)S(1)}, f32[16,128]{1,0:T(8,128)S(1)}, u32[]{:S(2)}, u32[]{:S(2)}) collective-permute-start(f32[16,128]{1,0:T(8,128)S(1)} %member.1.own_fm), channel_id=1, source_target_pairs={{0,16},{16,0},{1,17},{17,1},{2,18},{18,2},{3,19},{19,3},{4,20},{20... | collective-permute-start | bytes 24584 | tf_op jit(solution)/shard_map/ppermute | solution.py:627
  10.3 0.0 collective-permute-done.1.rest_0_
  10.3 2.4 %inner.1 = (f32[576,256]{1,0:T(8,128)S(1)}, f32[256,128]{1,0:T(8,128)S(1)}, f32[128,256]{1,0:T(8,128)S(1)}) custom-call(f32[2,128,128]{2,1,0:T(8,128)S(1)} %bitcast.20, f32[2,256,128]{2,1,0:T(8,128)S(1)} %bitcast.13, f32[2,16,128]{2,1,0:T(8,128)S(1)} %bitcast.22, f32[256,128]{1,0:T(8,128)S(1)} %get-tuple-element.18.fy, ...), custom_call_target="tpu_custom_call" | custom-call | tf_op jit(solution)/shard_map/inner/pallas_call | solution.py:629
  12.7 0.0 collective-permute-done.3.other_fm
  12.7 0.0 collective-permute-done.far
  12.7 1.1 %outer.1 = f32[512,128]{1,0:T(8,128)S(1)} custom-call(f32[2,128,128]{2,1,0:T(8,128)S(1)} %bitcast.21, f32[2,256,128]{2,1,0:T(8,128)S(1)} %bitcast.14, f32[2,16,128]{2,1,0:T(8,128)S(1)} %bitcast.23, f32[2,200,128]{2,1,0:T(8,128)S(1)} %collective-permute-done.far, f32[128,256]{1,0:T(8,128)S(1)} %get-tuple-element.21.fy, ...), custom_call_target="tpu_custom_call" | custom-call | tf_op jit(solution)/shard_map/outer/pallas_call | solution.py:641
  13.9 12.7 %all_to_all.10 = f32[32,16,1,128]{3,1,2,0:T(8,128)S(1)} all-to-all(f32[32,16,1,128]{3,1,2,0:T(8,128)S(1)} %bitcast.16), channel_id=1, replica_groups={{0,2,4,6,8,10,12,14,1,3,5,7,9,11,13,15,16,18,20,22,24,26,28,30,17,19,21..., dimensions={0} | all-to-all | bytes 524288 | tf_op jit(solution)/shard_map/all_to_all | solution.py:546
  26.6 0.5 %project.1 = f32[384,128]{1,0:T(8,128)S(1)} custom-call(f32[512,128]{1,0:T(8,128)S(1)} %bitcast.15, f32[16,128]{1,0:T(8,128)S(1)} %member.1.own_fm, f32[16,128]{1,0:T(8,128)S(1)} %collective-permute-done.3.other_fm), custom_call_target="tpu_custom_call" | custom-call | tf_op jit(solution)/shard_map/project/pallas_call | solution.py:653
  27.1 11.1 %all_to_all.11 = f32[32,12,1,128]{3,2,1,0:T(1,128)S(1)} all-to-all(f32[32,12,1,128]{3,2,1,0:T(1,128)S(1)} %bitcast.19), channel_id=1, replica_groups={{0,2,4,6,8,10,12,14,1,3,5,7,9,11,13,15,16,18,20,22,24,26,28,30,17,19,21..., dimensions={0} | all-to-all | bytes 393216 | tf_op jit(solution)/shard_map/all_to_all | solution.py:546
  38.2 1.0 %gather.1 = f32[16,3,8,128]{3,2,1,0:T(8,128)} custom-call(f32[384,128]{1,0:T(8,128)S(1)} %bitcast.18), custom_call_target="tpu_custom_call" | custom-call | tf_op jit(solution)/shard_map/gather/pallas_call | solution.py:661
Async XLA Ops:
  1.0 11.7 %collective-permute-start = (f32[2,200,128]{2,1,0:T(8,128)S(1)}, f32[2,200,128]{2,1,0:T(8,128)S(1)}, u32[]{:S(2)}, u32[]{:S(2)}) collective-permute-start(f32[2,200,128]{2,1,0:T(8,128)S(1)} %bitcast.17), channel_id=1, source_target_pairs={{0,15},{1,2},{2,1},{3,4},{4,3},{5,6},{6,5},{7,8},{8,7},{9,10},{10,... | collective-permute-start | bytes 614408 | tf_op jit(solution)/shard_map/ppermute | solution.py:617
  3.7 5.3 %copy-start = (f32[16,32]{1,0:T(8,128)S(1)}, f32[16,32]{1,0:T(8,128)}, u32[]{:S(2)}) copy-start(f32[16,32]{1,0:T(8,128)} %fm.1) | copy-start | bytes 6148
  5.0 3.9 %collective-permute-start.2 = (f32[200,128]{1,0:T(8,128)S(1)}, f32[200,128]{1,0:T(8,128)S(1)}, u32[]{:S(2)}, u32[]{:S(2)}) collective-permute-start(f32[200,128]{1,0:T(8,128)S(1)} %bitcast.25), channel_id=1, source_target_pairs={{0,1},{1,0},{2,3},{3,2},{4,5},{5,4},{6,7},{7,6},{8,9},{9,8},{10,11... | collective-permute-start | bytes 307208 | tf_op jit(solution)/shard_map/ppermute | solution.py:618
  8.0 2.3 %collective-permute-start.1 = (f32[200,128]{1,0:T(8,128)S(1)}, f32[200,128]{1,0:T(8,128)S(1)}, u32[]{:S(2)}, u32[]{:S(2)}) collective-permute-start(f32[200,128]{1,0:T(8,128)S(1)} %bitcast.24), channel_id=1, source_target_pairs={{0,1},{1,0},{2,3},{3,2},{4,5},{5,4},{6,7},{7,6},{8,9},{9,8},{10,11... | collective-permute-start | bytes 307208 | tf_op jit(solution)/shard_map/ppermute | solution.py:618
  9.0 3.7 %collective-permute-start.3 = (f32[16,128]{1,0:T(8,128)S(1)}, f32[16,128]{1,0:T(8,128)S(1)}, u32[]{:S(2)}, u32[]{:S(2)}) collective-permute-start(f32[16,128]{1,0:T(8,128)S(1)} %member.1.own_fm), channel_id=1, source_target_pairs={{0,16},{16,0},{1,17},{17,1},{2,18},{18,2},{3,19},{19,3},{4,20},{20... | collective-permute-start | bytes 24584 | tf_op jit(solution)/shard_map/ppermute | solution.py:627

commit v11 on v10

--- a/solution.py
+++ b/solution.py
@@ -176,22 +176,27 @@
         copy.wait()
 
 
-def own_kernel(d, m, w, fy, fx, far, own_d, own_m, own_w, own_fy, own_fx, near, half_sems, sems):
+def near_kernel(d, m, w, far, *rest):
+    *near, sems = rest
+    odd = lax.rem(lax.axis_index("gx"), 2)
+    for copy in half_copies((d, m, w), near, odd, 0, sems):
+        copy.wait()
+
+
+def own_kernel(d, m, w, fy, fx, near, own_d, own_m, own_w, own_fy, own_fx, sems):
     tiles = own_d.shape[0]
-    odd = lax.rem(lax.axis_index("gx"), 2)
-    copies = half_copies((d, m, w), near, odd, 0, half_sems)
-    wholes = []
+    pairs = []
     for whole, cut in ((d, own_d), (m, own_m), (w, own_w)):
         for t in range(tiles):
-            wholes.append((whole.at[:, :, pl.ds(t * LANES, LANES)], cut.at[t]))
-    wholes += [(fy, own_fy), (fx, own_fx)]
-    wholes = [
+            pairs.append((whole.at[:, :, pl.ds(t * LANES, LANES)], cut.at[t]))
+    pairs += [(fy, own_fy), (fx, own_fx)]
+    copies = [
         pltpu.make_async_copy(source, target, sems.at[i])
-        for i, (source, target) in enumerate(wholes)
+        for i, (source, target) in enumerate(pairs)
     ]
-    for copy in wholes:
+    for copy in copies:
         copy.start()
-    for copy in copies + wholes:
+    for copy in copies:
         copy.wait()
 
 
@@ -329,7 +334,7 @@
     return firsts, thirds
 
 
-def member_kernel(near, fm, out):
+def member_kernel(near, own_w, fm, out):
     out[...] = jnp.concatenate([fm[...]] * (LANES // fm.shape[1]), axis=1)
 
 
@@ -598,19 +603,25 @@
         compiler_params=params,
         name="far",
     )(*held(*own))
-    *own, fy, fx, near = pl.pallas_call(
+    near = pl.pallas_call(
+        near_kernel,
+        out_shape=[shape(*packed)] * tiles,
+        in_specs=[anywhere] * 4,
+        out_specs=[vmem] * tiles,
+        scratch_shapes=[pltpu.SemaphoreType.DMA((3 * tiles,))],
+        compiler_params=params,
+        name="near",
+    )(*held(*own), far)
+    *own, fy, fx = pl.pallas_call(
         own_kernel,
         out_shape=[shape(tiles, n, rows, LANES) for n in lines]
-        + [shape(*factor_y.shape), shape(*factor_x.shape), [shape(*packed)] * tiles],
+        + [shape(*factor_y.shape), shape(*factor_x.shape)],
         in_specs=[anywhere] * 6,
-        out_specs=[vmem] * 5 + [[vmem] * tiles],
-        scratch_shapes=[
-            pltpu.SemaphoreType.DMA((3 * tiles,)),
-            pltpu.SemaphoreType.DMA((3 * tiles + 2,)),
-        ],
+        out_specs=[vmem] * 5,
+        scratch_shapes=[pltpu.SemaphoreType.DMA((3 * tiles + 2,))],
         compiler_params=params,
         name="own",
-    )(*held(*own, factor_y, factor_x), far)
+    )(*held(*own, factor_y, factor_x), near[-1])
     own = [a.reshape(tiles, -1, LANES) for a in own]
     far = far.reshape(tiles, -1, LANES)
     near = [a.reshape(-1, LANES) for a in near]
@@ -619,11 +630,11 @@
     own_fm = pl.pallas_call(
         member_kernel,
         out_shape=shape(members, LANES),
-        in_specs=[anywhere, vmem],
+        in_specs=[anywhere, anywhere, vmem],
         out_specs=vmem,
         compiler_params=params,
         name="member",
-    )(near[-1], factor_m)
+    )(near[-1], own[-1], factor_m)
     other_fm = lax.ppermute(own_fm, "mem", [(0, 1), (1, 0)])
     sections = 2 * STEPS
     edges, early, turned_fy = pl.pallas_call(

time: 39.7 us -> 39.8 us (level)
  waiting for transfers between devices: 0.88 us -> 0.01 us
  Pallas kernels: 7.52 us -> 8.36 us
    pallas_call x0 -> x1, Pallas kernels: none -> 0.98 us  [on_device(): pl.pallas_call(near_kernel, out_shape=[shape(*packed)] * tiles, in_specs=...]
    ppermute x2, waiting for transfers between devices: 0.87 us -> 0.01 us  [on_device(): lax.ppermute(a, 'gx', [(i, i ^ 1) for i in range(n_gx)])]
  transfers between devices with their start and end apart: 4 -> 4, of which waited for: 1 -> 0; matrix products, arithmetic and copies ran while one was open for 0% -> 0% of each run, Pallas kernels for 10% -> 12%
where the time goes in v11:
time: 39.8 us; the launch traced here: 39.2 us
  blocking collectives  23.8 us (60%)
  Pallas kernels  8.36 us (21%)
  starting transfers between devices  6.93 us (17%)
    all_to_all x2, blocking collectives, exchange(): lax.all_to_all(block, ('mem', 'gx'), split_axis=0, concat_axis=0, axis_in...  23.8 us
    ppermute x2, starting transfers between devices, on_device(): lax.ppermute(a, 'gx', [(i, i ^ 1) for i in range(n_gx)])  3.02 us
    ppermute x1, starting transfers between devices, on_device(): lax.ppermute(far, 'gx', [(i, (i - 1 + i % 2 * 2) % n_gx) for i in range(n...  2.67 us
    pallas_call x1, Pallas kernels, on_device(): pl.pallas_call(inner_kernel, out_shape=[shape(sections * 9 * members, cel...  2.43 us
    ppermute x1, starting transfers between devices, on_device(): other_fm = lax.ppermute(own_fm, 'mem', [(0, 1), (1, 0)])  1.25 us
    pallas_call x1, Pallas kernels, on_device(): pl.pallas_call(own_kernel, out_shape=[shape(tiles, n, rows, LANES) for n...  1.21 us
    pallas_call x1, Pallas kernels, on_device(): pl.pallas_call(functools.partial(outer_kernel, n_gx), out_shape=shape(dev...  1.15 us
    pallas_call x1, Pallas kernels, on_device(): pl.pallas_call(functools.partial(gather_kernel, shares, lows), out_shape=...  0.99 us
  transfers between devices with their start and end apart: 4, of which 0 were waited for; matrix products, arithmetic and copies ran while one was open for 0% of the time, Pallas kernels for 12%

profile of v11, /device:TPU:1, one launch (start us, length us, event | category | flops | bytes accessed | tf_op | source)
XLA Modules:
  0.0 39.2 jit_solution(5612117538349026354)
XLA Ops:
  0.0 1.0 %far.1 = f32[2,50,4,128]{3,2,1,0:T(4,128)S(1)} custom-call(f32[16,8,256]{2,1,0:T(8,128)} %d.5, f32[32,8,256]{2,1,0:T(8,128)} %bitcast.27, f32[2,8,256]{2,1,0:T(8,128)} %w.5), custom_call_target="tpu_custom_call" | custom-call | tf_op jit(solution)/shard_map/far/pallas_call | solution.py:597
  1.0 2.7 %collective-permute-start = (f32[2,200,128]{2,1,0:T(8,128)S(1)}, f32[2,200,128]{2,1,0:T(8,128)S(1)}, u32[]{:S(2)}, u32[]{:S(2)}) collective-permute-start(f32[2,200,128]{2,1,0:T(8,128)S(1)} %bitcast.17), channel_id=1, source_target_pairs={{0,15},{1,2},{2,1},{3,4},{4,3},{5,6},{6,5},{7,8},{8,7},{9,10},{10,... | collective-permute-start | bytes 614408 | tf_op jit(solution)/shard_map/ppermute | solution.py:628
  3.7 1.0 %near.1 = (f32[50,4,128]{2,1,0:T(4,128)S(1)}, f32[50,4,128]{2,1,0:T(4,128)S(1)}) custom-call(f32[16,8,256]{2,1,0:T(8,128)} %d.5, f32[32,8,256]{2,1,0:T(8,128)} %bitcast.28, f32[2,8,256]{2,1,0:T(8,128)} %w.5, f32[2,50,4,128]{3,2,1,0:T(4,128)S(1)} %far.1), custom_call_target="tpu_custom_call" | custom-call | tf_op jit(solution)/shard_map/near/pallas_call | solution.py:606
  4.6 2.9 %collective-permute-start.2 = (f32[200,128]{1,0:T(8,128)S(1)}, f32[200,128]{1,0:T(8,128)S(1)}, u32[]{:S(2)}, u32[]{:S(2)}) collective-permute-start(f32[200,128]{1,0:T(8,128)S(1)} %bitcast.25), channel_id=1, source_target_pairs={{0,1},{1,0},{2,3},{3,2},{4,5},{5,4},{6,7},{7,6},{8,9},{9,8},{10,11... | collective-permute-start | bytes 307208 | tf_op jit(solution)/shard_map/ppermute | solution.py:629
  7.6 0.1 collective-permute-start.1
  7.7 0.0 copy-start
  7.7 1.2 %own.1 = (f32[2,16,8,128]{3,2,1,0:T(8,128)S(1)}, f32[2,32,8,128]{3,2,1,0:T(8,128)S(1)}, f32[2,2,8,128]{3,2,1,0:T(8,128)S(1)}, f32[256,128]{1,0:T(8,128)S(1)}, f32[8,128]{1,0:T(8,128)S(1)}) custom-call(f32[16,8,256]{2,1,0:T(8,128)} %d.5, f32[32,8,256]{2,1,0:T(8,128)} %bitcast.29, f32[2,8,256]{2,1,0:T(8,128)} %w.5, f32[256,128]{1,0:T(8,128)} %fy.1, ...), custom_call_target="tpu_custom_call" | custom-call | tf_op jit(solution)/shard_map/own/pallas_call | solution.py:615
  8.9 0.0 collective-permute-done.2.rest_1_.near
  8.9 0.0 copy-done
  8.9 0.1 member.1.own_fm
  9.0 1.2 %collective-permute-start.3 = (f32[16,128]{1,0:T(8,128)S(1)}, f32[16,128]{1,0:T(8,128)S(1)}, u32[]{:S(2)}, u32[]{:S(2)}) collective-permute-start(f32[16,128]{1,0:T(8,128)S(1)} %member.1.own_fm), channel_id=1, source_target_pairs={{0,16},{16,0},{1,17},{17,1},{2,18},{18,2},{3,19},{19,3},{4,20},{20... | collective-permute-start | bytes 24584 | tf_op jit(solution)/shard_map/ppermute | solution.py:638
  10.2 0.0 collective-permute-done.1.rest_0_
  10.2 2.4 %inner.1 = (f32[576,256]{1,0:T(8,128)S(1)}, f32[256,128]{1,0:T(8,128)S(1)}, f32[128,256]{1,0:T(8,128)S(1)}) custom-call(f32[2,128,128]{2,1,0:T(8,128)S(1)} %bitcast.20, f32[2,256,128]{2,1,0:T(8,128)S(1)} %bitcast.13, f32[2,16,128]{2,1,0:T(8,128)S(1)} %bitcast.23, f32[256,128]{1,0:T(8,128)S(1)} %get-tuple-element.19.fy, ...), custom_call_target="tpu_custom_call" | custom-call | tf_op jit(solution)/shard_map/inner/pallas_call | solution.py:640
  12.7 0.0 collective-permute-done.3.other_fm
  12.7 0.0 collective-permute-done.far
  12.7 1.1 %outer.1 = f32[512,128]{1,0:T(8,128)S(1)} custom-call(f32[2,128,128]{2,1,0:T(8,128)S(1)} %bitcast.21, f32[2,256,128]{2,1,0:T(8,128)S(1)} %bitcast.14, f32[2,16,128]{2,1,0:T(8,128)S(1)} %bitcast.24, f32[2,200,128]{2,1,0:T(8,128)S(1)} %collective-permute-done.far, f32[128,256]{1,0:T(8,128)S(1)} %get-tuple-element.21.fy, ...), custom_call_target="tpu_custom_call" | custom-call | tf_op jit(solution)/shard_map/outer/pallas_call | solution.py:652
  13.8 12.7 %all_to_all.10 = f32[32,16,1,128]{3,1,2,0:T(8,128)S(1)} all-to-all(f32[32,16,1,128]{3,1,2,0:T(8,128)S(1)} %bitcast.16), channel_id=1, replica_groups={{0,2,4,6,8,10,12,14,1,3,5,7,9,11,13,15,16,18,20,22,24,26,28,30,17,19,21..., dimensions={0} | all-to-all | bytes 524288 | tf_op jit(solution)/shard_map/all_to_all | solution.py:551
  26.6 0.5 %project.1 = f32[384,128]{1,0:T(8,128)S(1)} custom-call(f32[512,128]{1,0:T(8,128)S(1)} %bitcast.15, f32[16,128]{1,0:T(8,128)S(1)} %member.1.own_fm, f32[16,128]{1,0:T(8,128)S(1)} %collective-permute-done.3.other_fm), custom_call_target="tpu_custom_call" | custom-call | tf_op jit(solution)/shard_map/project/pallas_call | solution.py:664
  27.1 11.1 %all_to_all.11 = f32[32,12,1,128]{3,2,1,0:T(1,128)S(1)} all-to-all(f32[32,12,1,128]{3,2,1,0:T(1,128)S(1)} %bitcast.19), channel_id=1, replica_groups={{0,2,4,6,8,10,12,14,1,3,5,7,9,11,13,15,16,18,20,22,24,26,28,30,17,19,21..., dimensions={0} | all-to-all | bytes 393216 | tf_op jit(solution)/shard_map/all_to_all | solution.py:551
  38.2 1.0 %gather.1 = f32[16,3,8,128]{3,2,1,0:T(8,128)} custom-call(f32[384,128]{1,0:T(8,128)S(1)} %bitcast.18), custom_call_target="tpu_custom_call" | custom-call | tf_op jit(solution)/shard_map/gather/pallas_call | solution.py:672
Async XLA Ops:
  1.0 11.7 %collective-permute-start = (f32[2,200,128]{2,1,0:T(8,128)S(1)}, f32[2,200,128]{2,1,0:T(8,128)S(1)}, u32[]{:S(2)}, u32[]{:S(2)}) collective-permute-start(f32[2,200,128]{2,1,0:T(8,128)S(1)} %bitcast.17), channel_id=1, source_target_pairs={{0,15},{1,2},{2,1},{3,4},{4,3},{5,6},{6,5},{7,8},{8,7},{9,10},{10,... | collective-permute-start | bytes 614408 | tf_op jit(solution)/shard_map/ppermute | solution.py:628
  4.6 4.2 %collective-permute-start.2 = (f32[200,128]{1,0:T(8,128)S(1)}, f32[200,128]{1,0:T(8,128)S(1)}, u32[]{:S(2)}, u32[]{:S(2)}) collective-permute-start(f32[200,128]{1,0:T(8,128)S(1)} %bitcast.25), channel_id=1, source_target_pairs={{0,1},{1,0},{2,3},{3,2},{4,5},{5,4},{6,7},{7,6},{8,9},{9,8},{10,11... | collective-permute-start | bytes 307208 | tf_op jit(solution)/shard_map/ppermute | solution.py:629
  7.6 2.6 %collective-permute-start.1 = (f32[200,128]{1,0:T(8,128)S(1)}, f32[200,128]{1,0:T(8,128)S(1)}, u32[]{:S(2)}, u32[]{:S(2)}) collective-permute-start(f32[200,128]{1,0:T(8,128)S(1)} %bitcast.26), channel_id=1, source_target_pairs={{0,1},{1,0},{2,3},{3,2},{4,5},{5,4},{6,7},{7,6},{8,9},{9,8},{10,11... | collective-permute-start | bytes 307208 | tf_op jit(solution)/shard_map/ppermute | solution.py:629
  7.7 1.2 %copy-start = (f32[16,32]{1,0:T(8,128)S(1)}, f32[16,32]{1,0:T(8,128)}, u32[]{:S(2)}) copy-start(f32[16,32]{1,0:T(8,128)} %fm.1) | copy-start | bytes 6148
  9.0 3.7 %collective-permute-start.3 = (f32[16,128]{1,0:T(8,128)S(1)}, f32[16,128]{1,0:T(8,128)S(1)}, u32[]{:S(2)}, u32[]{:S(2)}) collective-permute-start(f32[16,128]{1,0:T(8,128)S(1)} %member.1.own_fm), channel_id=1, source_target_pairs={{0,16},{16,0},{1,17},{17,1},{2,18},{18,2},{3,19},{19,3},{4,20},{20... | collective-permute-start | bytes 24584 | tf_op jit(solution)/shard_map/ppermute | solution.py:638

commit v12 on v10

--- a/solution.py
+++ b/solution.py
@@ -481,10 +481,9 @@
     both = product(turned_fx, jnp.concatenate([firsts, thirds], axis=1))
     firsts = product(both[:, : 2 * LANES], diagonal)
     thirds = product(both[:, 2 * LANES :], small)
-    core = jnp.concatenate([firsts[:, :LANES], thirds, firsts[:, LANES:]], axis=1)
     high = out.shape[0] // devices
-    for t in range(3):
-        tall[t] = core[:, t * LANES : (t + 1) * LANES]
+    for t, part in enumerate((firsts[:, :LANES], thirds, firsts[:, LANES:])):
+        tall[t] = part
     pairs = n_gx // 2
     lane = lax.broadcasted_iota(jnp.int32, (pairs, LANES), 1)
     for odd in range(2):

time: 39.7 us -> 39.7 us (level)
  no operation moved by 1% of the time
where the time goes in v12:
time: 39.7 us; the launch traced here: 39.2 us
  blocking collectives  23.8 us (60%)
  Pallas kernels  7.52 us (19%)
  starting transfers between devices  6.95 us (18%)
  waiting for transfers between devices  0.88 us (2%)
    all_to_all x2, blocking collectives, exchange(): lax.all_to_all(block, ('mem', 'gx'), split_axis=0, concat_axis=0, axis_in...  23.8 us
    ppermute x2, starting transfers between devices, on_device(): lax.ppermute(a, 'gx', [(i, i ^ 1) for i in range(n_gx)])  3.04 us
    ppermute x1, starting transfers between devices, on_device(): lax.ppermute(far, 'gx', [(i, (i - 1 + i % 2 * 2) % n_gx) for i in range(n...  2.67 us
    pallas_call x1, Pallas kernels, on_device(): pl.pallas_call(inner_kernel, out_shape=[shape(sections * 9 * members, cel...  2.43 us
    pallas_call x1, Pallas kernels, on_device(): pl.pallas_call(own_kernel, out_shape=[shape(tiles, n, rows, LANES) for n...  1.36 us
    ppermute x1, starting transfers between devices, on_device(): other_fm = lax.ppermute(own_fm, 'mem', [(0, 1), (1, 0)])  1.24 us
    pallas_call x1, Pallas kernels, on_device(): pl.pallas_call(functools.partial(outer_kernel, n_gx), out_shape=shape(dev...  1.15 us
    pallas_call x1, Pallas kernels, on_device(): pl.pallas_call(functools.partial(gather_kernel, shares, lows), out_shape=...  0.99 us
  transfers between devices with their start and end apart: 4, of which 1 were waited for; matrix products, arithmetic and copies ran while one was open for 0% of the time, Pallas kernels for 10%

profile of v12, /device:TPU:1, one launch (start us, length us, event | category | flops | bytes accessed | tf_op | source)
XLA Modules:
  0.0 39.2 jit_solution(12286604854050360895)
XLA Ops:
  0.0 1.0 %far.1 = f32[2,50,4,128]{3,2,1,0:T(4,128)S(1)} custom-call(f32[16,8,256]{2,1,0:T(8,128)} %d.3, f32[32,8,256]{2,1,0:T(8,128)} %bitcast.26, f32[2,8,256]{2,1,0:T(8,128)} %w.3), custom_call_target="tpu_custom_call" | custom-call | tf_op jit(solution)/shard_map/far/pallas_call | solution.py:591
  1.0 2.7 %collective-permute-start = (f32[2,200,128]{2,1,0:T(8,128)S(1)}, f32[2,200,128]{2,1,0:T(8,128)S(1)}, u32[]{:S(2)}, u32[]{:S(2)}) collective-permute-start(f32[2,200,128]{2,1,0:T(8,128)S(1)} %bitcast.17), channel_id=1, source_target_pairs={{0,15},{1,2},{2,1},{3,4},{4,3},{5,6},{6,5},{7,8},{8,7},{9,10},{10,... | collective-permute-start | bytes 614408 | tf_op jit(solution)/shard_map/ppermute | solution.py:616
  3.7 0.0 copy-start
  3.7 1.4 %own.1 = (f32[2,16,8,128]{3,2,1,0:T(8,128)S(1)}, f32[2,32,8,128]{3,2,1,0:T(8,128)S(1)}, f32[2,2,8,128]{3,2,1,0:T(8,128)S(1)}, f32[256,128]{1,0:T(8,128)S(1)}, f3...) custom-call(f32[16,8,256]{2,1,0:T(8,128)} %d.3, f32[32,8,256]{2,1,0:T(8,128)} %bitcast.27, ...), custom_call_target="tpu_custom_call" | custom-call | tf_op jit(solution)/shard_map/own/pallas_call | solution.py:600
  5.0 3.0 %collective-permute-start.2 = (f32[200,128]{1,0:T(8,128)S(1)}, f32[200,128]{1,0:T(8,128)S(1)}, u32[]{:S(2)}, u32[]{:S(2)}) collective-permute-start(f32[200,128]{1,0:T(8,128)S(1)} %bitcast.25), channel_id=1, source_target_pairs={{0,1},{1,0},{2,3},{3,2},{4,5},{5,4},{6,7},{7,6},{8,9},{9,8},{10,11... | collective-permute-start | bytes 307208 | tf_op jit(solution)/shard_map/ppermute | solution.py:617
  8.0 0.1 collective-permute-start.1
  8.1 0.9 %collective-permute-done.2.rest_1_.near = f32[200,128]{1,0:T(8,128)S(1)} collective-permute-done((f32[200,128]{1,0:T(8,128)S(1)}, f32[200,128]{1,0:T(8,128)S(1)}, u32[]{:S(2)}, u32[]{:S(2)}) %collective-permute-start.2) | collective-permute-done | bytes 102432 | tf_op jit(solution)/shard_map/ppermute | solution.py:617
  8.9 0.0 copy-done
  8.9 0.1 member.1.own_fm
  9.0 1.2 %collective-permute-start.3 = (f32[16,128]{1,0:T(8,128)S(1)}, f32[16,128]{1,0:T(8,128)S(1)}, u32[]{:S(2)}, u32[]{:S(2)}) collective-permute-start(f32[16,128]{1,0:T(8,128)S(1)} %member.1.own_fm), channel_id=1, source_target_pairs={{0,16},{16,0},{1,17},{17,1},{2,18},{18,2},{3,19},{19,3},{4,20},{20... | collective-permute-start | bytes 24584 | tf_op jit(solution)/shard_map/ppermute | solution.py:626
  10.3 0.0 collective-permute-done.1.rest_0_
  10.3 2.4 %inner.1 = (f32[576,256]{1,0:T(8,128)S(1)}, f32[256,128]{1,0:T(8,128)S(1)}, f32[128,256]{1,0:T(8,128)S(1)}) custom-call(f32[2,128,128]{2,1,0:T(8,128)S(1)} %bitcast.20, f32[2,256,128]{2,1,0:T(8,128)S(1)} %bitcast.13, f32[2,16,128]{2,1,0:T(8,128)S(1)} %bitcast.22, f32[256,128]{1,0:T(8,128)S(1)} %get-tuple-element.18.fy, ...), custom_call_target="tpu_custom_call" | custom-call | tf_op jit(solution)/shard_map/inner/pallas_call | solution.py:628
  12.7 0.0 collective-permute-done.3.other_fm
  12.7 0.0 collective-permute-done.far
  12.7 1.1 %outer.1 = f32[512,128]{1,0:T(8,128)S(1)} custom-call(f32[2,128,128]{2,1,0:T(8,128)S(1)} %bitcast.21, f32[2,256,128]{2,1,0:T(8,128)S(1)} %bitcast.14, f32[2,16,128]{2,1,0:T(8,128)S(1)} %bitcast.23, f32[2,200,128]{2,1,0:T(8,128)S(1)} %collective-permute-done.far, f32[128,256]{1,0:T(8,128)S(1)} %get-tuple-element.21.fy, ...), custom_call_target="tpu_custom_call" | custom-call | tf_op jit(solution)/shard_map/outer/pallas_call | solution.py:640
  13.9 12.7 %all_to_all.10 = f32[32,16,1,128]{3,1,2,0:T(8,128)S(1)} all-to-all(f32[32,16,1,128]{3,1,2,0:T(8,128)S(1)} %bitcast.16), channel_id=1, replica_groups={{0,2,4,6,8,10,12,14,1,3,5,7,9,11,13,15,16,18,20,22,24,26,28,30,17,19,21..., dimensions={0} | all-to-all | bytes 524288 | tf_op jit(solution)/shard_map/all_to_all | solution.py:545
  26.6 0.5 %project.1 = f32[384,128]{1,0:T(8,128)S(1)} custom-call(f32[512,128]{1,0:T(8,128)S(1)} %bitcast.15, f32[16,128]{1,0:T(8,128)S(1)} %member.1.own_fm, f32[16,128]{1,0:T(8,128)S(1)} %collective-permute-done.3.other_fm), custom_call_target="tpu_custom_call" | custom-call | tf_op jit(solution)/shard_map/project/pallas_call | solution.py:652
  27.1 11.1 %all_to_all.11 = f32[32,12,1,128]{3,2,1,0:T(1,128)S(1)} all-to-all(f32[32,12,1,128]{3,2,1,0:T(1,128)S(1)} %bitcast.19), channel_id=1, replica_groups={{0,2,4,6,8,10,12,14,1,3,5,7,9,11,13,15,16,18,20,22,24,26,28,30,17,19,21..., dimensions={0} | all-to-all | bytes 393216 | tf_op jit(solution)/shard_map/all_to_all | solution.py:545
  38.2 1.0 %gather.1 = f32[16,3,8,128]{3,2,1,0:T(8,128)} custom-call(f32[384,128]{1,0:T(8,128)S(1)} %bitcast.18), custom_call_target="tpu_custom_call" | custom-call | tf_op jit(solution)/shard_map/gather/pallas_call | solution.py:660
Async XLA Ops:
  1.0 11.7 %collective-permute-start = (f32[2,200,128]{2,1,0:T(8,128)S(1)}, f32[2,200,128]{2,1,0:T(8,128)S(1)}, u32[]{:S(2)}, u32[]{:S(2)}) collective-permute-start(f32[2,200,128]{2,1,0:T(8,128)S(1)} %bitcast.17), channel_id=1, source_target_pairs={{0,15},{1,2},{2,1},{3,4},{4,3},{5,6},{6,5},{7,8},{8,7},{9,10},{10,... | collective-permute-start | bytes 614408 | tf_op jit(solution)/shard_map/ppermute | solution.py:616
  3.7 5.3 %copy-start = (f32[16,32]{1,0:T(8,128)S(1)}, f32[16,32]{1,0:T(8,128)}, u32[]{:S(2)}) copy-start(f32[16,32]{1,0:T(8,128)} %fm.1) | copy-start | bytes 6148
  5.0 3.9 %collective-permute-start.2 = (f32[200,128]{1,0:T(8,128)S(1)}, f32[200,128]{1,0:T(8,128)S(1)}, u32[]{:S(2)}, u32[]{:S(2)}) collective-permute-start(f32[200,128]{1,0:T(8,128)S(1)} %bitcast.25), channel_id=1, source_target_pairs={{0,1},{1,0},{2,3},{3,2},{4,5},{5,4},{6,7},{7,6},{8,9},{9,8},{10,11... | collective-permute-start | bytes 307208 | tf_op jit(solution)/shard_map/ppermute | solution.py:617
  8.0 2.3 %collective-permute-start.1 = (f32[200,128]{1,0:T(8,128)S(1)}, f32[200,128]{1,0:T(8,128)S(1)}, u32[]{:S(2)}, u32[]{:S(2)}) collective-permute-start(f32[200,128]{1,0:T(8,128)S(1)} %bitcast.24), channel_id=1, source_target_pairs={{0,1},{1,0},{2,3},{3,2},{4,5},{5,4},{6,7},{7,6},{8,9},{9,8},{10,11... | collective-permute-start | bytes 307208 | tf_op jit(solution)/shard_map/ppermute | solution.py:617
  9.0 3.7 %collective-permute-start.3 = (f32[16,128]{1,0:T(8,128)S(1)}, f32[16,128]{1,0:T(8,128)S(1)}, u32[]{:S(2)}, u32[]{:S(2)}) collective-permute-start(f32[16,128]{1,0:T(8,128)S(1)} %member.1.own_fm), channel_id=1, source_target_pairs={{0,16},{16,0},{1,17},{17,1},{2,18},{18,2},{3,19},{19,3},{4,20},{20... | collective-permute-start | bytes 24584 | tf_op jit(solution)/shard_map/ppermute | solution.py:626
